TPU v7x, 512 devices: a whole 4x8x8 slice. The times are simulated.
512 devices in a mesh: psg: 128 (over z, y, core), row: 4 (over x).
Axes of the slice: x: 4, y: 8, z: 8, core: 2. Of those that a mesh axis runs over, the one named last changes fastest.
Arguments:
- query: bfloat16 [384, 4096], P('row'), may hold values from -3 to 3
- out_grad: bfloat16 [384, 4096], P('row'), may hold values from -5120 to 5120
- keys: bfloat16 [16384, 4096], P('psg', 'row'), may hold values from -1.5 to 1.5
- values: bfloat16 [16384, 4096], P('psg', 'row'), may hold values from -1.5 to 1.5
Outputs:
- query_grad: bfloat16 [384, 4096], P('row')
- key_grad: bfloat16 [16384, 4096], P('psg', 'row')
- value_grad: bfloat16 [16384, 4096], P('psg', 'row')
All inputs are finite; a program needn't handle non-finite values.
Results may differ from a plain program's by a relative error of at most 0.0073.
Values may be sent and summed in bfloat16 or wider, within the bound.
No kernel may reach another device: no remote copies, remote signals or barrier semaphores. Data moves between devices by JAX's collectives and lax.ppermute only.
A program may use at most 64 MiB of HBM per device.

v0:
```python
import math

import jax
import jax.numpy as jnp
from jax import lax
from jax.sharding import PartitionSpec as P

DH = 64


def local(query, out_grad, keys, values):
    query_all, gradient_totals = (
        lax.all_to_all(query, "row", split_axis=1, concat_axis=0, tiled=True),
        lax.all_to_all(out_grad, "row", split_axis=1, concat_axis=0, tiled=True),
    )
    row_count = query_all.shape[0]
    mem_count = keys.shape[0]
    feature_count = keys.shape[1]
    head_count = feature_count // DH
    group_size = math.gcd(head_count, 4)
    query_heads = query_all.reshape(row_count, head_count, DH)
    grad_heads = gradient_totals.reshape(row_count, head_count, DH)
    key_heads = keys.reshape(mem_count, head_count, DH)
    value_heads = values.reshape(mem_count, head_count, DH)

    def products(start):
        query_block = query_heads[:, start : start + group_size]
        gradient_block = grad_heads[:, start : start + group_size]
        key_block = key_heads[:, start : start + group_size]
        value_block = value_heads[:, start : start + group_size]
        score_blk = jnp.einsum(
            "ikn,gkn->kig", query_block, key_block, preferred_element_type=jnp.float32
        )
        grad_prob = jnp.einsum(
            "ikn,gkn->kig", gradient_block, value_block, preferred_element_type=jnp.float32
        )
        return (query_block, gradient_block, key_block, score_blk, grad_prob)

    peak_parts = []
    total_parts = []
    weighted_parts = []
    for start in range(0, head_count, group_size):
        query_block, gradient_block, key_block, score_blk, grad_prob = products(start)
        peak_blk = jnp.max(score_blk, axis=2)
        expo = jnp.exp(score_blk - peak_blk[:, :, None])
        peak_parts.append(peak_blk)
        total_parts.append(jnp.sum(expo, axis=2))
        weighted_parts.append(jnp.sum(expo * grad_prob, axis=2))
    peak_local = jnp.concatenate(peak_parts, axis=0)
    total_local = jnp.concatenate(total_parts, axis=0)
    weighted_shard_sum = jnp.concatenate(weighted_parts, axis=0)
    peak_all = lax.pmax(peak_local, "psg")
    rescale = jnp.exp(peak_local - peak_all)
    total_all, weighted_all = lax.psum((total_local * rescale, weighted_shard_sum * rescale), "psg")
    offset_all = weighted_all / total_all
    query_terms = []
    key_terms = []
    value_terms = []
    for start in range(0, head_count, group_size):
        query_block, gradient_block, key_block, score_blk, grad_prob = products(start)
        stop = start + group_size
        prob = jnp.exp(score_blk - peak_all[start:stop, :, None]) / total_all[start:stop, :, None]
        grad_score = prob * (grad_prob - offset_all[start:stop, :, None])
        probability_narrow = prob.astype(jnp.bfloat16)
        score_narrow = grad_score.astype(jnp.bfloat16)
        value_terms.append(
            jnp.einsum(
                "byu,ybq->ubq",
                probability_narrow,
                gradient_block,
                preferred_element_type=jnp.float32,
            ).astype(jnp.bfloat16)
        )
        key_terms.append(
            jnp.einsum(
                "byu,ybq->ubq", score_narrow, query_block, preferred_element_type=jnp.float32
            ).astype(jnp.bfloat16)
        )
        query_terms.append(
            jnp.einsum("zsx,xzp->szp", score_narrow, key_block, preferred_element_type=jnp.float32)
        )
    value_grad = jnp.concatenate(value_terms, axis=1).reshape(mem_count, feature_count)
    key_grad = jnp.concatenate(key_terms, axis=1).reshape(mem_count, feature_count)
    query_local = jnp.concatenate(query_terms, axis=1).reshape(row_count, feature_count)
    summed = lax.psum(query_local, "psg").astype(jnp.bfloat16)
    query_grad = lax.all_to_all(summed, "row", split_axis=0, concat_axis=1, tiled=True)
    return (query_grad, key_grad, value_grad)


def solution(mesh):
    placed = (P("row", None), P("row", None), P("psg", "row"), P("psg", "row"))
    return jax.shard_map(
        local,
        mesh=mesh,
        in_specs=placed,
        out_specs=(P("row", None), P("psg", "row"), P("psg", "row")),
        check_vma=False,
    )
```

profile of v0, /device:TPU:1, one launch (start us, length us, event | category | flops | bytes accessed | tf_op | source)
XLA Modules:
  0.0 1554.7 jit_solution(14182565560062381787)
XLA Ops:
  0.7 2.2 copy.125
  2.8 5.0 all-to-all-start
  8.0 1.0 copy.124
  9.8 6.4 all-to-all-done
  16.1 3.5 all-to-all-start.1
  21.7 1.2 fusion.49
  22.9 1.2 fusion.50
  24.1 500.3 %pmax.7 = f32[16,384]{1,0:T(8,128)S(1)} all-reduce(f32[16,384]{1,0:T(8,128)S(1)} %pad_maximum_fusion.3), channel_id=1, replica_groups=mesh['psg'=128,'row'=4] {'psg'}, use_global_device_ids=true, to_apply=%region_4.0 | all-reduce | flops 6144 | bytes 49152 | tf_op jit(solution)/shard_map/pmax | solution.py:52
  524.4 1.4 copy.89
  525.8 2.0 reshape.56
  527.9 2.4 fusion.8
  530.3 1.2 fusion.9
  531.5 1.2 fusion.10
  532.7 1.2 fusion.11
  534.0 490.9 %all-reduce = (f32[16,384]{1,0:T(8,128)S(1)}, f32[16,384]{1,0:T(8,128)S(1)}) all-reduce(f32[16,384]{1,0:T(8,128)S(1)} %get-tuple-element.29, f32[16,384]{1,0:T(8,128)S(1)} %get-tuple-element.28), channel_id=1, replica_groups=mesh['psg'=128,'row'=4] {'psg'}, use_global_device_ids=true, to_apply=%region_14.0 | all-reduce | flops 12288 | bytes 98304 | tf_op jit(solution)/shard_map/psum | solution.py:54
  1025.5 1.5 fusion.4
  1029.4 1.0 convolution_bitcast_fusion.3
  1030.6 1.0 convolution_bitcast_fusion.2
  1033.1 1.7 multiply_convert_fusion
  1036.1 1.6 copy.95
  1037.7 503.5 %all-reduce.2 = bf16[384,1024]{1,0:T(8,128)(2,1)} all-reduce(f32[384,1024]{1,0:T(8,128)} %copy.95), channel_id=1, replica_groups=mesh['psg'=128,'row'=4] {'psg'}, use_global_device_ids=true, to_apply=%region_15.0 | all-reduce | flops 393216 | bytes 2359296 | tf_op jit(solution)/shard_map/psum | solution.py:85
  1541.2 4.2 all-to-all-start.2
  1546.9 6.9 all-to-all-done.2
  1553.8 0.9 copy.121
  (54 shorter events, 10.5 us)
Async XLA Ops:
  0.6 7.2 copy-start.9
  0.6 7.3 copy-start.8
  2.8 6.1 copy-start.10
  2.8 13.3 all-to-all-start
  16.1 508.3 %all-to-all-start.1 = ((bf16[96,4,1024]{2,0,1:T(8,128)(2,1)}), bf16[96,4,1024]{2,0,1:T(8,128)(2,1)S(1)}, u32[]{:S(2)}, u32[]{:S(2)}) async-start(bf16[96,4,1024]{2,0,1:T(8,128)(2,1)} %bitcast.61), calls=%async_computation.1 | async-start | bytes 1572864 | tf_op jit(solution)/shard_map/all_to_all | solution.py:14
  527.8 2.5 copy-start
  527.8 2.5 copy-start.7
  1024.9 6.7 copy-start.12
  1024.9 7.0 copy-start.11
  1025.5 1.5 copy-start.1
  1027.0 1.1 copy-start.2
  1027.1 1.4 copy-start.3
  1027.1 1.6 copy-start.4
  1034.9 1.0 copy-start.5
  1034.9 1.1 copy-start.6
  1541.2 12.5 all-to-all-start.2
where the time goes:
time: 1560 us; the launch traced here: 1550 us
  blocking collectives  1490 us (96%)
  local copies, waits for them, and re-layouts  15.8 us (1%)
    psum x1, blocking collectives, local(): summed = lax.psum(query_local, 'psg').astype(jnp.bfloat16)  503 us
    pmax x1, blocking collectives, local(): peak_all = lax.pmax(peak_local, 'psg')  500 us
    psum x1, blocking collectives, local(): lax.psum((total_local * rescale, weighted_shard_sum * rescale), 'psg')  491 us
  transfers between devices with their start and end apart: 3, of which 2 were waited for; matrix products, arithmetic and copies ran while one was open for 1% of the time, Pallas kernels for 0%

commit v1 on v0

v1 whole, which is shorter than its diff:
```python
import jax
import jax.numpy as jnp
from jax import lax
from jax.experimental import pallas as pl
from jax.experimental.pallas import tpu as pltpu
from jax.sharding import Mesh
from jax.sharding import PartitionSpec as P

F32 = jnp.float32
BF16 = jnp.bfloat16
NZ, NY, NC, NX = 8, 8, 2, 4
HEADS = 16
BLOCK = 128
ROWS = 384
MINE = ROWS // NX
MEMS = HEADS * BLOCK
STEP = 256
NT = (((1,), (1,)), ((), ()))
TN = (((0,), (0,)), ((), ()))
NN = (((1,), (0,)), ((), ()))

VMEM = pl.BlockSpec(memory_space=pltpu.VMEM)
SMEM = pl.BlockSpec(memory_space=pltpu.SMEM)


def call(body, out_shape, n_in, scratch=(), smem=0, flops=0, moved=0, exps=0):
    outs = out_shape if isinstance(out_shape, (tuple, list)) else None
    return pl.pallas_call(
        body,
        out_shape=out_shape,
        in_specs=[SMEM] * smem + [VMEM] * n_in,
        out_specs=[VMEM] * len(outs) if outs else VMEM,
        scratch_shapes=list(scratch),
        compiler_params=pltpu.CompilerParams(vmem_limit_bytes=24 * 2**20),
        cost_estimate=pl.CostEstimate(flops=flops, bytes_accessed=moved, transcendentals=exps),
    )


def dot(a, b, dims):
    return lax.dot_general(a, b, dims, preferred_element_type=F32)


def low_lanes(shape):
    return lax.broadcasted_iota(jnp.int32, shape, len(shape) - 1) < 64


def pack_memory(k_ref, v_ref, out_ref):
    low = low_lanes((BLOCK, 128))
    for t in range(HEADS // 2):
        k = k_ref[:, 128 * t : 128 * t + 128].astype(F32)
        v = v_ref[:, 128 * t : 128 * t + 128].astype(F32)
        out_ref[2 * t] = jnp.where(low, k, pltpu.roll(v, 64, 1)).astype(BF16)
        out_ref[2 * t + 1] = jnp.where(low, pltpu.roll(k, 64, 1), v).astype(BF16)


def pack_query(at_ref, q_ref, g_ref, out_ref):
    y, c = at_ref[0], at_ref[1]
    low = low_lanes((MINE, 128))
    for x in range(NX):
        lanes = pl.ds(pl.multiple_of((x * NY + y) * 128, 128), 128)
        q = q_ref[:, lanes].astype(F32)
        g = g_ref[:, lanes].astype(F32)
        first = jnp.where(low, q, pltpu.roll(g, 64, 1))
        second = jnp.where(low, pltpu.roll(q, 64, 1), g)
        out_ref[x] = jnp.where(c == 0, first, second).astype(BF16)


def halves(qg_ref):
    qg = qg_ref[...]
    low = low_lanes(qg.shape)
    zero = jnp.zeros_like(qg)
    return jnp.where(low, qg, zero), jnp.where(low, zero, qg)


def local_stats(kv_ref, qg_ref, out_ref, s_ref):
    q, g = halves(qg_ref)
    peak = None
    for j in range(0, MEMS, STEP):
        s = dot(kv_ref[j : j + STEP, :], q, NT)
        s_ref[j : j + STEP, :] = s
        top = jnp.max(s, axis=0, keepdims=True)
        peak = top if peak is None else jnp.maximum(peak, top)
    total = jnp.zeros((1, ROWS), F32)
    weighted = jnp.zeros((1, ROWS), F32)
    for j in range(0, MEMS, STEP):
        e = jnp.exp(s_ref[j : j + STEP, :] - peak)
        w = e * dot(kv_ref[j : j + STEP, :], g, NT)
        total += jnp.sum(e, axis=0, keepdims=True)
        weighted += jnp.sum(w, axis=0, keepdims=True)
    lse = peak + jnp.log(total)
    mean = weighted / total
    for d in range(NZ):
        for t in range(3):
            out_ref[d, t : t + 1, :] = lse[:, 128 * t : 128 * t + 128]
            out_ref[d, 4 + t : 5 + t, :] = mean[:, 128 * t : 128 * t + 128]


def whole_stats(st_ref):
    logs, offsets = [], []
    for t in range(3):
        part = st_ref[:, t, :]
        mean = st_ref[:, 4 + t, :]
        peak = jnp.max(part, axis=0, keepdims=True)
        e = jnp.exp(part - peak)
        total = jnp.sum(e, axis=0, keepdims=True)
        logs.append(peak + jnp.log(total))
        offsets.append(jnp.sum(e * mean, axis=0, keepdims=True) / total)
    return jnp.concatenate(logs, axis=1), jnp.concatenate(offsets, axis=1)


def query_part(st_ref, kv_ref, qg_ref, out_ref, ds_ref):
    lse, offset = whole_stats(st_ref)
    q, g = halves(qg_ref)
    for j in range(0, MEMS, STEP):
        kv = kv_ref[j : j + STEP, :]
        prob = jnp.exp(dot(kv, q, NT) - lse)
        ds_ref[j : j + STEP, :] = (prob * (dot(kv, g, NT) - offset)).astype(BF16)
    turned = dot(kv_ref[...], ds_ref[...], TN)
    dq = turned.T
    low = low_lanes((8, 128))
    for x in range(NX):
        for z in range(NZ):
            a = MINE * x + 8 * z
            b = MINE * x + 64 + 8 * (z // 2)
            out_ref[z * NX + x] = jnp.where(low, dq[a : a + 8, :], pltpu.roll(dq[b : b + 8, :], 64, 1))


def memory_grads(st_ref, kv_ref, qg_ref, out_ref):
    lse, offset = whole_stats(st_ref)
    q, g = halves(qg_ref)
    for j in range(0, MEMS, STEP):
        kv = kv_ref[j : j + STEP, :]
        prob = jnp.exp(dot(kv, q, NT) - lse)
        ds = (prob * (dot(kv, g, NT) - offset)).astype(BF16)
        out = dot(ds, q, NN) + dot(prob.astype(BF16), g, NN)
        out_ref[j : j + STEP, :] = out.astype(BF16)


def add_query(at_ref, in_ref, out_ref):
    odd = at_ref[0] % 2 == 1
    low = low_lanes((8, 128))
    top = lax.broadcasted_iota(jnp.int32, (8, 128), 0) < 4
    t = []
    for x in range(NX):
        total = in_ref[x]
        for z in range(1, NZ):
            total = total + in_ref[z * NX + x]
        t.append(total)
    full = [jnp.where(low, t[2 * p], pltpu.roll(t[2 * p + 1], 64, 1)) for p in range(2)]
    half = [jnp.where(low, pltpu.roll(t[2 * p], 64, 1), t[2 * p + 1]) for p in range(2)]
    even_half = jnp.where(top, half[0], pltpu.roll(half[1], 4, 0))
    odd_half = jnp.where(top, pltpu.roll(half[0], 4, 0), half[1])
    last = jnp.where(odd, odd_half, even_half)
    piece = jnp.concatenate([full[0], full[1], last], axis=0).astype(BF16)
    out_ref[...] = jnp.broadcast_to(piece[None], out_ref.shape)


def join_query(in_ref, out_ref):
    low = low_lanes((8, 128))
    top = lax.broadcasted_iota(jnp.int32, (8, 128), 0) < 4
    for y in range(NY):

        def heads(f0, f1):
            return jnp.where(low, f0, pltpu.roll(f1, 64, 1)), jnp.where(low, pltpu.roll(f0, 64, 1), f1)

        for z4 in range(0, NZ, 4):
            pieces = [[in_ref[c, z4 + i, y].astype(F32) for i in range(4)] for c in range(NC)]
            for p in range(2):
                tiles = [heads(pieces[0][i][8 * p : 8 * p + 8], pieces[1][i][8 * p : 8 * p + 8]) for i in range(4)]
                ends = []
                for i in (0, 2):
                    g = []
                    for c in range(NC):
                        even, odd = pieces[c][i][16:24], pieces[c][i + 1][16:24]
                        if p == 0:
                            g.append(jnp.where(top, even, pltpu.roll(odd, 4, 0)))
                        else:
                            g.append(jnp.where(top, pltpu.roll(even, 4, 0), odd))
                    ends.append(heads(g[0], g[1]))
                for u in range(2):
                    lanes = slice(((2 * p + u) * NY + y) * 128, ((2 * p + u) * NY + y) * 128 + 128)
                    for i in (0, 2):
                        r = 8 * (z4 + i)
                        both = jnp.concatenate([tiles[i][u], tiles[i + 1][u]], axis=0)
                        out_ref[r : r + 16, lanes] = both.astype(BF16)
                    r = 64 + 4 * z4
                    both = jnp.concatenate([ends[0][u], ends[1][u]], axis=0)
                    out_ref[r : r + 16, lanes] = both.astype(BF16)


def unpack_memory(in_ref, k_ref, v_ref):
    low = low_lanes((BLOCK, 128))
    for t in range(HEADS // 2):
        a = in_ref[2 * t].astype(F32)
        b = in_ref[2 * t + 1].astype(F32)
        k_ref[:, 128 * t : 128 * t + 128] = jnp.where(low, a, pltpu.roll(b, 64, 1)).astype(BF16)
        v_ref[:, 128 * t : 128 * t + 128] = jnp.where(low, pltpu.roll(a, 64, 1), b).astype(BF16)


def local(query, out_grad, keys, values):
    shape = jax.ShapeDtypeStruct
    z, y, c = lax.axis_index("z"), lax.axis_index("y"), lax.axis_index("core")
    at = jnp.stack([y, c]).astype(jnp.int32)
    zs = jnp.stack([z, c]).astype(jnp.int32)
    mega = 2**20

    memory = call(pack_memory, shape((HEADS, BLOCK, 128), BF16), 2, moved=mega)(keys, values)
    memory = lax.all_to_all(memory, ("y", "core"), 0, 0, tiled=True).reshape(MEMS, 128)
    pairs = call(pack_query, shape((NX, MINE, 128), BF16), 2, smem=1, moved=mega)(at, query, out_grad)
    pairs = lax.all_to_all(pairs, "row", 0, 0, tiled=True).reshape(ROWS, 128)

    work = 2 * MEMS * ROWS * 128
    stats = call(
        local_stats,
        shape((NZ, 8, 128), F32),
        2,
        scratch=[pltpu.VMEM((MEMS, ROWS), F32)],
        flops=2 * work,
        moved=mega,
        exps=MEMS * ROWS,
    )(memory, pairs)
    stats = lax.all_to_all(stats, "z", 0, 0, tiled=True)

    part = call(
        query_part,
        shape((NZ * NX, 8, 128), F32),
        3,
        scratch=[pltpu.VMEM((MEMS, ROWS), BF16)],
        flops=3 * work,
        moved=mega,
        exps=MEMS * ROWS,
    )(stats, memory, pairs)
    part = lax.all_to_all(part, ("z", "row"), 0, 0, tiled=True)
    grads = call(memory_grads, shape((MEMS, 128), BF16), 3, flops=4 * work, moved=mega, exps=MEMS * ROWS)(
        stats, memory, pairs
    )
    piece = call(add_query, shape((NZ * NY, 24, 128), BF16), 1, smem=1, moved=mega)(zs, part)
    piece = lax.all_to_all(piece, ("z", "y"), 0, 0, tiled=True).reshape(NZ, NY, 24, 128)
    pieces = lax.all_gather(piece, "core", axis=0, tiled=False)
    query_grad = call(join_query, shape((MINE, 4096), BF16), 1, moved=2 * mega)(pieces)

    grads = lax.all_to_all(grads.reshape(HEADS, BLOCK, 128), ("y", "core"), 0, 0, tiled=True)
    key_grad, value_grad = call(
        unpack_memory, [shape((BLOCK, 1024), BF16), shape((BLOCK, 1024), BF16)], 1, moved=mega
    )(grads)
    return (query_grad, key_grad, value_grad)


def solution(mesh):
    fine = Mesh(mesh.devices.reshape(NZ, NY, NC, NX), ("z", "y", "core", "row"))
    psg = ("z", "y", "core")
    placed = (P("row", None), P("row", None), P(psg, "row"), P(psg, "row"))
    return jax.shard_map(
        local,
        mesh=fine,
        in_specs=placed,
        out_specs=(P("row", None), P(psg, "row"), P(psg, "row")),
        check_vma=False,
    )
```

time: 1560 us -> 122 us (0.08)
  blocking collectives: 1490 us -> 46.3 us
  waiting for transfers between devices: 13.2 us -> 42.2 us
    psum x2 -> x0, blocking collectives: 994 us -> none  [the longest x1 503 us: local(): summed = lax.psum(query_local, 'psg').astype(jnp.bfloat16)]
    pmax x1 -> x0, blocking collectives: 500 us -> none  [local(): peak_all = lax.pmax(peak_local, 'psg')]
    all_to_all x0 -> x2, blocking collectives: none -> 43 us  [the longest x1 26.3 us: local(): lax.all_to_all(memory, ('y', 'core'), 0, 0, tiled=True).reshape(MEMS, 128)]
    all_to_all x3 -> x4, waiting for transfers between devices: 13.2 us -> 42.2 us  [the longest x1 15.9 us: local(): lax.all_to_all(grads.reshape(HEADS, BLOCK, 128), ('y', 'core'), 0, 0, til...]
  transfers between devices with their start and end apart: 3 -> 4, of which waited for: 2 -> 4; matrix products, arithmetic and copies ran while one was open for 1% -> 0% of each run, Pallas kernels for 0% -> 5%
where the time goes in v1:
time: 122 us; the launch traced here: 121 us
  blocking collectives  46.3 us (38%)
  waiting for transfers between devices  42.2 us (35%)
  starting transfers between devices  18.3 us (15%)
  Pallas kernels  11.4 us (9%)
  local copies, waits for them, and re-layouts  2.27 us (2%)
    all_to_all x1, blocking collectives, local(): lax.all_to_all(memory, ('y', 'core'), 0, 0, tiled=True).reshape(MEMS, 128)  26.3 us
    all_to_all x1, blocking collectives, local(): stats = lax.all_to_all(stats, 'z', 0, 0, tiled=True)  16.7 us
    all_to_all x1, waiting for transfers between devices, local(): lax.all_to_all(grads.reshape(HEADS, BLOCK, 128), ('y', 'core'), 0, 0, til...  15.9 us
    all_to_all x1, waiting for transfers between devices, local(): lax.all_to_all(piece, ('z', 'y'), 0, 0, tiled=True).reshape(NZ, NY, 24, 128)  14.9 us
    all_to_all x1, waiting for transfers between devices, local(): part = lax.all_to_all(part, ('z', 'row'), 0, 0, tiled=True)  7.02 us
    all_to_all x1, starting transfers between devices, local(): lax.all_to_all(grads.reshape(HEADS, BLOCK, 128), ('y', 'core'), 0, 0, til...  4.99 us
    all_to_all x1, starting transfers between devices, local(): pairs = lax.all_to_all(pairs, 'row', 0, 0, tiled=True).reshape(ROWS, 128)  4.84 us
    all_to_all x1, starting transfers between devices, local(): lax.all_to_all(piece, ('z', 'y'), 0, 0, tiled=True).reshape(NZ, NY, 24, 128)  4.63 us
  transfers between devices with their start and end apart: 4, of which 4 were waited for; matrix products, arithmetic and copies ran while one was open for 0% of the time, Pallas kernels for 5%

profile of v1, /device:TPU:1, one launch (start us, length us, event | category | flops | bytes accessed | tf_op | source)
XLA Modules:
  0.0 121.4 jit_solution(11819305857759019883)
XLA Ops:
  0.6 0.1 pad_add_fusion.1.at_ref
  0.7 1.1 copy-done
  1.8 1.1 copy-done.1
  3.0 1.3 %shard_map.68 = bf16[4,96,128]{2,1,0:T(8,128)(2,1)} custom-call(s32[2]{0:T(128)S(1)} %pad_add_fusion.1.at_ref, bf16[96,4096]{1,0:T(8,128)(2,1)S(1)} %copy-done, bf16[96,4096]{1,0:T(8,128)(2,1)S(1)} %copy-done.1), custom_call_target="tpu_custom_call" | custom-call | bytes 1048576 | tf_op jit(solution)/shard_map/pallas_call | solution.py:209
  4.3 4.8 %all-to-all-start.1 = ((bf16[4,96,128]{2,1,0:T(8,128)(2,1)}), bf16[4,96,128]{2,1,0:T(8,128)(2,1)S(1)}, u32[]{:S(2)}, u32[]{:S(2)}) async-start(bf16[4,96,128]{2,1,0:T(8,128)(2,1)} %shard_map.68), calls=%async_computation.1 | async-start | bytes 196608 | tf_op jit(solution)/shard_map/all_to_all | solution.py:210
  9.1 0.0 copy-done.2
  9.1 0.2 shard_map.67
  9.4 4.4 %all-to-all-done.1 = bf16[4,96,128]{2,1,0:T(8,128)(2,1)S(1)} async-done(((bf16[4,96,128]{2,1,0:T(8,128)(2,1)}), bf16[4,96,128]{2,1,0:T(8,128)(2,1)S(1)}, u32[]{:S(2)}, u32[]{:S(2)}) %all-to-all-start.1) | async-done | bytes 98336 | tf_op jit(solution)/shard_map/all_to_all | solution.py:210
  13.8 26.3 %all_to_all.30 = bf16[16,128,128]{2,1,0:T(8,128)(2,1)S(1)} all-to-all(bf16[16,128,128]{2,1,0:T(8,128)(2,1)S(1)} %shard_map.67), channel_id=1, replica_groups=mesh['z'=8,'y'=8,'core'=2,'row'=4] {'y','core'}, dimensions={0} | all-to-all | bytes 1048576 | tf_op jit(solution)/shard_map/all_to_all | solution.py:208
  40.1 1.3 %shard_map.69 = f32[8,8,128]{2,1,0:T(8,128)S(1)} custom-call(bf16[2048,128]{1,0:T(8,128)(2,1)S(1)} %bitcast.7, bf16[384,128]{1,0:T(8,128)(2,1)S(1)} %bitcast.10), custom_call_target="tpu_custom_call" | custom-call | flops 402653184 | bytes 1048576 | tf_op jit(solution)/shard_map/pallas_call | solution.py:213
  41.4 16.7 %all_to_all.31.st_ref = f32[8,8,128]{2,1,0:T(8,128)S(1)} all-to-all(f32[8,8,128]{2,1,0:T(8,128)S(1)} %shard_map.69), channel_id=1, replica_groups=mesh['z'=8,'y'=8,'core'=2,'row'=4] {'z'}, dimensions={0} | all-to-all | bytes 65536 | tf_op jit(solution)/shard_map/all_to_all | solution.py:222
  58.1 2.1 %shard_map.70 = f32[32,8,128]{2,1,0:T(8,128)} custom-call(f32[8,8,128]{2,1,0:T(8,128)S(1)} %all_to_all.31.st_ref, bf16[2048,128]{1,0:T(8,128)(2,1)S(1)} %bitcast.8, bf16[384,128]{1,0:T(8,128)(2,1)S(1)} %bitcast.11), custom_call_target="tpu_custom_call" | custom-call | flops 603979776 | bytes 1048576 | tf_op jit(solution)/shard_map/pallas_call | solution.py:224
  60.2 3.9 %all-to-all-start.3 = ((f32[32,8,128]{2,1,0:T(8,128)}), f32[32,8,128]{2,1,0:T(8,128)S(1)}, u32[]{:S(2)}, u32[]{:S(2)}) async-start(f32[32,8,128]{2,1,0:T(8,128)} %shard_map.70), calls=%async_computation.3 | async-start | bytes 262144 | tf_op jit(solution)/shard_map/all_to_all | solution.py:233
  64.1 2.9 %shard_map.73 = bf16[2048,128]{1,0:T(8,128)(2,1)} custom-call(f32[8,8,128]{2,1,0:T(8,128)S(1)} %all_to_all.31.st_ref, bf16[2048,128]{1,0:T(8,128)(2,1)S(1)} %bitcast.9, bf16[384,128]{1,0:T(8,128)(2,1)S(1)} %bitcast.12), custom_call_target="tpu_custom_call" | custom-call | flops 805306368 | bytes 1048576 | tf_op jit(solution)/shard_map/pallas_call | solution.py:234
  66.9 7.0 %all-to-all-done.3.in_ref = f32[32,8,128]{2,1,0:T(8,128)S(1)} async-done(((f32[32,8,128]{2,1,0:T(8,128)}), f32[32,8,128]{2,1,0:T(8,128)S(1)}, u32[]{:S(2)}, u32[]{:S(2)}) %all-to-all-start.3) | async-done | bytes 131104 | tf_op jit(solution)/shard_map/all_to_all | solution.py:233
  74.0 5.0 %all-to-all-start.5 = ((bf16[16,128,128]{2,1,0:T(8,128)(2,1)}), bf16[16,128,128]{2,1,0:T(8,128)(2,1)S(1)}, u32[]{:S(2)}, u32[]{:S(2)}) async-start(bf16[16,128,128]{2,1,0:T(8,128)(2,1)} %bitcast.6), calls=%async_computation.5 | async-start | bytes 1048576 | tf_op jit(solution)/shard_map/all_to_all | solution.py:242
  79.0 0.1 pad_add_fusion.at_ref
  79.0 1.4 %shard_map.71 = bf16[64,24,128]{2,1,0:T(8,128)(2,1)} custom-call(s32[2]{0:T(128)S(1)} %pad_add_fusion.at_ref, f32[32,8,128]{2,1,0:T(8,128)S(1)} %all-to-all-done.3.in_ref), custom_call_target="tpu_custom_call" | custom-call | bytes 1048576 | tf_op jit(solution)/shard_map/pallas_call | solution.py:237
  80.4 15.9 %all-to-all-done.5.in_ref = bf16[16,128,128]{2,1,0:T(8,128)(2,1)S(1)} async-done(((bf16[16,128,128]{2,1,0:T(8,128)(2,1)}), bf16[16,128,128]{2,1,0:T(8,128)(2,1)S(1)}, u32[]{:S(2)}, u32[]{:S(2)}) %all-to-all-start.5) | async-done | bytes 524320 | tf_op jit(solution)/shard_map/all_to_all | solution.py:242
  96.3 4.6 %all-to-all-start.4 = ((bf16[64,24,128]{2,1,0:T(8,128)(2,1)}), bf16[64,24,128]{2,1,0:T(8,128)(2,1)S(1)}, u32[]{:S(2)}, u32[]{:S(2)}) async-start(bf16[64,24,128]{2,1,0:T(8,128)(2,1)} %shard_map.71), calls=%async_computation.4 | async-start | bytes 786432 | tf_op jit(solution)/shard_map/all_to_all | solution.py:238
  100.9 1.0 shard_map.74
  101.9 14.9 %all-to-all-done.4 = bf16[64,24,128]{2,1,0:T(8,128)(2,1)S(1)} async-done(((bf16[64,24,128]{2,1,0:T(8,128)(2,1)}), bf16[64,24,128]{2,1,0:T(8,128)(2,1)S(1)}, u32[]{:S(2)}, u32[]{:S(2)}) %all-to-all-start.4) | async-done | bytes 393248 | tf_op jit(solution)/shard_map/all_to_all | solution.py:238
  116.9 3.3 %all_gather.3.in_ref = bf16[2,8,8,24,128]{4,3,2,1,0:T(8,128)(2,1)S(1)} all-gather(bf16[1,8,8,24,128]{4,3,2,1,0:T(8,128)(2,1)S(1)} %bitcast.13), channel_id=1, replica_groups=mesh['z'=8,'y'=8,'core'=2,'row'=4] {'core'}, dimensions={0}, use_global_device_ids=true | all-gather | bytes 1179648 | tf_op jit(solution)/shard_map/all_gather | solution.py:239
  120.2 1.2 %shard_map.72 = bf16[96,4096]{1,0:T(8,128)(2,1)} custom-call(bf16[2,8,8,24,128]{4,3,2,1,0:T(8,128)(2,1)S(1)} %all_gather.3.in_ref), custom_call_target="tpu_custom_call" | custom-call | bytes 2097152 | tf_op jit(solution)/shard_map/pallas_call | solution.py:240
  (5 shorter events, 0.0 us)
Async XLA Ops:
  0.7 1.1 copy-start
  1.8 1.1 copy-start.1
  3.0 6.2 %copy-start.2 = (bf16[128,1024]{1,0:T(8,128)(2,1)S(1)}, bf16[128,1024]{1,0:T(8,128)(2,1)}, u32[]{:S(2)}) copy-start(bf16[128,1024]{1,0:T(8,128)(2,1)} %k_ref.1) | copy-start | bytes 786436
  3.0 6.2 %copy-start.3 = (bf16[128,1024]{1,0:T(8,128)(2,1)S(1)}, bf16[128,1024]{1,0:T(8,128)(2,1)}, u32[]{:S(2)}) copy-start(bf16[128,1024]{1,0:T(8,128)(2,1)} %v_ref.1) | copy-start | bytes 786436
  4.3 9.5 %all-to-all-start.1 = ((bf16[4,96,128]{2,1,0:T(8,128)(2,1)}), bf16[4,96,128]{2,1,0:T(8,128)(2,1)S(1)}, u32[]{:S(2)}, u32[]{:S(2)}) async-start(bf16[4,96,128]{2,1,0:T(8,128)(2,1)} %shard_map.68), calls=%async_computation.1 | async-start | bytes 196608 | tf_op jit(solution)/shard_map/all_to_all | solution.py:210
  60.2 13.8 %all-to-all-start.3 = ((f32[32,8,128]{2,1,0:T(8,128)}), f32[32,8,128]{2,1,0:T(8,128)S(1)}, u32[]{:S(2)}, u32[]{:S(2)}) async-start(f32[32,8,128]{2,1,0:T(8,128)} %shard_map.70), calls=%async_computation.3 | async-start | bytes 262144 | tf_op jit(solution)/shard_map/all_to_all | solution.py:233
  74.0 22.3 %all-to-all-start.5 = ((bf16[16,128,128]{2,1,0:T(8,128)(2,1)}), bf16[16,128,128]{2,1,0:T(8,128)(2,1)S(1)}, u32[]{:S(2)}, u32[]{:S(2)}) async-start(bf16[16,128,128]{2,1,0:T(8,128)(2,1)} %bitcast.6), calls=%async_computation.5 | async-start | bytes 1048576 | tf_op jit(solution)/shard_map/all_to_all | solution.py:242
  96.3 20.6 %all-to-all-start.4 = ((bf16[64,24,128]{2,1,0:T(8,128)(2,1)}), bf16[64,24,128]{2,1,0:T(8,128)(2,1)S(1)}, u32[]{:S(2)}, u32[]{:S(2)}) async-start(bf16[64,24,128]{2,1,0:T(8,128)(2,1)} %shard_map.71), calls=%async_computation.4 | async-start | bytes 786432 | tf_op jit(solution)/shard_map/all_to_all | solution.py:238

commit v2 on v1

v2 whole, which is shorter than its diff:
```python
import jax
import jax.numpy as jnp
from jax import lax
from jax.experimental import pallas as pl
from jax.experimental.pallas import tpu as pltpu
from jax.sharding import Mesh
from jax.sharding import PartitionSpec as P

F32 = jnp.float32
BF16 = jnp.bfloat16
NZ, NY, NC, NX = 8, 8, 2, 4
HEADS = 16
BLOCK = 128
ROWS = 384
MINE = ROWS // NX
MEMS = HEADS * BLOCK
STEP = 256
NT = (((1,), (1,)), ((), ()))
TN = (((0,), (0,)), ((), ()))
NN = (((1,), (0,)), ((), ()))

VMEM = pl.BlockSpec(memory_space=pltpu.VMEM)
SMEM = pl.BlockSpec(memory_space=pltpu.SMEM)


def call(body, out_shape, n_in, scratch=(), smem=0, flops=0, moved=0, exps=0):
    outs = out_shape if isinstance(out_shape, (tuple, list)) else None
    return pl.pallas_call(
        body,
        out_shape=out_shape,
        in_specs=[SMEM] * smem + [VMEM] * n_in,
        out_specs=[VMEM] * len(outs) if outs else VMEM,
        scratch_shapes=list(scratch),
        compiler_params=pltpu.CompilerParams(vmem_limit_bytes=40 * 2**20),
        cost_estimate=pl.CostEstimate(flops=flops, bytes_accessed=moved, transcendentals=exps),
    )


def dot(a, b, dims):
    return lax.dot_general(a, b, dims, preferred_element_type=F32)


def low_lanes(shape):
    return lax.broadcasted_iota(jnp.int32, shape, len(shape) - 1) < 64


def pack_memory(k_ref, v_ref, out_ref):
    low = low_lanes((BLOCK, 128))
    for t in range(HEADS // 2):
        k = k_ref[:, 128 * t : 128 * t + 128].astype(F32)
        v = v_ref[:, 128 * t : 128 * t + 128].astype(F32)
        out_ref[2 * t] = jnp.where(low, k, pltpu.roll(v, 64, 1)).astype(BF16)
        out_ref[2 * t + 1] = jnp.where(low, pltpu.roll(k, 64, 1), v).astype(BF16)


def pack_query(at_ref, q_ref, g_ref, *outs):
    x, y, c = at_ref[0], at_ref[1], at_ref[2]
    low = low_lanes((MINE, 128))
    for k in range(NX):
        lanes = pl.ds(pl.multiple_of((lax.rem(x + k, NX) * NY + y) * 128, 128), 128)
        q = q_ref[:, lanes].astype(F32)
        g = g_ref[:, lanes].astype(F32)
        first = jnp.where(low, q, pltpu.roll(g, 64, 1))
        second = jnp.where(low, pltpu.roll(q, 64, 1), g)
        outs[k][...] = jnp.where(c == 0, first, second).astype(BF16)


def pack_all_heads(at_ref, q_ref, g_ref, *outs):
    x = at_ref[0]
    low = low_lanes((MINE, 128))
    for k in range(NX):
        start = lax.rem(x + k, NX) * 1024
        for t in range(HEADS // 2):
            lanes = pl.ds(pl.multiple_of(start + 128 * t, 128), 128)
            q = q_ref[:, lanes].astype(F32)
            g = g_ref[:, lanes].astype(F32)
            outs[k][2 * t] = jnp.where(low, q, pltpu.roll(g, 64, 1)).astype(BF16)
            outs[k][2 * t + 1] = jnp.where(low, pltpu.roll(q, 64, 1), g).astype(BF16)


def halves(qg):
    low = low_lanes(qg.shape)
    zero = jnp.zeros_like(qg)
    return jnp.where(low, qg, zero), jnp.where(low, zero, qg)


def local_part(at_ref, kv_ref, q0, q1, q2, q3, out_ref, e_ref, gp_ref, ds_ref, p_ref):
    x = at_ref[0]
    q, g = halves(jnp.concatenate([q0[...], q1[...], q2[...], q3[...]], axis=0))
    peak = None
    for j in range(0, MEMS, STEP):
        s = dot(kv_ref[j : j + STEP, :], q, NT)
        e_ref[j : j + STEP, :] = s
        top = jnp.max(s, axis=0, keepdims=True)
        peak = top if peak is None else jnp.maximum(peak, top)
    total = jnp.zeros((1, ROWS), F32)
    weighted = jnp.zeros((1, ROWS), F32)
    for j in range(0, MEMS, STEP):
        e = jnp.exp(e_ref[j : j + STEP, :] - peak)
        e_ref[j : j + STEP, :] = e
        gp = dot(kv_ref[j : j + STEP, :], g, NT)
        gp_ref[j : j + STEP, :] = gp
        total += jnp.sum(e, axis=0, keepdims=True)
        weighted += jnp.sum(e * gp, axis=0, keepdims=True)
    lse = peak + jnp.log(total)
    mean = weighted / total
    inverse = 1.0 / total
    for j in range(0, MEMS, STEP):
        prob = e_ref[j : j + STEP, :] * inverse
        p_ref[j : j + STEP, :] = prob.astype(BF16)
        ds_ref[j : j + STEP, :] = (prob * (gp_ref[j : j + STEP, :] - mean)).astype(BF16)
    kv = kv_ref[...]
    first = dot(kv, ds_ref[...], TN)[:64]
    second = dot(kv, p_ref[...], TN)[:64]
    both = jnp.concatenate([first, second], axis=0).T
    pad = jnp.zeros((1, 128 - MINE), F32)
    for r in range(NX):
        owner = lax.rem(x - r + NX, NX)
        own = [jnp.concatenate([a[:, MINE * r : MINE * r + MINE], pad], axis=1) for a in (lse, mean)]
        for z in range(NZ):
            t = 128 * min(z, 2)
            a = MINE * r + 8 * z
            b = MINE * r + 64 + 4 * z
            out_ref[z * NX + owner, 0:8, :] = both[a : a + 8, :]
            rows = [both[b : b + 4, :], lse[:, t : t + 128], mean[:, t : t + 128]] + own
            out_ref[z * NX + owner, 8:16, :] = jnp.concatenate(rows, axis=0)


def weights(logs, means):
    peak = jnp.max(logs, axis=0, keepdims=True)
    e = jnp.exp(logs - peak)
    total = jnp.sum(e, axis=0, keepdims=True)
    w = e / total
    offset = jnp.sum(w * means, axis=0, keepdims=True)
    return peak + jnp.log(total), offset, w


def three(a):
    first = a.astype(BF16).astype(F32)
    second = (a - first).astype(BF16).astype(F32)
    return [first, second, a - first - second]


def add_query(at_ref, in_ref, out_ref, col_ref):
    z, x = at_ref[0], at_ref[1]
    odd = lax.rem(z, 2) == 1
    low = low_lanes((8, 128))
    top = lax.broadcasted_iota(jnp.int32, (8, 128), 0) < 4
    full, half = [], []
    for u in range(NX):
        logs = jnp.concatenate([in_ref[d * NX + u, 14:15, :] for d in range(NZ)], axis=0)
        means = jnp.concatenate([in_ref[d * NX + u, 15:16, :] for d in range(NZ)], axis=0)
        _, offset, w = weights(logs, means)
        shift = w * (means - offset)
        col_ref[u] = jnp.concatenate([w, shift, jnp.zeros((112, 128), F32)], axis=0).T
        cols = col_ref[u, pl.ds(pl.multiple_of(8 * z, 8), 8), :]
        ends = col_ref[u, pl.ds(pl.multiple_of(64 + 8 * (z // 2), 8), 8), :]
        ends = jnp.where(odd, pltpu.roll(ends, 4, 0), ends)
        a = jnp.zeros((8, 128), F32)
        b = jnp.zeros((8, 128), F32)
        for d in range(NZ):
            tile = in_ref[d * NX + u]
            a += tile[0:8] * jnp.where(low, cols[:, d : d + 1], cols[:, 8 + d : 9 + d])
            b += tile[8:16] * jnp.where(low, ends[:, d : d + 1], ends[:, 8 + d : 9 + d])
        full.append(a + pltpu.roll(a, 64, 1))
        half.append(b + pltpu.roll(b, 64, 1))
    f = [jnp.where(low, full[2 * p], full[2 * p + 1]) for p in range(2)]
    h = [jnp.where(low, half[2 * p], half[2 * p + 1]) for p in range(2)]
    logs = jnp.concatenate([in_ref[d * NX + x, 12:13, :] for d in range(NZ)], axis=0)
    means = jnp.concatenate([in_ref[d * NX + x, 13:14, :] for d in range(NZ)], axis=0)
    lse, offset, _ = weights(logs, means)
    stats = three(lse) + three(offset) + [jnp.zeros((2, 128), F32)]
    piece = jnp.concatenate([f[0], f[1], jnp.where(top, h[0], pltpu.roll(h[1], 4, 0))] + stats, axis=0)
    out_ref[...] = jnp.broadcast_to(piece.astype(BF16)[None], out_ref.shape)


def join_query(in_ref, out_ref):
    low = low_lanes((8, 128))
    top = lax.broadcasted_iota(jnp.int32, (8, 128), 0) < 4
    for y in range(NY):

        def heads(f0, f1):
            return jnp.where(low, f0, pltpu.roll(f1, 64, 1)), jnp.where(low, pltpu.roll(f0, 64, 1), f1)

        for z4 in range(0, NZ, 4):
            pieces = [[in_ref[c, z4 + i, y].astype(F32) for i in range(4)] for c in range(NC)]
            for p in range(2):
                tiles = [heads(pieces[0][i][8 * p : 8 * p + 8], pieces[1][i][8 * p : 8 * p + 8]) for i in range(4)]
                ends = []
                for i in (0, 2):
                    g = []
                    for c in range(NC):
                        even, odd = pieces[c][i][16:24], pieces[c][i + 1][16:24]
                        if p == 0:
                            g.append(jnp.where(top, even, pltpu.roll(odd, 4, 0)))
                        else:
                            g.append(jnp.where(top, pltpu.roll(even, 4, 0), odd))
                    ends.append(heads(g[0], g[1]))
                for u in range(2):
                    lanes = slice(((2 * p + u) * NY + y) * 128, ((2 * p + u) * NY + y) * 128 + 128)
                    for i in (0, 2):
                        r = 8 * (z4 + i)
                        both = jnp.concatenate([tiles[i][u], tiles[i + 1][u]], axis=0)
                        out_ref[r : r + 16, lanes] = both.astype(BF16)
                    r = 64 + 4 * z4
                    both = jnp.concatenate([ends[0][u], ends[1][u]], axis=0)
                    out_ref[r : r + 16, lanes] = both.astype(BF16)


def memory_grads(in_ref, kv_ref, q0, q1, q2, q3, k_ref, v_ref):
    low = low_lanes((BLOCK, 128))
    for y in range(NY):
        outs = []
        for c in range(NC):
            h = y * NC + c
            logs, offsets = [], []
            for t in range(3):
                piece = in_ref[c, t, y].astype(F32)
                logs.append(piece[24:25] + piece[25:26] + piece[26:27])
                offsets.append(piece[27:28] + piece[28:29] + piece[29:30])
            lse = jnp.concatenate(logs, axis=1)
            offset = jnp.concatenate(offsets, axis=1)
            q, g = halves(jnp.concatenate([q0[h], q1[h], q2[h], q3[h]], axis=0))
            kv = kv_ref[h]
            prob = jnp.exp(dot(kv, q, NT) - lse)
            ds = (prob * (dot(kv, g, NT) - offset)).astype(BF16)
            outs.append(dot(ds, q, NN) + dot(prob.astype(BF16), g, NN))
        a, b = outs
        lanes = slice(128 * y, 128 * y + 128)
        k_ref[:, lanes] = jnp.where(low, a, pltpu.roll(b, 64, 1)).astype(BF16)
        v_ref[:, lanes] = jnp.where(low, pltpu.roll(a, 64, 1), b).astype(BF16)


def around(parts):
    return parts[:1] + [
        lax.ppermute(parts[k], "row", [(i, (i + k) % NX) for i in range(NX)]) for k in range(1, NX)
    ]


def local(query, out_grad, keys, values):
    shape = jax.ShapeDtypeStruct
    z, y, c = lax.axis_index("z"), lax.axis_index("y"), lax.axis_index("core")
    x = lax.axis_index("row")
    at = jnp.stack([x, y, c]).astype(jnp.int32)
    zx = jnp.stack([z, x]).astype(jnp.int32)
    mega = 2**20

    home = call(pack_memory, shape((HEADS, BLOCK, 128), BF16), 2, moved=mega)(keys, values)
    memory = lax.all_to_all(home, ("y", "core"), 0, 0, tiled=True).reshape(MEMS, 128)
    mine = call(pack_query, [shape((MINE, 128), BF16)] * NX, 2, smem=1, moved=mega)(at, query, out_grad)
    mine = around(list(mine))
    every = call(pack_all_heads, [shape((HEADS, MINE, 128), BF16)] * NX, 2, smem=1, moved=3 * mega)(
        at, query, out_grad
    )
    every = around(list(every))

    work = 2 * MEMS * ROWS * 128
    part = call(
        local_part,
        shape((NZ * NX, 16, 128), F32),
        5,
        smem=1,
        scratch=[pltpu.VMEM((MEMS, ROWS), F32)] * 2 + [pltpu.VMEM((MEMS, ROWS), BF16)] * 2,
        flops=4 * work,
        moved=mega,
        exps=MEMS * ROWS,
    )(at, memory, *mine)
    part = lax.all_to_all(part, ("z", "row"), 0, 0, tiled=True)
    piece = call(
        add_query,
        shape((NZ * NY, 32, 128), BF16),
        1,
        smem=1,
        scratch=[pltpu.VMEM((NX, 128, 128), F32)],
        moved=mega,
    )(zx, part)
    piece = lax.all_to_all(piece, ("z", "y"), 0, 0, tiled=True).reshape(NZ, NY, 32, 128)
    pieces = lax.all_gather(piece, "core", axis=0, tiled=False)
    query_grad = call(join_query, shape((MINE, 4096), BF16), 1, moved=2 * mega)(pieces)
    key_grad, value_grad = call(
        memory_grads,
        [shape((BLOCK, 1024), BF16), shape((BLOCK, 1024), BF16)],
        6,
        flops=4 * work,
        moved=3 * mega,
        exps=MEMS * ROWS,
    )(pieces, home, *every)
    return (query_grad, key_grad, value_grad)


def solution(mesh):
    fine = Mesh(mesh.devices.reshape(NZ, NY, NC, NX), ("z", "y", "core", "row"))
    psg = ("z", "y", "core")
    placed = (P("row", None), P("row", None), P(psg, "row"), P(psg, "row"))
    return jax.shard_map(
        local,
        mesh=fine,
        in_specs=placed,
        out_specs=(P("row", None), P(psg, "row"), P(psg, "row")),
        check_vma=False,
    )
```

time: 122 us -> 127 us (1.041)
  blocking collectives: 46.3 us -> 22.1 us
  starting transfers between devices: 18.3 us -> 39.8 us
  between operations: 0.68 us -> 14.1 us
  waiting for transfers between devices: 42.2 us -> 31.6 us
  Pallas kernels: 11.4 us -> 14.9 us
    all_to_all x3 -> x1, waiting for transfers between devices: 35.2 us -> 5.82 us  [local(): lax.all_to_all(home, ('y', 'core'), 0, 0, tiled=True).reshape(MEMS, 128)]
    all_to_all x2 -> x1, blocking collectives: 43 us -> 22.1 us  [local(): lax.all_to_all(piece, ('z', 'y'), 0, 0, tiled=True).reshape(NZ, NY, 32, 128)]
    ppermute x0 -> x6, starting transfers between devices: none -> 18.1 us  [around(): lax.ppermute(parts[k], 'row', [(i, (i + k) % NX) for i in range(NX)])]
    ppermute x0 -> x6, waiting for transfers between devices: none -> 10.7 us  [around(): lax.ppermute(parts[k], 'row', [(i, (i + k) % NX) for i in range(NX)])]
    all_to_all x1, starting transfers between devices: 3.86 us -> 11.2 us  [local(): part = lax.all_to_all(part, ('z', 'row'), 0, 0, tiled=True)]
    all_to_all x1, waiting for transfers between devices: 7.02 us -> 12.6 us  [local(): part = lax.all_to_all(part, ('z', 'row'), 0, 0, tiled=True)]
    all_to_all x3 -> x1, starting transfers between devices: 14.5 us -> 10.4 us  [local(): lax.all_to_all(home, ('y', 'core'), 0, 0, tiled=True).reshape(MEMS, 128)]
    all_gather x1 -> x0, blocking collectives: 3.27 us -> none  [local(): pieces = lax.all_gather(piece, 'core', axis=0, tiled=False)]
  transfers between devices with their start and end apart: 4 -> 9, of which waited for: 4 -> 6; matrix products, arithmetic and copies ran while one was open for 0% -> 0% of each run, Pallas kernels for 5% -> 2%
where the time goes in v2:
time: 127 us; the launch traced here: 126 us
  starting transfers between devices  39.8 us (31%)
  waiting for transfers between devices  31.6 us (25%)
  blocking collectives  22.1 us (17%)
  Pallas kernels  14.9 us (12%)
  between operations  14.1 us (11%)
  local copies, waits for them, and re-layouts  3.13 us (2%)
    all_to_all x1, blocking collectives, local(): lax.all_to_all(piece, ('z', 'y'), 0, 0, tiled=True).reshape(NZ, NY, 32, 128)  22.1 us
    ppermute x6, starting transfers between devices, around(): lax.ppermute(parts[k], 'row', [(i, (i + k) % NX) for i in range(NX)])  18.1 us
    all_to_all x1, waiting for transfers between devices, local(): part = lax.all_to_all(part, ('z', 'row'), 0, 0, tiled=True)  12.6 us
    all_to_all x1, starting transfers between devices, local(): part = lax.all_to_all(part, ('z', 'row'), 0, 0, tiled=True)  11.2 us
    ppermute x6, waiting for transfers between devices, around(): lax.ppermute(parts[k], 'row', [(i, (i + k) % NX) for i in range(NX)])  10.7 us
    all_to_all x1, starting transfers between devices, local(): lax.all_to_all(home, ('y', 'core'), 0, 0, tiled=True).reshape(MEMS, 128)  10.4 us
    all_to_all x1, waiting for transfers between devices, local(): lax.all_to_all(home, ('y', 'core'), 0, 0, tiled=True).reshape(MEMS, 128)  5.82 us
    pallas_call x1, Pallas kernels, local(): call(memory_grads, [shape((BLOCK, 1024), BF16), shape((BLOCK, 1024), BF16...  5.32 us
  transfers between devices with their start and end apart: 9, of which 6 were waited for; matrix products, arithmetic and copies ran while one was open for 0% of the time, Pallas kernels for 2%

profile of v2, /device:TPU:1, one launch (start us, length us, event | category | flops | bytes accessed | tf_op | source)
XLA Modules:
  0.0 125.7 jit_solution(968370439583948363)
XLA Ops:
  7.2 0.9 copy-done.4
  8.1 0.9 copy-done.5
  9.1 1.0 shard_map.67.kv_ref
  10.1 10.4 %all-to-all-start = ((bf16[16,128,128]{2,1,0:T(8,128)(2,1)}), bf16[16,128,128]{2,1,0:T(8,128)(2,1)S(1)}, u32[]{:S(2)}, u32[]{:S(2)}) async-start(bf16[16,128,128]{2,1,0:T(8,128)(2,1)} %shard_map.67.kv_ref), calls=%async_computation | async-start | bytes 1048576 | tf_op jit(solution)/shard_map/all_to_all | solution.py:249
  21.2 1.9 %collective-permute-start = (bf16[96,128]{1,0:T(8,128)(2,1)S(1)}, bf16[96,128]{1,0:T(8,128)(2,1)S(1)}, u32[]{:S(2)}, u32[]{:S(2)}) collective-permute-start(bf16[96,128]{1,0:T(8,128)(2,1)S(1)} %get-tuple-element.14), channel_id=1, source_target_pairs={{0,1},{1,2},{2,3},{3,0},{4,5},{5,6},{6,7},{7,4},{8,9},{9,10},{10,1... | collective-permute-start | bytes 73736 | tf_op jit(solution)/shard_map/ppermute | solution.py:236
  23.2 4.0 %collective-permute-start.1 = (bf16[96,128]{1,0:T(8,128)(2,1)S(1)}, bf16[96,128]{1,0:T(8,128)(2,1)S(1)}, u32[]{:S(2)}, u32[]{:S(2)}) collective-permute-start(bf16[96,128]{1,0:T(8,128)(2,1)S(1)} %get-tuple-element.15), channel_id=1, source_target_pairs={{0,2},{1,3},{2,0},{3,1},{4,6},{5,7},{6,4},{7,5},{8,10},{9,11},{10,... | collective-permute-start | bytes 73736 | tf_op jit(solution)/shard_map/ppermute | solution.py:236
  27.1 3.1 %collective-permute-start.2 = (bf16[96,128]{1,0:T(8,128)(2,1)S(1)}, bf16[96,128]{1,0:T(8,128)(2,1)S(1)}, u32[]{:S(2)}, u32[]{:S(2)}) collective-permute-start(bf16[96,128]{1,0:T(8,128)(2,1)S(1)} %get-tuple-element.16), channel_id=1, source_target_pairs={{0,3},{1,0},{2,1},{3,2},{4,7},{5,4},{6,5},{7,6},{8,11},{9,8},{10,9... | collective-permute-start | bytes 73736 | tf_op jit(solution)/shard_map/ppermute | solution.py:236
  30.2 1.8 %collective-permute-done.2.q3 = bf16[96,128]{1,0:T(8,128)(2,1)S(1)} collective-permute-done((bf16[96,128]{1,0:T(8,128)(2,1)S(1)}, bf16[96,128]{1,0:T(8,128)(2,1)S(1)}, u32[]{:S(2)}, u32[]{:S(2)}) %collective-permute-start.2) | collective-permute-done | bytes 24608 | tf_op jit(solution)/shard_map/ppermute | solution.py:236
  32.0 5.8 %all-to-all-done = bf16[16,128,128]{2,1,0:T(8,128)(2,1)S(1)} async-done(((bf16[16,128,128]{2,1,0:T(8,128)(2,1)}), bf16[16,128,128]{2,1,0:T(8,128)(2,1)S(1)}, u32[]{:S(2)}, u32[]{:S(2)}) %all-to-all-start) | async-done | bytes 524320 | tf_op jit(solution)/shard_map/all_to_all | solution.py:249
  37.8 4.2 %shard_map.69 = f32[32,16,128]{2,1,0:T(8,128)} custom-call(s32[3]{0:T(128)S(1)} %pad_add_fusion.1.at_ref, bf16[2048,128]{1,0:T(8,128)(2,1)S(1)} %bitcast.6, bf16[96,128]{1,0:T(8,128)(2,1)S(1)} %get-tuple-element.13.q0, bf16[96,128]{1,0:T(8,128)(2,1)S(1)} %collective-permute-done.q1, bf16[96,128]{1,0:T(8,128)(2,1)S(1)} %collective-permute-done.1.q2, ...), custom_call_target="tpu_custom_call" | custom-call | flops 805306368 | bytes 1048576 | tf_op jit(solution)/shard_map/pallas_call | solution.py:258
  42.0 11.2 %all-to-all-start.1 = ((f32[32,16,128]{2,1,0:T(8,128)}), f32[32,16,128]{2,1,0:T(8,128)S(1)}, u32[]{:S(2)}, u32[]{:S(2)}) async-start(f32[32,16,128]{2,1,0:T(8,128)} %shard_map.69), calls=%async_computation.1 | async-start | bytes 524288 | tf_op jit(solution)/shard_map/all_to_all | solution.py:268
  53.4 12.6 %all-to-all-done.1.in_ref = f32[32,16,128]{2,1,0:T(8,128)S(1)} async-done(((f32[32,16,128]{2,1,0:T(8,128)}), f32[32,16,128]{2,1,0:T(8,128)S(1)}, u32[]{:S(2)}, u32[]{:S(2)}) %all-to-all-start.1) | async-done | bytes 262176 | tf_op jit(solution)/shard_map/all_to_all | solution.py:268
  66.0 1.2 shard_map.70
  67.2 22.1 %all_to_all.15 = bf16[64,32,128]{2,1,0:T(8,128)(2,1)} all-to-all(bf16[64,32,128]{2,1,0:T(8,128)(2,1)S(1)} %shard_map.70), channel_id=1, replica_groups=mesh['z'=8,'y'=8,'core'=2,'row'=4] {'z','y'}, dimensions={0} | all-to-all | bytes 1048576 | tf_op jit(solution)/shard_map/all_to_all | solution.py:277
  89.2 1.2 shard_map.72
  90.5 1.9 %collective-permute-start.3 = (bf16[16,96,128]{2,1,0:T(8,128)(2,1)S(1)}, bf16[16,96,128]{2,1,0:T(8,128)(2,1)S(1)}, u32[]{:S(2)}, u32[]{:S(2)}) collective-permute-start(bf16[16,96,128]{2,1,0:T(8,128)(2,1)S(1)} %get-tuple-element.18), channel_id=1, source_target_pairs={{0,1},{1,2},{2,3},{3,0},{4,5},{5,6},{6,7},{7,4},{8,9},{9,10},{10,1... | collective-permute-start | bytes 1179656 | tf_op jit(solution)/shard_map/ppermute | solution.py:236
  92.4 4.2 %collective-permute-start.4 = (bf16[16,96,128]{2,1,0:T(8,128)(2,1)S(1)}, bf16[16,96,128]{2,1,0:T(8,128)(2,1)S(1)}, u32[]{:S(2)}, u32[]{:S(2)}) collective-permute-start(bf16[16,96,128]{2,1,0:T(8,128)(2,1)S(1)} %get-tuple-element.19), channel_id=1, source_target_pairs={{0,2},{1,3},{2,0},{3,1},{4,6},{5,7},{6,4},{7,5},{8,10},{9,11},{10,... | collective-permute-start | bytes 1179656 | tf_op jit(solution)/shard_map/ppermute | solution.py:236
  96.6 3.1 %collective-permute-start.5 = (bf16[16,96,128]{2,1,0:T(8,128)(2,1)S(1)}, bf16[16,96,128]{2,1,0:T(8,128)(2,1)S(1)}, u32[]{:S(2)}, u32[]{:S(2)}) collective-permute-start(bf16[16,96,128]{2,1,0:T(8,128)(2,1)S(1)} %get-tuple-element.20), channel_id=1, source_target_pairs={{0,3},{1,0},{2,1},{3,2},{4,7},{5,4},{6,5},{7,6},{8,11},{9,8},{10,9... | collective-permute-start | bytes 1179656 | tf_op jit(solution)/shard_map/ppermute | solution.py:236
  99.7 2.5 %all-gather.2.cloned.1.call-done.in_ref = bf16[2,8,8,32,128]{4,3,2,1,0:T(8,128)(2,1)} async-done(((bf16[1,8,8,32,128]{4,3,2,1,0:T(8,128)(2,1)}), bf16[2,8,8,32,128]{4,3,2,1,0:T(8,128)(2,1)}) %all-gather.2.cloned.1.call-update) | async-done | bytes 1048592 | tf_op jit(solution)/shard_map/all_gather | solution.py:278
  102.2 1.2 copy-done
  103.4 1.2 shard_map.71
  104.6 4.6 %collective-permute-done.4.q2 = bf16[16,96,128]{2,1,0:T(8,128)(2,1)S(1)} collective-permute-done((bf16[16,96,128]{2,1,0:T(8,128)(2,1)S(1)}, bf16[16,96,128]{2,1,0:T(8,128)(2,1)S(1)}, u32[]{:S(2)}, u32[]{:S(2)}) %collective-permute-start.4) | collective-permute-done | bytes 393248 | tf_op jit(solution)/shard_map/ppermute | solution.py:236
  109.3 4.3 %collective-permute-done.5.q3 = bf16[16,96,128]{2,1,0:T(8,128)(2,1)S(1)} collective-permute-done((bf16[16,96,128]{2,1,0:T(8,128)(2,1)S(1)}, bf16[16,96,128]{2,1,0:T(8,128)(2,1)S(1)}, u32[]{:S(2)}, u32[]{:S(2)}) %collective-permute-start.5) | collective-permute-done | bytes 393248 | tf_op jit(solution)/shard_map/ppermute | solution.py:236
  113.6 5.3 %shard_map.73 = (bf16[128,1024]{1,0:T(8,128)(2,1)}, bf16[128,1024]{1,0:T(8,128)(2,1)}) custom-call(bf16[2,8,8,32,128]{4,3,2,1,0:T(8,128)(2,1)S(1)} %copy-done.1, bf16[16,128,128]{2,1,0:T(8,128)(2,1)} %shard_map.67.kv_ref, bf16[16,96,128]{2,1,0:T(8,128)(2,1)S(1)} %get-tuple-element.17.q0, bf16[16,96,128]{2,1,0:T(8,128)(2,1)S(1)} %collective-permute-done.3.q1, ...), custom_call_target="tpu_custom_call" | custom-call | flops 805306368 | bytes 3145728 | tf_op jit(solution)/shard_map/pallas_call | solution.py:280
  (17 shorter events, 0.9 us)
Async XLA Ops:
  7.2 1.0 copy-start.4
  8.1 0.9 copy-start.5
  9.1 11.5 %copy-start.3 = (bf16[96,4096]{1,0:T(8,128)(2,1)S(1)}, bf16[96,4096]{1,0:T(8,128)(2,1)}, u32[]{:S(2)}) copy-start(bf16[96,4096]{1,0:T(8,128)(2,1)} %g_ref.3) | copy-start | bytes 2359300
  10.1 10.5 %copy-start.2 = (bf16[96,4096]{1,0:T(8,128)(2,1)S(1)}, bf16[96,4096]{1,0:T(8,128)(2,1)}, u32[]{:S(2)}) copy-start(bf16[96,4096]{1,0:T(8,128)(2,1)} %q_ref.3) | copy-start | bytes 2359300
  10.1 27.7 %all-to-all-start = ((bf16[16,128,128]{2,1,0:T(8,128)(2,1)}), bf16[16,128,128]{2,1,0:T(8,128)(2,1)S(1)}, u32[]{:S(2)}, u32[]{:S(2)}) async-start(bf16[16,128,128]{2,1,0:T(8,128)(2,1)} %shard_map.67.kv_ref), calls=%async_computation | async-start | bytes 1048576 | tf_op jit(solution)/shard_map/all_to_all | solution.py:249
  21.2 9.0 %collective-permute-start = (bf16[96,128]{1,0:T(8,128)(2,1)S(1)}, bf16[96,128]{1,0:T(8,128)(2,1)S(1)}, u32[]{:S(2)}, u32[]{:S(2)}) collective-permute-start(bf16[96,128]{1,0:T(8,128)(2,1)S(1)} %get-tuple-element.14), channel_id=1, source_target_pairs={{0,1},{1,2},{2,3},{3,0},{4,5},{5,6},{6,7},{7,4},{8,9},{9,10},{10,1... | collective-permute-start | bytes 73736 | tf_op jit(solution)/shard_map/ppermute | solution.py:236
  23.2 7.1 %collective-permute-start.1 = (bf16[96,128]{1,0:T(8,128)(2,1)S(1)}, bf16[96,128]{1,0:T(8,128)(2,1)S(1)}, u32[]{:S(2)}, u32[]{:S(2)}) collective-permute-start(bf16[96,128]{1,0:T(8,128)(2,1)S(1)} %get-tuple-element.15), channel_id=1, source_target_pairs={{0,2},{1,3},{2,0},{3,1},{4,6},{5,7},{6,4},{7,5},{8,10},{9,11},{10,... | collective-permute-start | bytes 73736 | tf_op jit(solution)/shard_map/ppermute | solution.py:236
  27.1 4.9 %collective-permute-start.2 = (bf16[96,128]{1,0:T(8,128)(2,1)S(1)}, bf16[96,128]{1,0:T(8,128)(2,1)S(1)}, u32[]{:S(2)}, u32[]{:S(2)}) collective-permute-start(bf16[96,128]{1,0:T(8,128)(2,1)S(1)} %get-tuple-element.16), channel_id=1, source_target_pairs={{0,3},{1,0},{2,1},{3,2},{4,7},{5,4},{6,5},{7,6},{8,11},{9,8},{10,9... | collective-permute-start | bytes 73736 | tf_op jit(solution)/shard_map/ppermute | solution.py:236
  42.0 23.9 %all-to-all-start.1 = ((f32[32,16,128]{2,1,0:T(8,128)}), f32[32,16,128]{2,1,0:T(8,128)S(1)}, u32[]{:S(2)}, u32[]{:S(2)}) async-start(f32[32,16,128]{2,1,0:T(8,128)} %shard_map.69), calls=%async_computation.1 | async-start | bytes 524288 | tf_op jit(solution)/shard_map/all_to_all | solution.py:268
  53.3 48.9 %all-gather.2.cloned.1.call-start = ((), (), s32[]{:S(2)}) async-start(), calls=%async_computation.3 | async-start | bytes 1572864 | tf_op jit(solution)/shard_map/all_gather | solution.py:278
  90.5 14.2 %collective-permute-start.3 = (bf16[16,96,128]{2,1,0:T(8,128)(2,1)S(1)}, bf16[16,96,128]{2,1,0:T(8,128)(2,1)S(1)}, u32[]{:S(2)}, u32[]{:S(2)}) collective-permute-start(bf16[16,96,128]{2,1,0:T(8,128)(2,1)S(1)} %get-tuple-element.18), channel_id=1, source_target_pairs={{0,1},{1,2},{2,3},{3,0},{4,5},{5,6},{6,7},{7,4},{8,9},{9,10},{10,1... | collective-permute-start | bytes 1179656 | tf_op jit(solution)/shard_map/ppermute | solution.py:236
  92.4 16.9 %collective-permute-start.4 = (bf16[16,96,128]{2,1,0:T(8,128)(2,1)S(1)}, bf16[16,96,128]{2,1,0:T(8,128)(2,1)S(1)}, u32[]{:S(2)}, u32[]{:S(2)}) collective-permute-start(bf16[16,96,128]{2,1,0:T(8,128)(2,1)S(1)} %get-tuple-element.19), channel_id=1, source_target_pairs={{0,2},{1,3},{2,0},{3,1},{4,6},{5,7},{6,4},{7,5},{8,10},{9,11},{10,... | collective-permute-start | bytes 1179656 | tf_op jit(solution)/shard_map/ppermute | solution.py:236
  96.6 17.0 %collective-permute-start.5 = (bf16[16,96,128]{2,1,0:T(8,128)(2,1)S(1)}, bf16[16,96,128]{2,1,0:T(8,128)(2,1)S(1)}, u32[]{:S(2)}, u32[]{:S(2)}) collective-permute-start(bf16[16,96,128]{2,1,0:T(8,128)(2,1)S(1)} %get-tuple-element.20), channel_id=1, source_target_pairs={{0,3},{1,0},{2,1},{3,2},{4,7},{5,4},{6,5},{7,6},{8,11},{9,8},{10,9... | collective-permute-start | bytes 1179656 | tf_op jit(solution)/shard_map/ppermute | solution.py:236
  102.2 1.2 copy-start
  103.4 10.2 %copy-start.1 = (bf16[2,8,8,32,128]{4,3,2,1,0:T(8,128)(2,1)S(1)}, bf16[2,8,8,32,128]{4,3,2,1,0:T(8,128)(2,1)}, u32[]{:S(2)}) copy-start(bf16[2,8,8,32,128]{4,3,2,1,0:T(8,128)(2,1)} %all-gather.2.cloned.1.call-done.in_ref) | copy-start | bytes 3145732
Sparse Core Ops, SparseCore 0:
  89.4 12.7 all-gather.1

commit v3 on v2

--- a/solution.py
+++ b/solution.py
@@ -17,6 +17,7 @@
 STEP = 256
 NT = (((1,), (1,)), ((), ()))
 TN = (((0,), (0,)), ((), ()))
+SWAP = [(0, 1), (1, 0)]
 NN = (((1,), (0,)), ((), ()))
 
 VMEM = pl.BlockSpec(memory_space=pltpu.VMEM)
@@ -54,19 +55,7 @@
 
 
 def pack_query(at_ref, q_ref, g_ref, *outs):
-    x, y, c = at_ref[0], at_ref[1], at_ref[2]
-    low = low_lanes((MINE, 128))
-    for k in range(NX):
-        lanes = pl.ds(pl.multiple_of((lax.rem(x + k, NX) * NY + y) * 128, 128), 128)
-        q = q_ref[:, lanes].astype(F32)
-        g = g_ref[:, lanes].astype(F32)
-        first = jnp.where(low, q, pltpu.roll(g, 64, 1))
-        second = jnp.where(low, pltpu.roll(q, 64, 1), g)
-        outs[k][...] = jnp.where(c == 0, first, second).astype(BF16)
-
-
-def pack_all_heads(at_ref, q_ref, g_ref, *outs):
-    x = at_ref[0]
+    x, c = at_ref[0], at_ref[2]
     low = low_lanes((MINE, 128))
     for k in range(NX):
         start = lax.rem(x + k, NX) * 1024
@@ -74,8 +63,11 @@
             lanes = pl.ds(pl.multiple_of(start + 128 * t, 128), 128)
             q = q_ref[:, lanes].astype(F32)
             g = g_ref[:, lanes].astype(F32)
-            outs[k][2 * t] = jnp.where(low, q, pltpu.roll(g, 64, 1)).astype(BF16)
-            outs[k][2 * t + 1] = jnp.where(low, pltpu.roll(q, 64, 1), g).astype(BF16)
+            first = jnp.where(low, q, pltpu.roll(g, 64, 1))
+            second = jnp.where(low, pltpu.roll(q, 64, 1), g)
+            outs[k][t] = jnp.where(c == 0, first, second).astype(BF16)
+            if k == 0:
+                outs[NX][t] = jnp.where(c == 0, second, first).astype(BF16)
 
 
 def halves(qg):
@@ -85,8 +77,8 @@
 
 
 def local_part(at_ref, kv_ref, q0, q1, q2, q3, out_ref, e_ref, gp_ref, ds_ref, p_ref):
-    x = at_ref[0]
-    q, g = halves(jnp.concatenate([q0[...], q1[...], q2[...], q3[...]], axis=0))
+    x, y = at_ref[0], at_ref[1]
+    q, g = halves(jnp.concatenate([q0[y], q1[y], q2[y], q3[y]], axis=0))
     peak = None
     for j in range(0, MEMS, STEP):
         s = dot(kv_ref[j : j + STEP, :], q, NT)
@@ -174,7 +166,12 @@
     out_ref[...] = jnp.broadcast_to(piece.astype(BF16)[None], out_ref.shape)
 
 
-def join_query(in_ref, out_ref):
+def by_core(at_ref, a, b):
+    first = at_ref[0] == 0
+    return jnp.where(first, a, b), jnp.where(first, b, a)
+
+
+def join_query(at_ref, own_ref, other_ref, out_ref):
     low = low_lanes((8, 128))
     top = lax.broadcasted_iota(jnp.int32, (8, 128), 0) < 4
     for y in range(NY):
@@ -183,7 +180,9 @@
             return jnp.where(low, f0, pltpu.roll(f1, 64, 1)), jnp.where(low, pltpu.roll(f0, 64, 1), f1)
 
         for z4 in range(0, NZ, 4):
-            pieces = [[in_ref[c, z4 + i, y].astype(F32) for i in range(4)] for c in range(NC)]
+            where = [(z4 + i) * NY + y for i in range(4)]
+            pairs = [by_core(at_ref, own_ref[w].astype(F32), other_ref[w].astype(F32)) for w in where]
+            pieces = [[pairs[i][c] for i in range(4)] for c in range(NC)]
             for p in range(2):
                 tiles = [heads(pieces[0][i][8 * p : 8 * p + 8], pieces[1][i][8 * p : 8 * p + 8]) for i in range(4)]
                 ends = []
@@ -207,25 +206,34 @@
                     out_ref[r : r + 16, lanes] = both.astype(BF16)
 
 
-def memory_grads(in_ref, kv_ref, q0, q1, q2, q3, k_ref, v_ref):
+def head_grads(told_ref, y, kv, qs):
+    logs, offsets = [], []
+    for t in range(3):
+        piece = told_ref[t * NY + y].astype(F32)
+        logs.append(piece[24:25] + piece[25:26] + piece[26:27])
+        offsets.append(piece[27:28] + piece[28:29] + piece[29:30])
+    lse = jnp.concatenate(logs, axis=1)
+    offset = jnp.concatenate(offsets, axis=1)
+    q, g = halves(jnp.concatenate([q_ref[y] for q_ref in qs], axis=0))
+    prob = jnp.exp(dot(kv, q, NT) - lse)
+    ds = (prob * (dot(kv, g, NT) - offset)).astype(BF16)
+    return dot(ds, q, NN) + dot(prob.astype(BF16), g, NN)
+
+
+def own_grads(core_ref, told_ref, kv_ref, q0, q1, q2, q3, out_ref):
+    c = core_ref[0]
+    for y in range(NY):
+        out_ref[y] = head_grads(told_ref, y, kv_ref[2 * y + c], (q0, q1, q2, q3)).astype(BF16)
+
+
+def other_grads(core_ref, told_ref, kv_ref, q0, q1, q2, q3, own_ref, k_ref, v_ref):
+    c = core_ref[0]
     low = low_lanes((BLOCK, 128))
     for y in range(NY):
-        outs = []
-        for c in range(NC):
-            h = y * NC + c
-            logs, offsets = [], []
-            for t in range(3):
-                piece = in_ref[c, t, y].astype(F32)
-                logs.append(piece[24:25] + piece[25:26] + piece[26:27])
-                offsets.append(piece[27:28] + piece[28:29] + piece[29:30])
-            lse = jnp.concatenate(logs, axis=1)
-            offset = jnp.concatenate(offsets, axis=1)
-            q, g = halves(jnp.concatenate([q0[h], q1[h], q2[h], q3[h]], axis=0))
-            kv = kv_ref[h]
-            prob = jnp.exp(dot(kv, q, NT) - lse)
-            ds = (prob * (dot(kv, g, NT) - offset)).astype(BF16)
-            outs.append(dot(ds, q, NN) + dot(prob.astype(BF16), g, NN))
-        a, b = outs
+        other = head_grads(told_ref, y, kv_ref[2 * y + 1 - c], (q0, q1, q2, q3))
+        own = own_ref[y].astype(F32)
+        a = jnp.where(c == 0, own, other)
+        b = jnp.where(c == 0, other, own)
         lanes = slice(128 * y, 128 * y + 128)
         k_ref[:, lanes] = jnp.where(low, a, pltpu.roll(b, 64, 1)).astype(BF16)
         v_ref[:, lanes] = jnp.where(low, pltpu.roll(a, 64, 1), b).astype(BF16)
@@ -243,16 +251,16 @@
     x = lax.axis_index("row")
     at = jnp.stack([x, y, c]).astype(jnp.int32)
     zx = jnp.stack([z, x]).astype(jnp.int32)
+    corez = c.astype(jnp.int32)[None]
     mega = 2**20
 
     home = call(pack_memory, shape((HEADS, BLOCK, 128), BF16), 2, moved=mega)(keys, values)
     memory = lax.all_to_all(home, ("y", "core"), 0, 0, tiled=True).reshape(MEMS, 128)
-    mine = call(pack_query, [shape((MINE, 128), BF16)] * NX, 2, smem=1, moved=mega)(at, query, out_grad)
-    mine = around(list(mine))
-    every = call(pack_all_heads, [shape((HEADS, MINE, 128), BF16)] * NX, 2, smem=1, moved=3 * mega)(
+    *mine, rest = call(pack_query, [shape((NY, MINE, 128), BF16)] * (NX + 1), 2, smem=1, moved=3 * mega)(
         at, query, out_grad
     )
-    every = around(list(every))
+    mine = around(mine)
+    rest = [rest] + [lax.ppermute(a, "core", SWAP) for a in mine[1:]]
 
     work = 2 * MEMS * ROWS * 128
     part = call(
@@ -274,17 +282,22 @@
         scratch=[pltpu.VMEM((NX, 128, 128), F32)],
         moved=mega,
     )(zx, part)
-    piece = lax.all_to_all(piece, ("z", "y"), 0, 0, tiled=True).reshape(NZ, NY, 32, 128)
-    pieces = lax.all_gather(piece, "core", axis=0, tiled=False)
-    query_grad = call(join_query, shape((MINE, 4096), BF16), 1, moved=2 * mega)(pieces)
+    piece, *rest = lax.optimization_barrier((piece, *rest))
+    piece = lax.all_to_all(piece, ("z", "y"), 0, 0, tiled=True)
+    other = lax.ppermute(piece, "core", SWAP)
+    query_grad = call(join_query, shape((MINE, 4096), BF16), 2, smem=1, moved=2 * mega)(corez, piece, other)
+    own = call(own_grads, shape((NY, BLOCK, 128), BF16), 6, smem=1, flops=2 * work, moved=mega, exps=MEMS * ROWS)(
+        corez, piece, home, *mine
+    )
     key_grad, value_grad = call(
-        memory_grads,
+        other_grads,
         [shape((BLOCK, 1024), BF16), shape((BLOCK, 1024), BF16)],
-        6,
-        flops=4 * work,
-        moved=3 * mega,
+        7,
+        smem=1,
+        flops=2 * work,
+        moved=2 * mega,
         exps=MEMS * ROWS,
-    )(pieces, home, *every)
+    )(corez, other, home, *rest, own)
     return (query_grad, key_grad, value_grad)
 
 

time: 127 us -> 99.4 us (0.78)
  waiting for transfers between devices: 31.6 us -> 9.73 us
  between operations: 14.1 us -> 0.77 us
  starting transfers between devices: 39.8 us -> 45.2 us
  blocking collectives: 22.1 us -> 25.5 us
    ppermute x0 -> x4, starting transfers between devices: none -> 14.5 us  [the longest x3 7.66 us: local(): rest = [rest] + [lax.ppermute(a, 'core', SWAP) for a in mine[1:]]]
    all_to_all x1, waiting for transfers between devices: 12.6 us -> 2.71 us  [local(): part = lax.all_to_all(part, ('z', 'row'), 0, 0, tiled=True)]
    ppermute x6 -> x3, starting transfers between devices: 18.1 us -> 8.95 us  [around(): lax.ppermute(parts[k], 'row', [(i, (i + k) % NX) for i in range(NX)])]
    all_to_all x1, waiting for transfers between devices: 5.82 us -> 0.2 us  [local(): lax.all_to_all(home, ('y', 'core'), 0, 0, tiled=True).reshape(MEMS, 128)]
    ppermute x6 -> x3, waiting for transfers between devices: 10.7 us -> 6.8 us  [around(): lax.ppermute(parts[k], 'row', [(i, (i + k) % NX) for i in range(NX)])]
    all_to_all x1, blocking collectives: 22.1 us -> 25.5 us  [local(): piece = lax.all_to_all(piece, ('z', 'y'), 0, 0, tiled=True)]
    all_gather x1 -> x0, waiting for transfers between devices: 2.52 us -> none  [local(): pieces = lax.all_gather(piece, 'core', axis=0, tiled=False)]
    unnamed x12 -> x8, local copies, waits for them, and re-layouts: 3.13 us -> 1.9 us
  transfers between devices with their start and end apart: 9 -> 9, of which waited for: 6 -> 5; matrix products, arithmetic and copies ran while one was open for 0% -> 0% of each run, Pallas kernels for 2% -> 5%
where the time goes in v3:
time: 99.4 us; the launch traced here: 98.7 us
  starting transfers between devices  45.2 us (45%)
  blocking collectives  25.5 us (26%)
  Pallas kernels  15.5 us (16%)
  waiting for transfers between devices  9.73 us (10%)
  local copies, waits for them, and re-layouts  1.9 us (2%)
    all_to_all x1, blocking collectives, local(): piece = lax.all_to_all(piece, ('z', 'y'), 0, 0, tiled=True)  25.5 us
    all_to_all x1, starting transfers between devices, local(): part = lax.all_to_all(part, ('z', 'row'), 0, 0, tiled=True)  11.3 us
    all_to_all x1, starting transfers between devices, local(): lax.all_to_all(home, ('y', 'core'), 0, 0, tiled=True).reshape(MEMS, 128)  10.4 us
    ppermute x3, starting transfers between devices, around(): lax.ppermute(parts[k], 'row', [(i, (i + k) % NX) for i in range(NX)])  8.95 us
    ppermute x3, starting transfers between devices, local(): rest = [rest] + [lax.ppermute(a, 'core', SWAP) for a in mine[1:]]  7.66 us
    ppermute x1, starting transfers between devices, local(): other = lax.ppermute(piece, 'core', SWAP)  6.86 us
    ppermute x3, waiting for transfers between devices, around(): lax.ppermute(parts[k], 'row', [(i, (i + k) % NX) for i in range(NX)])  6.8 us
    pallas_call x1, Pallas kernels, local(): call(local_part, shape((NZ * NX, 16, 128), F32), 5, smem=1, scratch=[pltp...  4.18 us
  transfers between devices with their start and end apart: 9, of which 5 were waited for; matrix products, arithmetic and copies ran while one was open for 0% of the time, Pallas kernels for 5%

profile of v3, /device:TPU:1, one launch (start us, length us, event | category | flops | bytes accessed | tf_op | source)
XLA Modules:
  0.0 98.7 jit_solution(800894457624070681)
XLA Ops:
  0.6 0.9 copy-done.2
  1.6 0.9 copy-done.3
  2.5 1.0 %shard_map.67.kv_ref = bf16[16,128,128]{2,1,0:T(8,128)(2,1)} custom-call(bf16[128,1024]{1,0:T(8,128)(2,1)S(1)} %copy-done.2, bf16[128,1024]{1,0:T(8,128)(2,1)S(1)} %copy-done.3), custom_call_target="tpu_custom_call" | custom-call | bytes 1048576 | tf_op jit(solution)/shard_map/pallas_call | solution.py:257
  3.6 10.4 %all-to-all-start = ((bf16[16,128,128]{2,1,0:T(8,128)(2,1)}), bf16[16,128,128]{2,1,0:T(8,128)(2,1)S(1)}, u32[]{:S(2)}, u32[]{:S(2)}) async-start(bf16[16,128,128]{2,1,0:T(8,128)(2,1)} %shard_map.67.kv_ref), calls=%async_computation | async-start | bytes 1048576 | tf_op jit(solution)/shard_map/all_to_all | solution.py:258
  14.0 1.3 %shard_map.68 = (bf16[8,96,128]{2,1,0:T(8,128)(2,1)S(1)}, bf16[8,96,128]{2,1,0:T(8,128)(2,1)S(1)}, bf16[8,96,128]{2,1,0:T(8,128)(2,1)S(1)}, bf16[8,96,128]{2,1,0:T(8,128)(2,1)S(1)}, bf16[8,96,128]{2,1,0:T(8,128)(2,1)S(1)}) custom-call(s32[3]{0:T(128)S(1)} %pad_add_fusion.1.at_ref, bf16[96,4096]{1,0:T(8,128)(2,1)S(1)} %copy-done, bf16[96,4096]{1,0:T(8,128)(2,1)S(1)} %copy-done.1), custom_call_target="tpu_custom_call" | custom-call | bytes 3145728 | tf_op jit(solution)/shard_map/pallas_call | solution.py:259
  15.3 1.9 %collective-permute-start = (bf16[8,96,128]{2,1,0:T(8,128)(2,1)S(1)}, bf16[8,96,128]{2,1,0:T(8,128)(2,1)S(1)}, u32[]{:S(2)}, u32[]{:S(2)}) collective-permute-start(bf16[8,96,128]{2,1,0:T(8,128)(2,1)S(1)} %get-tuple-element.16), channel_id=1, source_target_pairs={{0,1},{1,2},{2,3},{3,0},{4,5},{5,6},{6,7},{7,4},{8,9},{9,10},{10,1... | collective-permute-start | bytes 589832 | tf_op jit(solution)/shard_map/ppermute | solution.py:244
  17.2 4.0 %collective-permute-start.1 = (bf16[8,96,128]{2,1,0:T(8,128)(2,1)S(1)}, bf16[8,96,128]{2,1,0:T(8,128)(2,1)S(1)}, u32[]{:S(2)}, u32[]{:S(2)}) collective-permute-start(bf16[8,96,128]{2,1,0:T(8,128)(2,1)S(1)} %get-tuple-element.17), channel_id=1, source_target_pairs={{0,2},{1,3},{2,0},{3,1},{4,6},{5,7},{6,4},{7,5},{8,10},{9,11},{10,... | collective-permute-start | bytes 589832 | tf_op jit(solution)/shard_map/ppermute | solution.py:244
  21.2 3.1 %collective-permute-start.2 = (bf16[8,96,128]{2,1,0:T(8,128)(2,1)S(1)}, bf16[8,96,128]{2,1,0:T(8,128)(2,1)S(1)}, u32[]{:S(2)}, u32[]{:S(2)}) collective-permute-start(bf16[8,96,128]{2,1,0:T(8,128)(2,1)S(1)} %get-tuple-element.18), channel_id=1, source_target_pairs={{0,3},{1,0},{2,1},{3,2},{4,7},{5,4},{6,5},{7,6},{8,11},{9,8},{10,9... | collective-permute-start | bytes 589832 | tf_op jit(solution)/shard_map/ppermute | solution.py:244
  24.3 0.8 collective-permute-done.q1
  25.1 3.4 %collective-permute-done.1.q2 = bf16[8,96,128]{2,1,0:T(8,128)(2,1)S(1)} collective-permute-done((bf16[8,96,128]{2,1,0:T(8,128)(2,1)S(1)}, bf16[8,96,128]{2,1,0:T(8,128)(2,1)S(1)}, u32[]{:S(2)}, u32[]{:S(2)}) %collective-permute-start.1) | collective-permute-done | bytes 196640 | tf_op jit(solution)/shard_map/ppermute | solution.py:244
  28.5 2.6 %collective-permute-done.2.q3 = bf16[8,96,128]{2,1,0:T(8,128)(2,1)S(1)} collective-permute-done((bf16[8,96,128]{2,1,0:T(8,128)(2,1)S(1)}, bf16[8,96,128]{2,1,0:T(8,128)(2,1)S(1)}, u32[]{:S(2)}, u32[]{:S(2)}) %collective-permute-start.2) | collective-permute-done | bytes 196640 | tf_op jit(solution)/shard_map/ppermute | solution.py:244
  31.1 0.2 all-to-all-done
  31.3 4.2 %shard_map.69 = f32[32,16,128]{2,1,0:T(8,128)} custom-call(s32[3]{0:T(128)S(1)} %pad_add_fusion.1.at_ref, bf16[2048,128]{1,0:T(8,128)(2,1)S(1)} %bitcast.5, bf16[8,96,128]{2,1,0:T(8,128)(2,1)S(1)} %get-tuple-element.15.q0, bf16[8,96,128]{2,1,0:T(8,128)(2,1)S(1)} %collective-permute-done.q1, bf16[8,96,128]{2,1,0:T(8,128)(2,1)S(1)} %collective-permute-done.1.q2, ...), custom_call_target="tpu_custom_call" | custom-call | flops 805306368 | bytes 1048576 | tf_op jit(solution)/shard_map/pallas_call | solution.py:266
  35.5 11.3 %all-to-all-start.1 = ((f32[32,16,128]{2,1,0:T(8,128)}), f32[32,16,128]{2,1,0:T(8,128)S(1)}, u32[]{:S(2)}, u32[]{:S(2)}) async-start(f32[32,16,128]{2,1,0:T(8,128)} %shard_map.69), calls=%async_computation.1 | async-start | bytes 524288 | tf_op jit(solution)/shard_map/all_to_all | solution.py:276
  46.8 3.3 %collective-permute-start.3 = (bf16[8,96,128]{2,1,0:T(8,128)(2,1)S(1)}, bf16[8,96,128]{2,1,0:T(8,128)(2,1)S(1)}, u32[]{:S(2)}, u32[]{:S(2)}) collective-permute-start(bf16[8,96,128]{2,1,0:T(8,128)(2,1)S(1)} %collective-permute-done.q1), channel_id=1, source_target_pairs={{0,4},{4,0},{1,5},{5,1},{2,6},{6,2},{3,7},{7,3},{8,12},{12,8},{9,1... | collective-permute-start | bytes 589832 | tf_op jit(solution)/shard_map/ppermute | solution.py:263
  50.2 1.9 %collective-permute-start.4 = (bf16[8,96,128]{2,1,0:T(8,128)(2,1)S(1)}, bf16[8,96,128]{2,1,0:T(8,128)(2,1)S(1)}, u32[]{:S(2)}, u32[]{:S(2)}) collective-permute-start(bf16[8,96,128]{2,1,0:T(8,128)(2,1)S(1)} %collective-permute-done.1.q2), channel_id=1, source_target_pairs={{0,4},{4,0},{1,5},{5,1},{2,6},{6,2},{3,7},{7,3},{8,12},{12,8},{9,1... | collective-permute-start | bytes 589832 | tf_op jit(solution)/shard_map/ppermute | solution.py:263
  52.1 2.4 %collective-permute-start.5 = (bf16[8,96,128]{2,1,0:T(8,128)(2,1)S(1)}, bf16[8,96,128]{2,1,0:T(8,128)(2,1)S(1)}, u32[]{:S(2)}, u32[]{:S(2)}) collective-permute-start(bf16[8,96,128]{2,1,0:T(8,128)(2,1)S(1)} %collective-permute-done.2.q3), channel_id=1, source_target_pairs={{0,4},{4,0},{1,5},{5,1},{2,6},{6,2},{3,7},{7,3},{8,12},{12,8},{9,1... | collective-permute-start | bytes 589832 | tf_op jit(solution)/shard_map/ppermute | solution.py:263
  54.6 2.7 %all-to-all-done.1.in_ref = f32[32,16,128]{2,1,0:T(8,128)S(1)} async-done(((f32[32,16,128]{2,1,0:T(8,128)}), f32[32,16,128]{2,1,0:T(8,128)S(1)}, u32[]{:S(2)}, u32[]{:S(2)}) %all-to-all-start.1) | async-done | bytes 262176 | tf_op jit(solution)/shard_map/all_to_all | solution.py:276
  57.3 1.2 %shard_map.70 = bf16[64,32,128]{2,1,0:T(8,128)(2,1)S(1)} custom-call(s32[2]{0:T(128)S(1)} %pad_add_fusion.at_ref, f32[32,16,128]{2,1,0:T(8,128)S(1)} %all-to-all-done.1.in_ref), custom_call_target="tpu_custom_call" | custom-call | bytes 1048576 | tf_op jit(solution)/shard_map/pallas_call | solution.py:277
  58.5 25.5 %all_to_all.15.own_ref.told_ref = bf16[64,32,128]{2,1,0:T(8,128)(2,1)S(1)} all-to-all(bf16[64,32,128]{2,1,0:T(8,128)(2,1)S(1)} %shard_map.70), channel_id=1, replica_groups=mesh['z'=8,'y'=8,'core'=2,'row'=4] {'z','y'}, dimensions={0} | all-to-all | bytes 1048576 | tf_op jit(solution)/shard_map/all_to_all | solution.py:286
  84.0 6.9 %collective-permute-start.6 = (bf16[64,32,128]{2,1,0:T(8,128)(2,1)S(1)}, bf16[64,32,128]{2,1,0:T(8,128)(2,1)S(1)}, u32[]{:S(2)}, u32[]{:S(2)}) collective-permute-start(bf16[64,32,128]{2,1,0:T(8,128)(2,1)S(1)} %all_to_all.15.own_ref.told_ref), channel_id=1, source_target_pairs={{0,4},{4,0},{1,5},{5,1},{2,6},{6,2},{3,7},{7,3},{8,12},{12,8},{9,1... | collective-permute-start | bytes 1572872 | tf_op jit(solution)/shard_map/ppermute | solution.py:287
  90.9 2.8 %shard_map.72.own_ref = bf16[8,128,128]{2,1,0:T(8,128)(2,1)S(1)} custom-call(s32[1]{0:T(128)} %bitcast.at_ref.core_ref, bf16[64,32,128]{2,1,0:T(8,128)(2,1)S(1)} %all_to_all.15.own_ref.told_ref, bf16[16,128,128]{2,1,0:T(8,128)(2,1)} %shard_map.67.kv_ref, bf16[8,96,128]{2,1,0:T(8,128)(2,1)S(1)} %get-tuple-element.15.q0, ...), custom_call_target="tpu_custom_call" | custom-call | flops 402653184 | bytes 1048576 | tf_op jit(solution)/shard_map/pallas_call | solution.py:289
  93.7 1.3 %shard_map.71 = bf16[96,4096]{1,0:T(8,128)(2,1)} custom-call(s32[1]{0:T(128)} %bitcast.at_ref.core_ref, bf16[64,32,128]{2,1,0:T(8,128)(2,1)S(1)} %all_to_all.15.own_ref.told_ref, bf16[64,32,128]{2,1,0:T(8,128)(2,1)S(1)} %collective-permute-done.6.other_ref.told_ref), custom_call_target="tpu_custom_call" | custom-call | bytes 2097152 | tf_op jit(solution)/shard_map/pallas_call | solution.py:288
  95.0 3.7 %shard_map.73 = (bf16[128,1024]{1,0:T(8,128)(2,1)}, bf16[128,1024]{1,0:T(8,128)(2,1)}) custom-call(s32[1]{0:T(128)} %bitcast.at_ref.core_ref, bf16[64,32,128]{2,1,0:T(8,128)(2,1)S(1)} %collective-permute-done.6.other_ref.told_ref, bf16[16,128,128]{2,1,0:T(8,128)(2,1)} %shard_map.67.kv_ref, bf16[8,96,128]{2,1,0:T(8,128)(2,1)S(1)} %get-tuple-element.21.q0, ...), custom_call_target="tpu_custom_call" | custom-call | flops 402653184 | bytes 2097152 | tf_op jit(solution)/shard_map/pallas_call | solution.py:292
  (12 shorter events, 0.2 us)
Async XLA Ops:
  0.6 1.0 copy-start.2
  1.6 0.9 copy-start.3
  2.5 11.5 %copy-start.1 = (bf16[96,4096]{1,0:T(8,128)(2,1)S(1)}, bf16[96,4096]{1,0:T(8,128)(2,1)}, u32[]{:S(2)}) copy-start(bf16[96,4096]{1,0:T(8,128)(2,1)} %g_ref.1) | copy-start | bytes 2359300
  3.6 10.5 %copy-start = (bf16[96,4096]{1,0:T(8,128)(2,1)S(1)}, bf16[96,4096]{1,0:T(8,128)(2,1)}, u32[]{:S(2)}) copy-start(bf16[96,4096]{1,0:T(8,128)(2,1)} %q_ref.1) | copy-start | bytes 2359300
  3.6 27.7 %all-to-all-start = ((bf16[16,128,128]{2,1,0:T(8,128)(2,1)}), bf16[16,128,128]{2,1,0:T(8,128)(2,1)S(1)}, u32[]{:S(2)}, u32[]{:S(2)}) async-start(bf16[16,128,128]{2,1,0:T(8,128)(2,1)} %shard_map.67.kv_ref), calls=%async_computation | async-start | bytes 1048576 | tf_op jit(solution)/shard_map/all_to_all | solution.py:258
  15.3 9.8 %collective-permute-start = (bf16[8,96,128]{2,1,0:T(8,128)(2,1)S(1)}, bf16[8,96,128]{2,1,0:T(8,128)(2,1)S(1)}, u32[]{:S(2)}, u32[]{:S(2)}) collective-permute-start(bf16[8,96,128]{2,1,0:T(8,128)(2,1)S(1)} %get-tuple-element.16), channel_id=1, source_target_pairs={{0,1},{1,2},{2,3},{3,0},{4,5},{5,6},{6,7},{7,4},{8,9},{9,10},{10,1... | collective-permute-start | bytes 589832 | tf_op jit(solution)/shard_map/ppermute | solution.py:244
  17.2 11.3 %collective-permute-start.1 = (bf16[8,96,128]{2,1,0:T(8,128)(2,1)S(1)}, bf16[8,96,128]{2,1,0:T(8,128)(2,1)S(1)}, u32[]{:S(2)}, u32[]{:S(2)}) collective-permute-start(bf16[8,96,128]{2,1,0:T(8,128)(2,1)S(1)} %get-tuple-element.17), channel_id=1, source_target_pairs={{0,2},{1,3},{2,0},{3,1},{4,6},{5,7},{6,4},{7,5},{8,10},{9,11},{10,... | collective-permute-start | bytes 589832 | tf_op jit(solution)/shard_map/ppermute | solution.py:244
  21.2 9.9 %collective-permute-start.2 = (bf16[8,96,128]{2,1,0:T(8,128)(2,1)S(1)}, bf16[8,96,128]{2,1,0:T(8,128)(2,1)S(1)}, u32[]{:S(2)}, u32[]{:S(2)}) collective-permute-start(bf16[8,96,128]{2,1,0:T(8,128)(2,1)S(1)} %get-tuple-element.18), channel_id=1, source_target_pairs={{0,3},{1,0},{2,1},{3,2},{4,7},{5,4},{6,5},{7,6},{8,11},{9,8},{10,9... | collective-permute-start | bytes 589832 | tf_op jit(solution)/shard_map/ppermute | solution.py:244
  35.5 21.8 %all-to-all-start.1 = ((f32[32,16,128]{2,1,0:T(8,128)}), f32[32,16,128]{2,1,0:T(8,128)S(1)}, u32[]{:S(2)}, u32[]{:S(2)}) async-start(f32[32,16,128]{2,1,0:T(8,128)} %shard_map.69), calls=%async_computation.1 | async-start | bytes 524288 | tf_op jit(solution)/shard_map/all_to_all | solution.py:276
  46.8 11.7 %collective-permute-start.3 = (bf16[8,96,128]{2,1,0:T(8,128)(2,1)S(1)}, bf16[8,96,128]{2,1,0:T(8,128)(2,1)S(1)}, u32[]{:S(2)}, u32[]{:S(2)}) collective-permute-start(bf16[8,96,128]{2,1,0:T(8,128)(2,1)S(1)} %collective-permute-done.q1), channel_id=1, source_target_pairs={{0,4},{4,0},{1,5},{5,1},{2,6},{6,2},{3,7},{7,3},{8,12},{12,8},{9,1... | collective-permute-start | bytes 589832 | tf_op jit(solution)/shard_map/ppermute | solution.py:263
  50.2 8.3 %collective-permute-start.4 = (bf16[8,96,128]{2,1,0:T(8,128)(2,1)S(1)}, bf16[8,96,128]{2,1,0:T(8,128)(2,1)S(1)}, u32[]{:S(2)}, u32[]{:S(2)}) collective-permute-start(bf16[8,96,128]{2,1,0:T(8,128)(2,1)S(1)} %collective-permute-done.1.q2), channel_id=1, source_target_pairs={{0,4},{4,0},{1,5},{5,1},{2,6},{6,2},{3,7},{7,3},{8,12},{12,8},{9,1... | collective-permute-start | bytes 589832 | tf_op jit(solution)/shard_map/ppermute | solution.py:263
  52.1 6.4 %collective-permute-start.5 = (bf16[8,96,128]{2,1,0:T(8,128)(2,1)S(1)}, bf16[8,96,128]{2,1,0:T(8,128)(2,1)S(1)}, u32[]{:S(2)}, u32[]{:S(2)}) collective-permute-start(bf16[8,96,128]{2,1,0:T(8,128)(2,1)S(1)} %collective-permute-done.2.q3), channel_id=1, source_target_pairs={{0,4},{4,0},{1,5},{5,1},{2,6},{6,2},{3,7},{7,3},{8,12},{12,8},{9,1... | collective-permute-start | bytes 589832 | tf_op jit(solution)/shard_map/ppermute | solution.py:263
  84.0 9.7 %collective-permute-start.6 = (bf16[64,32,128]{2,1,0:T(8,128)(2,1)S(1)}, bf16[64,32,128]{2,1,0:T(8,128)(2,1)S(1)}, u32[]{:S(2)}, u32[]{:S(2)}) collective-permute-start(bf16[64,32,128]{2,1,0:T(8,128)(2,1)S(1)} %all_to_all.15.own_ref.told_ref), channel_id=1, source_target_pairs={{0,4},{4,0},{1,5},{5,1},{2,6},{6,2},{3,7},{7,3},{8,12},{12,8},{9,1... | collective-permute-start | bytes 1572872 | tf_op jit(solution)/shard_map/ppermute | solution.py:287

commit v4 on v3

--- a/solution.py
+++ b/solution.py
@@ -32,8 +32,20 @@
         in_specs=[SMEM] * smem + [VMEM] * n_in,
         out_specs=[VMEM] * len(outs) if outs else VMEM,
         scratch_shapes=list(scratch),
-        compiler_params=pltpu.CompilerParams(vmem_limit_bytes=40 * 2**20),
+        compiler_params=pltpu.CompilerParams(vmem_limit_bytes=24 * 2**20),
         cost_estimate=pl.CostEstimate(flops=flops, bytes_accessed=moved, transcendentals=exps),
+    )
+
+
+def fetching(body, out_shape, n_in, scratch):
+    return pl.pallas_call(
+        body,
+        out_shape=out_shape,
+        in_specs=[SMEM] + [pl.BlockSpec(memory_space=pl.ANY)] * n_in,
+        out_specs=[VMEM] * len(out_shape),
+        scratch_shapes=scratch,
+        compiler_params=pltpu.CompilerParams(vmem_limit_bytes=60 * 2**20),
+        cost_estimate=pl.CostEstimate(flops=0, bytes_accessed=2**20, transcendentals=0),
     )
 
 
@@ -45,13 +57,40 @@
     return lax.broadcasted_iota(jnp.int32, shape, len(shape) - 1) < 64
 
 
-def pack_memory(k_ref, v_ref, out_ref):
+def pack_memory(core_ref, k_hbm, v_hbm, out_ref, own_ref, away_ref, k_ref, v_ref, sems):
+    c = core_ref[0]
     low = low_lanes((BLOCK, 128))
+    copies = []
+    for i in range(2):
+        lanes = pl.ds(512 * i, 512)
+        copies.append(pltpu.make_async_copy(k_hbm.at[:, lanes], k_ref.at[:, lanes], sems.at[0, i]))
+        copies.append(pltpu.make_async_copy(v_hbm.at[:, lanes], v_ref.at[:, lanes], sems.at[1, i]))
+    for copy in copies:
+        copy.start()
     for t in range(HEADS // 2):
+        if t % 4 == 0:
+            copies[t // 2].wait()
+            copies[t // 2 + 1].wait()
         k = k_ref[:, 128 * t : 128 * t + 128].astype(F32)
         v = v_ref[:, 128 * t : 128 * t + 128].astype(F32)
-        out_ref[2 * t] = jnp.where(low, k, pltpu.roll(v, 64, 1)).astype(BF16)
-        out_ref[2 * t + 1] = jnp.where(low, pltpu.roll(k, 64, 1), v).astype(BF16)
+        first = jnp.where(low, k, pltpu.roll(v, 64, 1))
+        second = jnp.where(low, pltpu.roll(k, 64, 1), v)
+        out_ref[2 * t] = first.astype(BF16)
+        out_ref[2 * t + 1] = second.astype(BF16)
+        own_ref[t] = jnp.where(c == 0, first, second).astype(BF16)
+        away_ref[t] = jnp.where(c == 0, second, first).astype(BF16)
+
+
+def pack_mine(at_ref, q_ref, g_ref, *outs):
+    x, y, c = at_ref[0], at_ref[1], at_ref[2]
+    low = low_lanes((MINE, 128))
+    for k in range(NX):
+        lanes = pl.ds(pl.multiple_of((lax.rem(x + k, NX) * NY + y) * 128, 128), 128)
+        q = q_ref[:, lanes].astype(F32)
+        g = g_ref[:, lanes].astype(F32)
+        first = jnp.where(low, q, pltpu.roll(g, 64, 1))
+        second = jnp.where(low, pltpu.roll(q, 64, 1), g)
+        outs[k][...] = jnp.where(c == 0, first, second).astype(BF16)
 
 
 def pack_query(at_ref, q_ref, g_ref, *outs):
@@ -66,8 +105,6 @@
             first = jnp.where(low, q, pltpu.roll(g, 64, 1))
             second = jnp.where(low, pltpu.roll(q, 64, 1), g)
             outs[k][t] = jnp.where(c == 0, first, second).astype(BF16)
-            if k == 0:
-                outs[NX][t] = jnp.where(c == 0, second, first).astype(BF16)
 
 
 def halves(qg):
@@ -77,8 +114,8 @@
 
 
 def local_part(at_ref, kv_ref, q0, q1, q2, q3, out_ref, e_ref, gp_ref, ds_ref, p_ref):
-    x, y = at_ref[0], at_ref[1]
-    q, g = halves(jnp.concatenate([q0[y], q1[y], q2[y], q3[y]], axis=0))
+    x = at_ref[0]
+    q, g = halves(jnp.concatenate([q0[...], q1[...], q2[...], q3[...]], axis=0))
     peak = None
     for j in range(0, MEMS, STEP):
         s = dot(kv_ref[j : j + STEP, :], q, NT)
@@ -220,20 +257,18 @@
     return dot(ds, q, NN) + dot(prob.astype(BF16), g, NN)
 
 
-def own_grads(core_ref, told_ref, kv_ref, q0, q1, q2, q3, out_ref):
-    c = core_ref[0]
+def chip_grads(told_ref, own_ref, away_ref, q0, q1, q2, q3, mine_ref, sent_ref):
     for y in range(NY):
-        out_ref[y] = head_grads(told_ref, y, kv_ref[2 * y + c], (q0, q1, q2, q3)).astype(BF16)
-
-
-def other_grads(core_ref, told_ref, kv_ref, q0, q1, q2, q3, own_ref, k_ref, v_ref):
-    c = core_ref[0]
+        kv = jnp.concatenate([own_ref[y], away_ref[y]], axis=0)
+        out = head_grads(told_ref, y, kv, (q0, q1, q2, q3)).astype(BF16)
+        mine_ref[y] = out[:BLOCK]
+        sent_ref[y] = out[BLOCK:]
+
+
+def join_memory(core_ref, own_ref, other_ref, k_ref, v_ref):
     low = low_lanes((BLOCK, 128))
     for y in range(NY):
-        other = head_grads(told_ref, y, kv_ref[2 * y + 1 - c], (q0, q1, q2, q3))
-        own = own_ref[y].astype(F32)
-        a = jnp.where(c == 0, own, other)
-        b = jnp.where(c == 0, other, own)
+        a, b = by_core(core_ref, own_ref[y].astype(F32), other_ref[y].astype(F32))
         lanes = slice(128 * y, 128 * y + 128)
         k_ref[:, lanes] = jnp.where(low, a, pltpu.roll(b, 64, 1)).astype(BF16)
         v_ref[:, lanes] = jnp.where(low, pltpu.roll(a, 64, 1), b).astype(BF16)
@@ -254,13 +289,17 @@
     corez = c.astype(jnp.int32)[None]
     mega = 2**20
 
-    home = call(pack_memory, shape((HEADS, BLOCK, 128), BF16), 2, moved=mega)(keys, values)
+    half = shape((NY, BLOCK, 128), BF16)
+    home, home_own, home_away = fetching(
+        pack_memory,
+        [shape((HEADS, BLOCK, 128), BF16), half, half],
+        2,
+        [pltpu.VMEM((BLOCK, 1024), BF16)] * 2 + [pltpu.SemaphoreType.DMA((2, 2))],
+    )(corez, keys, values)
     memory = lax.all_to_all(home, ("y", "core"), 0, 0, tiled=True).reshape(MEMS, 128)
-    *mine, rest = call(pack_query, [shape((NY, MINE, 128), BF16)] * (NX + 1), 2, smem=1, moved=3 * mega)(
-        at, query, out_grad
-    )
-    mine = around(mine)
-    rest = [rest] + [lax.ppermute(a, "core", SWAP) for a in mine[1:]]
+    mine = call(pack_mine, [shape((MINE, 128), BF16)] * NX, 2, smem=1, moved=mega)(at, query, out_grad)
+    mine = around(list(mine))
+    away = lax.ppermute(home_away, "core", SWAP)
 
     work = 2 * MEMS * ROWS * 128
     part = call(
@@ -274,6 +313,8 @@
         exps=MEMS * ROWS,
     )(at, memory, *mine)
     part = lax.all_to_all(part, ("z", "row"), 0, 0, tiled=True)
+    heads = call(pack_query, [shape((NY, MINE, 128), BF16)] * NX, 2, smem=1, moved=3 * mega)(at, query, out_grad)
+    part, away, *heads = lax.optimization_barrier((part, away, *heads))
     piece = call(
         add_query,
         shape((NZ * NY, 32, 128), BF16),
@@ -282,22 +323,19 @@
         scratch=[pltpu.VMEM((NX, 128, 128), F32)],
         moved=mega,
     )(zx, part)
-    piece, *rest = lax.optimization_barrier((piece, *rest))
     piece = lax.all_to_all(piece, ("z", "y"), 0, 0, tiled=True)
+    heads = around(list(heads))
+    piece, *heads = lax.optimization_barrier((piece, *heads))
     other = lax.ppermute(piece, "core", SWAP)
+    grads, sent = call(chip_grads, [half, half], 7, flops=4 * work, moved=2 * mega, exps=MEMS * ROWS)(
+        piece, home_own, away, *heads
+    )
+    sent = lax.ppermute(sent, "core", SWAP)
     query_grad = call(join_query, shape((MINE, 4096), BF16), 2, smem=1, moved=2 * mega)(corez, piece, other)
-    own = call(own_grads, shape((NY, BLOCK, 128), BF16), 6, smem=1, flops=2 * work, moved=mega, exps=MEMS * ROWS)(
-        corez, piece, home, *mine
-    )
-    key_grad, value_grad = call(
-        other_grads,
-        [shape((BLOCK, 1024), BF16), shape((BLOCK, 1024), BF16)],
-        7,
-        smem=1,
-        flops=2 * work,
-        moved=2 * mega,
-        exps=MEMS * ROWS,
-    )(corez, other, home, *rest, own)
+    sent, query_grad = lax.optimization_barrier((sent, query_grad))
+    key_grad, value_grad = call(join_memory, [shape((BLOCK, 1024), BF16)] * 2, 2, smem=1, moved=mega)(
+        corez, grads, sent
+    )
     return (query_grad, key_grad, value_grad)
 
 

time: 99.4 us -> 95.4 us (0.960)
  blocking collectives: 25.5 us -> 0 us
  waiting for transfers between devices: 9.73 us -> 25.6 us
  starting transfers between devices: 45.2 us -> 53.3 us
  local copies, waits for them, and re-layouts: 1.9 us -> 0.02 us
    all_to_all x1 -> x0, blocking collectives: 25.5 us -> none  [local(): piece = lax.all_to_all(piece, ('z', 'y'), 0, 0, tiled=True)]
    ppermute x3 -> x6, starting transfers between devices: 8.95 us -> 18.1 us  [around(): lax.ppermute(parts[k], 'row', [(i, (i + k) % NX) for i in range(NX)])]
    all_to_all x1, waiting for transfers between devices: 2.71 us -> 9.25 us  [local(): part = lax.all_to_all(part, ('z', 'row'), 0, 0, tiled=True)]
    all_to_all x1, waiting for transfers between devices: 0.2 us -> 5.82 us  [local(): lax.all_to_all(home, ('y', 'core'), 0, 0, tiled=True).reshape(MEMS, 128)]
    all_to_all x0 -> x1, starting transfers between devices: none -> 4.76 us  [local(): piece = lax.all_to_all(piece, ('z', 'y'), 0, 0, tiled=True)]
    ppermute x3 -> x2, starting transfers between devices: 7.66 us -> 3.84 us  [the longest x1 1.92 us: local(): away = lax.ppermute(home_away, 'core', SWAP)]
    all_to_all x0 -> x1, waiting for transfers between devices: none -> 2.34 us  [local(): piece = lax.all_to_all(piece, ('z', 'y'), 0, 0, tiled=True)]
    unnamed x8, local copies, waits for them, and re-layouts: 1.9 us -> 0.02 us
  transfers between devices with their start and end apart: 9 -> 12, of which waited for: 5 -> 8; matrix products, arithmetic and copies ran while one was open for 0% -> 0% of each run, Pallas kernels for 5% -> 6%
where the time goes in v4:
time: 95.4 us; the launch traced here: 94.8 us
  starting transfers between devices  53.3 us (56%)
  waiting for transfers between devices  25.6 us (27%)
  Pallas kernels  14.9 us (16%)
    ppermute x6, starting transfers between devices, around(): lax.ppermute(parts[k], 'row', [(i, (i + k) % NX) for i in range(NX)])  18.1 us
    all_to_all x1, starting transfers between devices, local(): part = lax.all_to_all(part, ('z', 'row'), 0, 0, tiled=True)  11.4 us
    all_to_all x1, starting transfers between devices, local(): lax.all_to_all(home, ('y', 'core'), 0, 0, tiled=True).reshape(MEMS, 128)  10.3 us
    all_to_all x1, waiting for transfers between devices, local(): part = lax.all_to_all(part, ('z', 'row'), 0, 0, tiled=True)  9.25 us
    ppermute x6, waiting for transfers between devices, around(): lax.ppermute(parts[k], 'row', [(i, (i + k) % NX) for i in range(NX)])  7.79 us
    all_to_all x1, waiting for transfers between devices, local(): lax.all_to_all(home, ('y', 'core'), 0, 0, tiled=True).reshape(MEMS, 128)  5.82 us
    ppermute x1, starting transfers between devices, local(): other = lax.ppermute(piece, 'core', SWAP)  5.03 us
    all_to_all x1, starting transfers between devices, local(): piece = lax.all_to_all(piece, ('z', 'y'), 0, 0, tiled=True)  4.76 us
  transfers between devices with their start and end apart: 12, of which 8 were waited for; matrix products, arithmetic and copies ran while one was open for 0% of the time, Pallas kernels for 6%

profile of v4, /device:TPU:1, one launch (start us, length us, event | category | flops | bytes accessed | tf_op | source)
XLA Modules:
  0.0 94.8 jit_solution(15078681349477624561)
XLA Ops:
  0.7 2.4 %shard_map.67 = (bf16[16,128,128]{2,1,0:T(8,128)(2,1)}, bf16[8,128,128]{2,1,0:T(8,128)(2,1)}, bf16[8,128,128]{2,1,0:T(8,128)(2,1)}) custom-call(s32[1]{0:T(128)} %bitcast.3.core_ref.at_ref, bf16[128,1024]{1,0:T(8,128)(2,1)} %k_hbm.1, bf16[128,1024]{1,0:T(8,128)(2,1)} %v_hbm.1), custom_call_target="tpu_custom_call" | custom-call | bytes 1048576 | tf_op jit(solution)/shard_map/pallas_call | solution.py:293
  3.0 10.3 %all-to-all-start = ((bf16[16,128,128]{2,1,0:T(8,128)(2,1)}), bf16[16,128,128]{2,1,0:T(8,128)(2,1)S(1)}, u32[]{:S(2)}, u32[]{:S(2)}) async-start(bf16[16,128,128]{2,1,0:T(8,128)(2,1)} %get-tuple-element.31), calls=%async_computation | async-start | bytes 1048576 | tf_op jit(solution)/shard_map/all_to_all | solution.py:299
  14.0 1.9 %collective-permute-start = (bf16[96,128]{1,0:T(8,128)(2,1)S(1)}, bf16[96,128]{1,0:T(8,128)(2,1)S(1)}, u32[]{:S(2)}, u32[]{:S(2)}) collective-permute-start(bf16[96,128]{1,0:T(8,128)(2,1)S(1)} %get-tuple-element.33), channel_id=1, source_target_pairs={{0,1},{1,2},{2,3},{3,0},{4,5},{5,6},{6,7},{7,4},{8,9},{9,10},{10,1... | collective-permute-start | bytes 73736 | tf_op jit(solution)/shard_map/ppermute | solution.py:279
  16.0 4.0 %collective-permute-start.1 = (bf16[96,128]{1,0:T(8,128)(2,1)S(1)}, bf16[96,128]{1,0:T(8,128)(2,1)S(1)}, u32[]{:S(2)}, u32[]{:S(2)}) collective-permute-start(bf16[96,128]{1,0:T(8,128)(2,1)S(1)} %get-tuple-element.34), channel_id=1, source_target_pairs={{0,2},{1,3},{2,0},{3,1},{4,6},{5,7},{6,4},{7,5},{8,10},{9,11},{10,... | collective-permute-start | bytes 73736 | tf_op jit(solution)/shard_map/ppermute | solution.py:279
  19.9 3.1 %collective-permute-start.2 = (bf16[96,128]{1,0:T(8,128)(2,1)S(1)}, bf16[96,128]{1,0:T(8,128)(2,1)S(1)}, u32[]{:S(2)}, u32[]{:S(2)}) collective-permute-start(bf16[96,128]{1,0:T(8,128)(2,1)S(1)} %get-tuple-element.35), channel_id=1, source_target_pairs={{0,3},{1,0},{2,1},{3,2},{4,7},{5,4},{6,5},{7,6},{8,11},{9,8},{10,9... | collective-permute-start | bytes 73736 | tf_op jit(solution)/shard_map/ppermute | solution.py:279
  23.0 1.8 %collective-permute-done.2.q3 = bf16[96,128]{1,0:T(8,128)(2,1)S(1)} collective-permute-done((bf16[96,128]{1,0:T(8,128)(2,1)S(1)}, bf16[96,128]{1,0:T(8,128)(2,1)S(1)}, u32[]{:S(2)}, u32[]{:S(2)}) %collective-permute-start.2) | collective-permute-done | bytes 24608 | tf_op jit(solution)/shard_map/ppermute | solution.py:279
  24.8 5.8 %all-to-all-done = bf16[16,128,128]{2,1,0:T(8,128)(2,1)S(1)} async-done(((bf16[16,128,128]{2,1,0:T(8,128)(2,1)}), bf16[16,128,128]{2,1,0:T(8,128)(2,1)S(1)}, u32[]{:S(2)}, u32[]{:S(2)}) %all-to-all-start) | async-done | bytes 524320 | tf_op jit(solution)/shard_map/all_to_all | solution.py:299
  30.6 4.2 %shard_map.69 = f32[32,16,128]{2,1,0:T(8,128)} custom-call(s32[3]{0:T(128)S(1)} %pad_add_fusion.1.at_ref, bf16[2048,128]{1,0:T(8,128)(2,1)S(1)} %bitcast.5, bf16[96,128]{1,0:T(8,128)(2,1)S(1)} %get-tuple-element.32.q0, bf16[96,128]{1,0:T(8,128)(2,1)S(1)} %collective-permute-done.q1, bf16[96,128]{1,0:T(8,128)(2,1)S(1)} %collective-permute-done.1.q2, ...), custom_call_target="tpu_custom_call" | custom-call | flops 805306368 | bytes 1048576 | tf_op jit(solution)/shard_map/pallas_call | solution.py:305
  34.9 11.4 %all-to-all-start.1 = ((f32[32,16,128]{2,1,0:T(8,128)}), f32[32,16,128]{2,1,0:T(8,128)S(1)}, u32[]{:S(2)}, u32[]{:S(2)}) async-start(f32[32,16,128]{2,1,0:T(8,128)} %shard_map.69), calls=%async_computation.1 | async-start | bytes 524288 | tf_op jit(solution)/shard_map/all_to_all | solution.py:315
  46.2 1.9 %collective-permute-start.3 = (bf16[8,128,128]{2,1,0:T(8,128)(2,1)S(1)}, bf16[8,128,128]{2,1,0:T(8,128)(2,1)S(1)}, u32[]{:S(2)}, u32[]{:S(2)}) collective-permute-start(bf16[8,128,128]{2,1,0:T(8,128)(2,1)S(1)} %copy-done.3), channel_id=1, source_target_pairs={{0,4},{4,0},{1,5},{5,1},{2,6},{6,2},{3,7},{7,3},{8,12},{12,8},{9,1... | collective-permute-start | bytes 786440 | tf_op jit(solution)/shard_map/ppermute | solution.py:302
  48.2 1.3 %shard_map.70 = (bf16[8,96,128]{2,1,0:T(8,128)(2,1)S(1)}, bf16[8,96,128]{2,1,0:T(8,128)(2,1)S(1)}, bf16[8,96,128]{2,1,0:T(8,128)(2,1)S(1)}, bf16[8,96,128]{2,1,0:T(8,128)(2,1)S(1)}) custom-call(s32[3]{0:T(128)S(1)} %pad_add_fusion.1.at_ref, bf16[96,4096]{1,0:T(8,128)(2,1)S(1)} %copy-done, bf16[96,4096]{1,0:T(8,128)(2,1)S(1)} %copy-done.1), custom_call_target="tpu_custom_call" | custom-call | bytes 3145728 | tf_op jit(solution)/shard_map/pallas_call | solution.py:316
  49.7 9.3 %all-to-all-done.1.in_ref = f32[32,16,128]{2,1,0:T(8,128)S(1)} async-done(((f32[32,16,128]{2,1,0:T(8,128)}), f32[32,16,128]{2,1,0:T(8,128)S(1)}, u32[]{:S(2)}, u32[]{:S(2)}) %all-to-all-start.1) | async-done | bytes 262176 | tf_op jit(solution)/shard_map/all_to_all | solution.py:315
  58.9 2.0 %shard_map.71 = bf16[64,32,128]{2,1,0:T(8,128)(2,1)} custom-call(s32[2]{0:T(128)S(1)} %pad_add_fusion.at_ref, f32[32,16,128]{2,1,0:T(8,128)S(1)} %all-to-all-done.1.in_ref), custom_call_target="tpu_custom_call" | custom-call | bytes 1048576 | tf_op jit(solution)/shard_map/pallas_call | solution.py:318
  60.9 4.8 %all-to-all-start.2 = ((bf16[64,32,128]{2,1,0:T(8,128)(2,1)}), bf16[64,32,128]{2,1,0:T(8,128)(2,1)S(1)}, u32[]{:S(2)}, u32[]{:S(2)}) async-start(bf16[64,32,128]{2,1,0:T(8,128)(2,1)} %shard_map.71), calls=%async_computation.2 | async-start | bytes 1048576 | tf_op jit(solution)/shard_map/all_to_all | solution.py:326
  65.7 1.9 %collective-permute-start.4 = (bf16[8,96,128]{2,1,0:T(8,128)(2,1)S(1)}, bf16[8,96,128]{2,1,0:T(8,128)(2,1)S(1)}, u32[]{:S(2)}, u32[]{:S(2)}) collective-permute-start(bf16[8,96,128]{2,1,0:T(8,128)(2,1)S(1)} %get-tuple-element.43), channel_id=1, source_target_pairs={{0,1},{1,2},{2,3},{3,0},{4,5},{5,6},{6,7},{7,4},{8,9},{9,10},{10,1... | collective-permute-start | bytes 589832 | tf_op jit(solution)/shard_map/ppermute | solution.py:279
  67.6 4.1 %collective-permute-start.5 = (bf16[8,96,128]{2,1,0:T(8,128)(2,1)S(1)}, bf16[8,96,128]{2,1,0:T(8,128)(2,1)S(1)}, u32[]{:S(2)}, u32[]{:S(2)}) collective-permute-start(bf16[8,96,128]{2,1,0:T(8,128)(2,1)S(1)} %get-tuple-element.44), channel_id=1, source_target_pairs={{0,2},{1,3},{2,0},{3,1},{4,6},{5,7},{6,4},{7,5},{8,10},{9,11},{10,... | collective-permute-start | bytes 589832 | tf_op jit(solution)/shard_map/ppermute | solution.py:279
  71.7 3.1 %collective-permute-start.6 = (bf16[8,96,128]{2,1,0:T(8,128)(2,1)S(1)}, bf16[8,96,128]{2,1,0:T(8,128)(2,1)S(1)}, u32[]{:S(2)}, u32[]{:S(2)}) collective-permute-start(bf16[8,96,128]{2,1,0:T(8,128)(2,1)S(1)} %get-tuple-element.45), channel_id=1, source_target_pairs={{0,3},{1,0},{2,1},{3,2},{4,7},{5,4},{6,5},{7,6},{8,11},{9,8},{10,9... | collective-permute-start | bytes 589832 | tf_op jit(solution)/shard_map/ppermute | solution.py:279
  74.8 3.6 %collective-permute-done.5.q2 = bf16[8,96,128]{2,1,0:T(8,128)(2,1)S(1)} collective-permute-done((bf16[8,96,128]{2,1,0:T(8,128)(2,1)S(1)}, bf16[8,96,128]{2,1,0:T(8,128)(2,1)S(1)}, u32[]{:S(2)}, u32[]{:S(2)}) %collective-permute-start.5) | collective-permute-done | bytes 196640 | tf_op jit(solution)/shard_map/ppermute | solution.py:279
  78.4 2.4 %collective-permute-done.6.q3 = bf16[8,96,128]{2,1,0:T(8,128)(2,1)S(1)} collective-permute-done((bf16[8,96,128]{2,1,0:T(8,128)(2,1)S(1)}, bf16[8,96,128]{2,1,0:T(8,128)(2,1)S(1)}, u32[]{:S(2)}, u32[]{:S(2)}) %collective-permute-start.6) | collective-permute-done | bytes 196640 | tf_op jit(solution)/shard_map/ppermute | solution.py:279
  80.8 2.3 %all-to-all-done.2.told_ref.own_ref = bf16[64,32,128]{2,1,0:T(8,128)(2,1)S(1)} async-done(((bf16[64,32,128]{2,1,0:T(8,128)(2,1)}), bf16[64,32,128]{2,1,0:T(8,128)(2,1)S(1)}, u32[]{:S(2)}, u32[]{:S(2)}) %all-to-all-start.2) | async-done | bytes 524320 | tf_op jit(solution)/shard_map/all_to_all | solution.py:326
  83.2 5.0 %collective-permute-start.8 = (bf16[64,32,128]{2,1,0:T(8,128)(2,1)S(1)}, bf16[64,32,128]{2,1,0:T(8,128)(2,1)S(1)}, u32[]{:S(2)}, u32[]{:S(2)}) collective-permute-start(bf16[64,32,128]{2,1,0:T(8,128)(2,1)S(1)} %all-to-all-done.2.told_ref.own_ref), channel_id=1, source_target_pairs={{0,4},{4,0},{1,5},{5,1},{2,6},{6,2},{3,7},{7,3},{8,12},{12,8},{9,1... | collective-permute-start | bytes 1572872 | tf_op jit(solution)/shard_map/ppermute | solution.py:329
  88.2 2.1 %shard_map.72 = (bf16[8,128,128]{2,1,0:T(8,128)(2,1)S(1)}, bf16[8,128,128]{2,1,0:T(8,128)(2,1)S(1)}) custom-call(bf16[64,32,128]{2,1,0:T(8,128)(2,1)S(1)} %all-to-all-done.2.told_ref.own_ref, bf16[8,128,128]{2,1,0:T(8,128)(2,1)S(1)} %copy-done.2, bf16[8,128,128]{2,1,0:T(8,128)(2,1)S(1)} %collective-permute-done.3.away_ref, ...), custom_call_target="tpu_custom_call" | custom-call | flops 805306368 | bytes 2097152 | tf_op jit(solution)/shard_map/pallas_call | solution.py:330
  90.3 1.9 %collective-permute-start.7 = (bf16[8,128,128]{2,1,0:T(8,128)(2,1)S(1)}, bf16[8,128,128]{2,1,0:T(8,128)(2,1)S(1)}, u32[]{:S(2)}, u32[]{:S(2)}) collective-permute-start(bf16[8,128,128]{2,1,0:T(8,128)(2,1)S(1)} %get-tuple-element.53), channel_id=1, source_target_pairs={{0,4},{4,0},{1,5},{5,1},{2,6},{6,2},{3,7},{7,3},{8,12},{12,8},{9,1... | collective-permute-start | bytes 786440 | tf_op jit(solution)/shard_map/ppermute | solution.py:333
  92.2 1.3 %shard_map.73 = bf16[96,4096]{1,0:T(8,128)(2,1)} custom-call(s32[1]{0:T(128)} %bitcast.3.core_ref.at_ref, bf16[64,32,128]{2,1,0:T(8,128)(2,1)S(1)} %all-to-all-done.2.told_ref.own_ref, bf16[64,32,128]{2,1,0:T(8,128)(2,1)S(1)} %collective-permute-done.8.other_ref), custom_call_target="tpu_custom_call" | custom-call | bytes 2097152 | tf_op jit(solution)/shard_map/pallas_call | solution.py:334
  (18 shorter events, 2.2 us)
Async XLA Ops:
  0.6 12.7 %copy-start = (bf16[96,4096]{1,0:T(8,128)(2,1)S(1)}, bf16[96,4096]{1,0:T(8,128)(2,1)}, u32[]{:S(2)}) copy-start(bf16[96,4096]{1,0:T(8,128)(2,1)} %q_ref.3) | copy-start | bytes 2359300
  0.6 12.7 %copy-start.1 = (bf16[96,4096]{1,0:T(8,128)(2,1)S(1)}, bf16[96,4096]{1,0:T(8,128)(2,1)}, u32[]{:S(2)}) copy-start(bf16[96,4096]{1,0:T(8,128)(2,1)} %g_ref.3) | copy-start | bytes 2359300
  3.0 27.6 %all-to-all-start = ((bf16[16,128,128]{2,1,0:T(8,128)(2,1)}), bf16[16,128,128]{2,1,0:T(8,128)(2,1)S(1)}, u32[]{:S(2)}, u32[]{:S(2)}) async-start(bf16[16,128,128]{2,1,0:T(8,128)(2,1)} %get-tuple-element.31), calls=%async_computation | async-start | bytes 1048576 | tf_op jit(solution)/shard_map/all_to_all | solution.py:299
  14.0 9.0 %collective-permute-start = (bf16[96,128]{1,0:T(8,128)(2,1)S(1)}, bf16[96,128]{1,0:T(8,128)(2,1)S(1)}, u32[]{:S(2)}, u32[]{:S(2)}) collective-permute-start(bf16[96,128]{1,0:T(8,128)(2,1)S(1)} %get-tuple-element.33), channel_id=1, source_target_pairs={{0,1},{1,2},{2,3},{3,0},{4,5},{5,6},{6,7},{7,4},{8,9},{9,10},{10,1... | collective-permute-start | bytes 73736 | tf_op jit(solution)/shard_map/ppermute | solution.py:279
  16.0 7.1 %collective-permute-start.1 = (bf16[96,128]{1,0:T(8,128)(2,1)S(1)}, bf16[96,128]{1,0:T(8,128)(2,1)S(1)}, u32[]{:S(2)}, u32[]{:S(2)}) collective-permute-start(bf16[96,128]{1,0:T(8,128)(2,1)S(1)} %get-tuple-element.34), channel_id=1, source_target_pairs={{0,2},{1,3},{2,0},{3,1},{4,6},{5,7},{6,4},{7,5},{8,10},{9,11},{10,... | collective-permute-start | bytes 73736 | tf_op jit(solution)/shard_map/ppermute | solution.py:279
  19.9 4.9 %collective-permute-start.2 = (bf16[96,128]{1,0:T(8,128)(2,1)S(1)}, bf16[96,128]{1,0:T(8,128)(2,1)S(1)}, u32[]{:S(2)}, u32[]{:S(2)}) collective-permute-start(bf16[96,128]{1,0:T(8,128)(2,1)S(1)} %get-tuple-element.35), channel_id=1, source_target_pairs={{0,3},{1,0},{2,1},{3,2},{4,7},{5,4},{6,5},{7,6},{8,11},{9,8},{10,9... | collective-permute-start | bytes 73736 | tf_op jit(solution)/shard_map/ppermute | solution.py:279
  34.9 11.4 %copy-start.3 = (bf16[8,128,128]{2,1,0:T(8,128)(2,1)S(1)}, bf16[8,128,128]{2,1,0:T(8,128)(2,1)}, u32[]{:S(2)}) copy-start(bf16[8,128,128]{2,1,0:T(8,128)(2,1)} %get-tuple-element.36) | copy-start | bytes 786436
  34.9 24.1 %all-to-all-start.1 = ((f32[32,16,128]{2,1,0:T(8,128)}), f32[32,16,128]{2,1,0:T(8,128)S(1)}, u32[]{:S(2)}, u32[]{:S(2)}) async-start(f32[32,16,128]{2,1,0:T(8,128)} %shard_map.69), calls=%async_computation.1 | async-start | bytes 524288 | tf_op jit(solution)/shard_map/all_to_all | solution.py:315
  46.2 3.4 %collective-permute-start.3 = (bf16[8,128,128]{2,1,0:T(8,128)(2,1)S(1)}, bf16[8,128,128]{2,1,0:T(8,128)(2,1)S(1)}, u32[]{:S(2)}, u32[]{:S(2)}) collective-permute-start(bf16[8,128,128]{2,1,0:T(8,128)(2,1)S(1)} %copy-done.3), channel_id=1, source_target_pairs={{0,4},{4,0},{1,5},{5,1},{2,6},{6,2},{3,7},{7,3},{8,12},{12,8},{9,1... | collective-permute-start | bytes 786440 | tf_op jit(solution)/shard_map/ppermute | solution.py:302
  60.9 27.3 %copy-start.2 = (bf16[8,128,128]{2,1,0:T(8,128)(2,1)S(1)}, bf16[8,128,128]{2,1,0:T(8,128)(2,1)}, u32[]{:S(2)}) copy-start(bf16[8,128,128]{2,1,0:T(8,128)(2,1)} %get-tuple-element.47.own_ref) | copy-start | bytes 786436
  60.9 22.3 %all-to-all-start.2 = ((bf16[64,32,128]{2,1,0:T(8,128)(2,1)}), bf16[64,32,128]{2,1,0:T(8,128)(2,1)S(1)}, u32[]{:S(2)}, u32[]{:S(2)}) async-start(bf16[64,32,128]{2,1,0:T(8,128)(2,1)} %shard_map.71), calls=%async_computation.2 | async-start | bytes 1048576 | tf_op jit(solution)/shard_map/all_to_all | solution.py:326
  65.7 9.2 %collective-permute-start.4 = (bf16[8,96,128]{2,1,0:T(8,128)(2,1)S(1)}, bf16[8,96,128]{2,1,0:T(8,128)(2,1)S(1)}, u32[]{:S(2)}, u32[]{:S(2)}) collective-permute-start(bf16[8,96,128]{2,1,0:T(8,128)(2,1)S(1)} %get-tuple-element.43), channel_id=1, source_target_pairs={{0,1},{1,2},{2,3},{3,0},{4,5},{5,6},{6,7},{7,4},{8,9},{9,10},{10,1... | collective-permute-start | bytes 589832 | tf_op jit(solution)/shard_map/ppermute | solution.py:279
  67.6 10.8 %collective-permute-start.5 = (bf16[8,96,128]{2,1,0:T(8,128)(2,1)S(1)}, bf16[8,96,128]{2,1,0:T(8,128)(2,1)S(1)}, u32[]{:S(2)}, u32[]{:S(2)}) collective-permute-start(bf16[8,96,128]{2,1,0:T(8,128)(2,1)S(1)} %get-tuple-element.44), channel_id=1, source_target_pairs={{0,2},{1,3},{2,0},{3,1},{4,6},{5,7},{6,4},{7,5},{8,10},{9,11},{10,... | collective-permute-start | bytes 589832 | tf_op jit(solution)/shard_map/ppermute | solution.py:279
  71.7 9.1 %collective-permute-start.6 = (bf16[8,96,128]{2,1,0:T(8,128)(2,1)S(1)}, bf16[8,96,128]{2,1,0:T(8,128)(2,1)S(1)}, u32[]{:S(2)}, u32[]{:S(2)}) collective-permute-start(bf16[8,96,128]{2,1,0:T(8,128)(2,1)S(1)} %get-tuple-element.45), channel_id=1, source_target_pairs={{0,3},{1,0},{2,1},{3,2},{4,7},{5,4},{6,5},{7,6},{8,11},{9,8},{10,9... | collective-permute-start | bytes 589832 | tf_op jit(solution)/shard_map/ppermute | solution.py:279
  83.2 9.1 %collective-permute-start.8 = (bf16[64,32,128]{2,1,0:T(8,128)(2,1)S(1)}, bf16[64,32,128]{2,1,0:T(8,128)(2,1)S(1)}, u32[]{:S(2)}, u32[]{:S(2)}) collective-permute-start(bf16[64,32,128]{2,1,0:T(8,128)(2,1)S(1)} %all-to-all-done.2.told_ref.own_ref), channel_id=1, source_target_pairs={{0,4},{4,0},{1,5},{5,1},{2,6},{6,2},{3,7},{7,3},{8,12},{12,8},{9,1... | collective-permute-start | bytes 1572872 | tf_op jit(solution)/shard_map/ppermute | solution.py:329
  90.3 3.4 %collective-permute-start.7 = (bf16[8,128,128]{2,1,0:T(8,128)(2,1)S(1)}, bf16[8,128,128]{2,1,0:T(8,128)(2,1)S(1)}, u32[]{:S(2)}, u32[]{:S(2)}) collective-permute-start(bf16[8,128,128]{2,1,0:T(8,128)(2,1)S(1)} %get-tuple-element.53), channel_id=1, source_target_pairs={{0,4},{4,0},{1,5},{5,1},{2,6},{6,2},{3,7},{7,3},{8,12},{12,8},{9,1... | collective-permute-start | bytes 786440 | tf_op jit(solution)/shard_map/ppermute | solution.py:333

commit v5 on v4

--- a/solution.py
+++ b/solution.py
@@ -37,18 +37,6 @@
     )
 
 
-def fetching(body, out_shape, n_in, scratch):
-    return pl.pallas_call(
-        body,
-        out_shape=out_shape,
-        in_specs=[SMEM] + [pl.BlockSpec(memory_space=pl.ANY)] * n_in,
-        out_specs=[VMEM] * len(out_shape),
-        scratch_shapes=scratch,
-        compiler_params=pltpu.CompilerParams(vmem_limit_bytes=60 * 2**20),
-        cost_estimate=pl.CostEstimate(flops=0, bytes_accessed=2**20, transcendentals=0),
-    )
-
-
 def dot(a, b, dims):
     return lax.dot_general(a, b, dims, preferred_element_type=F32)
 
@@ -57,9 +45,7 @@
     return lax.broadcasted_iota(jnp.int32, shape, len(shape) - 1) < 64
 
 
-def pack_memory(core_ref, k_hbm, v_hbm, out_ref, own_ref, away_ref, k_ref, v_ref, sems):
-    c = core_ref[0]
-    low = low_lanes((BLOCK, 128))
+def pack_memory(k_hbm, v_hbm, out_ref, k_ref, v_ref, sems):
     copies = []
     for i in range(2):
         lanes = pl.ds(512 * i, 512)
@@ -71,14 +57,17 @@
         if t % 4 == 0:
             copies[t // 2].wait()
             copies[t // 2 + 1].wait()
-        k = k_ref[:, 128 * t : 128 * t + 128].astype(F32)
-        v = v_ref[:, 128 * t : 128 * t + 128].astype(F32)
-        first = jnp.where(low, k, pltpu.roll(v, 64, 1))
-        second = jnp.where(low, pltpu.roll(k, 64, 1), v)
-        out_ref[2 * t] = first.astype(BF16)
-        out_ref[2 * t + 1] = second.astype(BF16)
-        own_ref[t] = jnp.where(c == 0, first, second).astype(BF16)
-        away_ref[t] = jnp.where(c == 0, second, first).astype(BF16)
+        k = k_ref[:, 128 * t : 128 * t + 128]
+        v = v_ref[:, 128 * t : 128 * t + 128]
+        out_ref[2 * t] = jnp.concatenate([k[:, :64], v[:, :64]], axis=1)
+        out_ref[2 * t + 1] = jnp.concatenate([k[:, 64:], v[:, 64:]], axis=1)
+
+
+def split_heads(core_ref, in_ref, own_ref, away_ref):
+    c = core_ref[0]
+    for t in range(HEADS // 2):
+        own_ref[t] = in_ref[2 * t + c]
+        away_ref[t] = in_ref[2 * t + 1 - c]
 
 
 def pack_mine(at_ref, q_ref, g_ref, *outs):
@@ -113,35 +102,44 @@
     return jnp.where(low, qg, zero), jnp.where(low, zero, qg)
 
 
-def local_part(at_ref, kv_ref, q0, q1, q2, q3, out_ref, e_ref, gp_ref, ds_ref, p_ref):
+def local_part(at_ref, kv_ref, q0, q1, q2, q3, out_ref, s_ref, gp_ref, terms_ref):
     x = at_ref[0]
     q, g = halves(jnp.concatenate([q0[...], q1[...], q2[...], q3[...]], axis=0))
-    peak = None
-    for j in range(0, MEMS, STEP):
-        s = dot(kv_ref[j : j + STEP, :], q, NT)
-        e_ref[j : j + STEP, :] = s
-        top = jnp.max(s, axis=0, keepdims=True)
-        peak = top if peak is None else jnp.maximum(peak, top)
-    total = jnp.zeros((1, ROWS), F32)
-    weighted = jnp.zeros((1, ROWS), F32)
-    for j in range(0, MEMS, STEP):
-        e = jnp.exp(e_ref[j : j + STEP, :] - peak)
-        e_ref[j : j + STEP, :] = e
-        gp = dot(kv_ref[j : j + STEP, :], g, NT)
-        gp_ref[j : j + STEP, :] = gp
-        total += jnp.sum(e, axis=0, keepdims=True)
-        weighted += jnp.sum(e * gp, axis=0, keepdims=True)
-    lse = peak + jnp.log(total)
-    mean = weighted / total
-    inverse = 1.0 / total
-    for j in range(0, MEMS, STEP):
-        prob = e_ref[j : j + STEP, :] * inverse
-        p_ref[j : j + STEP, :] = prob.astype(BF16)
-        ds_ref[j : j + STEP, :] = (prob * (gp_ref[j : j + STEP, :] - mean)).astype(BF16)
     kv = kv_ref[...]
-    first = dot(kv, ds_ref[...], TN)[:64]
-    second = dot(kv, p_ref[...], TN)[:64]
-    both = jnp.concatenate([first, second], axis=0).T
+    for r in range(0, ROWS, 128):
+        rows = slice(r, r + 128)
+        s_ref[rows, :] = dot(q[rows], kv, NT)
+        gp_ref[rows, :] = dot(g[rows], kv, NT)
+    blocks = [slice(j, j + 128) for j in range(0, MEMS, 128)]
+    lses, means = [], []
+    for r in range(0, ROWS, 128):
+        rows = slice(r, r + 128)
+        top = s_ref[rows, blocks[0]]
+        for j in blocks[1:]:
+            top = jnp.maximum(top, s_ref[rows, j])
+        peak = jnp.max(top, axis=1, keepdims=True)
+        total = jnp.zeros((128, 128), F32)
+        weighted = jnp.zeros((128, 128), F32)
+        for j in blocks:
+            e = jnp.exp(s_ref[rows, j] - peak)
+            s_ref[rows, j] = e
+            total += e
+            weighted += e * gp_ref[rows, j]
+        total = jnp.sum(total, axis=1, keepdims=True)
+        inverse = 1.0 / total
+        mean = jnp.sum(weighted, axis=1, keepdims=True) * inverse
+        lses.append(peak + jnp.log(total))
+        means.append(mean)
+        for j in blocks:
+            prob = s_ref[rows, j] * inverse
+            terms_ref[rows, j] = (prob * (gp_ref[rows, j] - mean)).astype(BF16)
+            terms_ref[ROWS + r : ROWS + r + 128, j] = prob.astype(BF16)
+    both = dot(terms_ref[...], kv, NN)
+    both = jnp.where(low_lanes((ROWS, 128)), both[:ROWS], pltpu.roll(both[ROWS:], 64, 1))
+    first = lax.broadcasted_iota(jnp.int32, (128, 128), 1) == 0
+    turned = [jnp.where(first, a, b).T for a, b in zip(lses, means)]
+    lse = jnp.concatenate([a[0:1] for a in turned], axis=1)
+    mean = jnp.concatenate([a[1:2] for a in turned], axis=1)
     pad = jnp.zeros((1, 128 - MINE), F32)
     for r in range(NX):
         owner = lax.rem(x - r + NX, NX)
@@ -208,39 +206,76 @@
     return jnp.where(first, a, b), jnp.where(first, b, a)
 
 
-def join_query(at_ref, own_ref, other_ref, out_ref):
+def join_rows(at_ref, own_ref, other_ref, out_ref, y, z4):
     low = low_lanes((8, 128))
     top = lax.broadcasted_iota(jnp.int32, (8, 128), 0) < 4
+
+    def heads(f0, f1):
+        return jnp.where(low, f0, pltpu.roll(f1, 64, 1)), jnp.where(low, pltpu.roll(f0, 64, 1), f1)
+
+    where = [(z4 + i) * NY + y for i in range(4)]
+    pairs = [by_core(at_ref, own_ref[w].astype(F32), other_ref[w].astype(F32)) for w in where]
+    pieces = [[pairs[i][c] for i in range(4)] for c in range(NC)]
+    for p in range(2):
+        tiles = [heads(pieces[0][i][8 * p : 8 * p + 8], pieces[1][i][8 * p : 8 * p + 8]) for i in range(4)]
+        ends = []
+        for i in (0, 2):
+            g = []
+            for c in range(NC):
+                even, odd = pieces[c][i][16:24], pieces[c][i + 1][16:24]
+                if p == 0:
+                    g.append(jnp.where(top, even, pltpu.roll(odd, 4, 0)))
+                else:
+                    g.append(jnp.where(top, pltpu.roll(even, 4, 0), odd))
+            ends.append(heads(g[0], g[1]))
+        for u in range(2):
+            lanes = slice(((2 * p + u) * NY + y) * 128, ((2 * p + u) * NY + y) * 128 + 128)
+            for i in (0, 2):
+                r = 8 * (z4 + i)
+                both = jnp.concatenate([tiles[i][u], tiles[i + 1][u]], axis=0)
+                out_ref[r : r + 16, lanes] = both.astype(BF16)
+            r = 64 + 4 * z4
+            both = jnp.concatenate([ends[0][u], ends[1][u]], axis=0)
+            out_ref[r : r + 16, lanes] = both.astype(BF16)
+
+
+def sender(sems):
+    copies = []
+
+    def send(src, dst):
+        copy = pltpu.make_async_copy(src, dst, sems.at[len(copies)])
+        copy.start()
+        copies.append(copy)
+
+    return copies, send
+
+
+def join_query(at_ref, own_ref, other_ref, q_hbm, q_ref, sems):
+    copies, send = sender(sems)
+    for z4 in range(0, NZ, 4):
+        for y in range(NY):
+            join_rows(at_ref, own_ref, other_ref, q_ref, y, z4)
+        for start, size in ((8 * z4, 32), (64 + 4 * z4, 16)):
+            rows = pl.ds(start, size)
+            send(q_ref.at[rows, :], q_hbm.at[rows, :])
+    for copy in copies:
+        copy.wait()
+
+
+def join_memory(at_ref, grads_ref, sent_ref, k_hbm, v_hbm, k_ref, v_ref, sems):
+    copies, send = sender(sems)
+    low = low_lanes((BLOCK, 128))
     for y in range(NY):
-
-        def heads(f0, f1):
-            return jnp.where(low, f0, pltpu.roll(f1, 64, 1)), jnp.where(low, pltpu.roll(f0, 64, 1), f1)
-
-        for z4 in range(0, NZ, 4):
-            where = [(z4 + i) * NY + y for i in range(4)]
-            pairs = [by_core(at_ref, own_ref[w].astype(F32), other_ref[w].astype(F32)) for w in where]
-            pieces = [[pairs[i][c] for i in range(4)] for c in range(NC)]
-            for p in range(2):
-                tiles = [heads(pieces[0][i][8 * p : 8 * p + 8], pieces[1][i][8 * p : 8 * p + 8]) for i in range(4)]
-                ends = []
-                for i in (0, 2):
-                    g = []
-                    for c in range(NC):
-                        even, odd = pieces[c][i][16:24], pieces[c][i + 1][16:24]
-                        if p == 0:
-                            g.append(jnp.where(top, even, pltpu.roll(odd, 4, 0)))
-                        else:
-                            g.append(jnp.where(top, pltpu.roll(even, 4, 0), odd))
-                    ends.append(heads(g[0], g[1]))
-                for u in range(2):
-                    lanes = slice(((2 * p + u) * NY + y) * 128, ((2 * p + u) * NY + y) * 128 + 128)
-                    for i in (0, 2):
-                        r = 8 * (z4 + i)
-                        both = jnp.concatenate([tiles[i][u], tiles[i + 1][u]], axis=0)
-                        out_ref[r : r + 16, lanes] = both.astype(BF16)
-                    r = 64 + 4 * z4
-                    both = jnp.concatenate([ends[0][u], ends[1][u]], axis=0)
-                    out_ref[r : r + 16, lanes] = both.astype(BF16)
+        a, b = by_core(at_ref, grads_ref[y].astype(F32), sent_ref[y].astype(F32))
+        lanes = slice(128 * y, 128 * y + 128)
+        k_ref[:, lanes] = jnp.where(low, a, pltpu.roll(b, 64, 1)).astype(BF16)
+        v_ref[:, lanes] = jnp.where(low, pltpu.roll(a, 64, 1), b).astype(BF16)
+        if y % 2 == 1:
+            part = pl.ds(128 * (y - 1), 256)
+            send(k_ref.at[:, part], k_hbm.at[:, part])
+            send(v_ref.at[:, part], v_hbm.at[:, part])
+    for copy in copies:
+        copy.wait()
 
 
 def head_grads(told_ref, y, kv, qs):
@@ -265,15 +300,6 @@
         sent_ref[y] = out[BLOCK:]
 
 
-def join_memory(core_ref, own_ref, other_ref, k_ref, v_ref):
-    low = low_lanes((BLOCK, 128))
-    for y in range(NY):
-        a, b = by_core(core_ref, own_ref[y].astype(F32), other_ref[y].astype(F32))
-        lanes = slice(128 * y, 128 * y + 128)
-        k_ref[:, lanes] = jnp.where(low, a, pltpu.roll(b, 64, 1)).astype(BF16)
-        v_ref[:, lanes] = jnp.where(low, pltpu.roll(a, 64, 1), b).astype(BF16)
-
-
 def around(parts):
     return parts[:1] + [
         lax.ppermute(parts[k], "row", [(i, (i + k) % NX) for i in range(NX)]) for k in range(1, NX)
@@ -290,15 +316,19 @@
     mega = 2**20
 
     half = shape((NY, BLOCK, 128), BF16)
-    home, home_own, home_away = fetching(
+    home = pl.pallas_call(
         pack_memory,
-        [shape((HEADS, BLOCK, 128), BF16), half, half],
-        2,
-        [pltpu.VMEM((BLOCK, 1024), BF16)] * 2 + [pltpu.SemaphoreType.DMA((2, 2))],
-    )(corez, keys, values)
+        out_shape=shape((HEADS, BLOCK, 128), BF16),
+        in_specs=[pl.BlockSpec(memory_space=pl.ANY)] * 2,
+        out_specs=VMEM,
+        scratch_shapes=[pltpu.VMEM((BLOCK, 1024), BF16)] * 2 + [pltpu.SemaphoreType.DMA((2, 2))],
+        compiler_params=pltpu.CompilerParams(vmem_limit_bytes=60 * 2**20),
+        cost_estimate=pl.CostEstimate(flops=0, bytes_accessed=mega, transcendentals=0),
+    )(keys, values)
     memory = lax.all_to_all(home, ("y", "core"), 0, 0, tiled=True).reshape(MEMS, 128)
     mine = call(pack_mine, [shape((MINE, 128), BF16)] * NX, 2, smem=1, moved=mega)(at, query, out_grad)
     mine = around(list(mine))
+    home_own, home_away = call(split_heads, [half, half], 1, smem=1, moved=mega)(corez, home)
     away = lax.ppermute(home_away, "core", SWAP)
 
     work = 2 * MEMS * ROWS * 128
@@ -307,7 +337,7 @@
         shape((NZ * NX, 16, 128), F32),
         5,
         smem=1,
-        scratch=[pltpu.VMEM((MEMS, ROWS), F32)] * 2 + [pltpu.VMEM((MEMS, ROWS), BF16)] * 2,
+        scratch=[pltpu.VMEM((ROWS, MEMS), F32)] * 2 + [pltpu.VMEM((2 * ROWS, MEMS), BF16)],
         flops=4 * work,
         moved=mega,
         exps=MEMS * ROWS,
@@ -331,11 +361,20 @@
         piece, home_own, away, *heads
     )
     sent = lax.ppermute(sent, "core", SWAP)
-    query_grad = call(join_query, shape((MINE, 4096), BF16), 2, smem=1, moved=2 * mega)(corez, piece, other)
+    def joined(body, results, count):
+        return pl.pallas_call(
+            body,
+            out_shape=results,
+            in_specs=[SMEM] + [VMEM] * 2,
+            out_specs=[pl.BlockSpec(memory_space=pl.ANY)] * len(results),
+            scratch_shapes=[pltpu.VMEM(a.shape, a.dtype) for a in results] + [pltpu.SemaphoreType.DMA((count,))],
+            compiler_params=pltpu.CompilerParams(vmem_limit_bytes=24 * 2**20),
+            cost_estimate=pl.CostEstimate(flops=0, bytes_accessed=2 * mega, transcendentals=0),
+        )
+
+    (query_grad,) = joined(join_query, [shape((MINE, 4096), BF16)], 4)(corez, piece, other)
     sent, query_grad = lax.optimization_barrier((sent, query_grad))
-    key_grad, value_grad = call(join_memory, [shape((BLOCK, 1024), BF16)] * 2, 2, smem=1, moved=mega)(
-        corez, grads, sent
-    )
+    key_grad, value_grad = joined(join_memory, [shape((BLOCK, 1024), BF16)] * 2, 8)(corez, grads, sent)
     return (query_grad, key_grad, value_grad)
 
 

time: 95.4 us -> 94.8 us (level)
  local copies, waits for them, and re-layouts: 0.02 us -> 1.37 us
  waiting for transfers between devices: 25.6 us -> 24.3 us
    unnamed x8 -> x14, local copies, waits for them, and re-layouts: 0.02 us -> 1.37 us
    all_to_all x1, waiting for transfers between devices: 9.25 us -> 7.99 us  [local(): part = lax.all_to_all(part, ('z', 'row'), 0, 0, tiled=True)]
    pallas_call x3 -> x4, Pallas kernels: 4.66 us -> 4.31 us  [the longest x1 2.14 us: local(): pl.pallas_call(pack_memory, out_shape=shape((HEADS, BLOCK, 128), BF16), i...]
  transfers between devices with their start and end apart: 12 -> 12, of which waited for: 8 -> 7; matrix products, arithmetic and copies ran while one was open for 0% -> 0% of each run, Pallas kernels for 6% -> 6%
where the time goes in v5:
time: 94.8 us; the launch traced here: 94.2 us
  starting transfers between devices  53.4 us (56%)
  waiting for transfers between devices  24.3 us (26%)
  Pallas kernels  14.1 us (15%)
  local copies, waits for them, and re-layouts  1.37 us (1%)
    ppermute x6, starting transfers between devices, around(): lax.ppermute(parts[k], 'row', [(i, (i + k) % NX) for i in range(NX)])  18.1 us
    all_to_all x1, starting transfers between devices, local(): part = lax.all_to_all(part, ('z', 'row'), 0, 0, tiled=True)  11.4 us
    all_to_all x1, starting transfers between devices, local(): lax.all_to_all(home, ('y', 'core'), 0, 0, tiled=True).reshape(MEMS, 128)  10.4 us
    all_to_all x1, waiting for transfers between devices, local(): part = lax.all_to_all(part, ('z', 'row'), 0, 0, tiled=True)  7.99 us
    ppermute x6, waiting for transfers between devices, around(): lax.ppermute(parts[k], 'row', [(i, (i + k) % NX) for i in range(NX)])  7.81 us
    all_to_all x1, waiting for transfers between devices, local(): lax.all_to_all(home, ('y', 'core'), 0, 0, tiled=True).reshape(MEMS, 128)  5.82 us
    ppermute x1, starting transfers between devices, local(): other = lax.ppermute(piece, 'core', SWAP)  4.98 us
    all_to_all x1, starting transfers between devices, local(): piece = lax.all_to_all(piece, ('z', 'y'), 0, 0, tiled=True)  4.77 us
  transfers between devices with their start and end apart: 12, of which 7 were waited for; matrix products, arithmetic and copies ran while one was open for 0% of the time, Pallas kernels for 6%

profile of v5, /device:TPU:1, one launch (start us, length us, event | category | flops | bytes accessed | tf_op | source)
XLA Modules:
  0.0 94.2 jit_solution(10683407844422857517)
XLA Ops:
  0.6 2.1 %shard_map.67.in_ref = bf16[16,128,128]{2,1,0:T(8,128)(2,1)} custom-call(bf16[128,1024]{1,0:T(8,128)(2,1)} %k_hbm.1, bf16[128,1024]{1,0:T(8,128)(2,1)} %v_hbm.1), custom_call_target="tpu_custom_call" | custom-call | bytes 1048576 | tf_op jit(solution)/shard_map/pallas_call | solution.py:319
  2.8 10.4 %all-to-all-start = ((bf16[16,128,128]{2,1,0:T(8,128)(2,1)}), bf16[16,128,128]{2,1,0:T(8,128)(2,1)S(1)}, u32[]{:S(2)}, u32[]{:S(2)}) async-start(bf16[16,128,128]{2,1,0:T(8,128)(2,1)} %shard_map.67.in_ref), calls=%async_computation | async-start | bytes 1048576 | tf_op jit(solution)/shard_map/all_to_all | solution.py:328
  13.9 1.9 %collective-permute-start = (bf16[96,128]{1,0:T(8,128)(2,1)S(1)}, bf16[96,128]{1,0:T(8,128)(2,1)S(1)}, u32[]{:S(2)}, u32[]{:S(2)}) collective-permute-start(bf16[96,128]{1,0:T(8,128)(2,1)S(1)} %get-tuple-element.31), channel_id=1, source_target_pairs={{0,1},{1,2},{2,3},{3,0},{4,5},{5,6},{6,7},{7,4},{8,9},{9,10},{10,1... | collective-permute-start | bytes 73736 | tf_op jit(solution)/shard_map/ppermute | solution.py:305
  15.9 4.0 %collective-permute-start.1 = (bf16[96,128]{1,0:T(8,128)(2,1)S(1)}, bf16[96,128]{1,0:T(8,128)(2,1)S(1)}, u32[]{:S(2)}, u32[]{:S(2)}) collective-permute-start(bf16[96,128]{1,0:T(8,128)(2,1)S(1)} %get-tuple-element.32), channel_id=1, source_target_pairs={{0,2},{1,3},{2,0},{3,1},{4,6},{5,7},{6,4},{7,5},{8,10},{9,11},{10,... | collective-permute-start | bytes 73736 | tf_op jit(solution)/shard_map/ppermute | solution.py:305
  19.8 3.1 %collective-permute-start.2 = (bf16[96,128]{1,0:T(8,128)(2,1)S(1)}, bf16[96,128]{1,0:T(8,128)(2,1)S(1)}, u32[]{:S(2)}, u32[]{:S(2)}) collective-permute-start(bf16[96,128]{1,0:T(8,128)(2,1)S(1)} %get-tuple-element.33), channel_id=1, source_target_pairs={{0,3},{1,0},{2,1},{3,2},{4,7},{5,4},{6,5},{7,6},{8,11},{9,8},{10,9... | collective-permute-start | bytes 73736 | tf_op jit(solution)/shard_map/ppermute | solution.py:305
  22.9 1.8 %collective-permute-done.2.q3 = bf16[96,128]{1,0:T(8,128)(2,1)S(1)} collective-permute-done((bf16[96,128]{1,0:T(8,128)(2,1)S(1)}, bf16[96,128]{1,0:T(8,128)(2,1)S(1)}, u32[]{:S(2)}, u32[]{:S(2)}) %collective-permute-start.2) | collective-permute-done | bytes 24608 | tf_op jit(solution)/shard_map/ppermute | solution.py:305
  24.7 5.8 %all-to-all-done = bf16[16,128,128]{2,1,0:T(8,128)(2,1)S(1)} async-done(((bf16[16,128,128]{2,1,0:T(8,128)(2,1)}), bf16[16,128,128]{2,1,0:T(8,128)(2,1)S(1)}, u32[]{:S(2)}, u32[]{:S(2)}) %all-to-all-start) | async-done | bytes 524320 | tf_op jit(solution)/shard_map/all_to_all | solution.py:328
  30.5 3.8 %shard_map.69 = f32[32,16,128]{2,1,0:T(8,128)} custom-call(s32[3]{0:T(128)S(1)} %pad_add_fusion.1.at_ref, bf16[2048,128]{1,0:T(8,128)(2,1)S(1)} %bitcast.5, bf16[96,128]{1,0:T(8,128)(2,1)S(1)} %get-tuple-element.30.q0, bf16[96,128]{1,0:T(8,128)(2,1)S(1)} %collective-permute-done.q1, bf16[96,128]{1,0:T(8,128)(2,1)S(1)} %collective-permute-done.1.q2, ...), custom_call_target="tpu_custom_call" | custom-call | flops 805306368 | bytes 1048576 | tf_op jit(solution)/shard_map/pallas_call | solution.py:335
  34.3 11.4 %all-to-all-start.1 = ((f32[32,16,128]{2,1,0:T(8,128)}), f32[32,16,128]{2,1,0:T(8,128)S(1)}, u32[]{:S(2)}, u32[]{:S(2)}) async-start(f32[32,16,128]{2,1,0:T(8,128)} %shard_map.69), calls=%async_computation.1 | async-start | bytes 524288 | tf_op jit(solution)/shard_map/all_to_all | solution.py:345
  45.8 1.9 %collective-permute-start.3 = (bf16[8,128,128]{2,1,0:T(8,128)(2,1)S(1)}, bf16[8,128,128]{2,1,0:T(8,128)(2,1)S(1)}, u32[]{:S(2)}, u32[]{:S(2)}) collective-permute-start(bf16[8,128,128]{2,1,0:T(8,128)(2,1)S(1)} %get-tuple-element.34), channel_id=1, source_target_pairs={{0,4},{4,0},{1,5},{5,1},{2,6},{6,2},{3,7},{7,3},{8,12},{12,8},{9,1... | collective-permute-start | bytes 786440 | tf_op jit(solution)/shard_map/ppermute | solution.py:332
  47.7 1.3 %shard_map.71 = (bf16[8,96,128]{2,1,0:T(8,128)(2,1)S(1)}, bf16[8,96,128]{2,1,0:T(8,128)(2,1)S(1)}, bf16[8,96,128]{2,1,0:T(8,128)(2,1)S(1)}, bf16[8,96,128]{2,1,0:T(8,128)(2,1)S(1)}) custom-call(s32[3]{0:T(128)S(1)} %pad_add_fusion.1.at_ref, bf16[96,4096]{1,0:T(8,128)(2,1)S(1)} %copy-done.1, bf16[96,4096]{1,0:T(8,128)(2,1)S(1)} %copy-done.2), custom_call_target="tpu_custom_call" | custom-call | bytes 3145728 | tf_op jit(solution)/shard_map/pallas_call | solution.py:346
  50.4 8.0 %all-to-all-done.1.in_ref = f32[32,16,128]{2,1,0:T(8,128)S(1)} async-done(((f32[32,16,128]{2,1,0:T(8,128)}), f32[32,16,128]{2,1,0:T(8,128)S(1)}, u32[]{:S(2)}, u32[]{:S(2)}) %all-to-all-start.1) | async-done | bytes 262176 | tf_op jit(solution)/shard_map/all_to_all | solution.py:345
  58.4 2.0 %shard_map.72 = bf16[64,32,128]{2,1,0:T(8,128)(2,1)} custom-call(s32[2]{0:T(128)S(1)} %pad_add_fusion.at_ref, f32[32,16,128]{2,1,0:T(8,128)S(1)} %all-to-all-done.1.in_ref), custom_call_target="tpu_custom_call" | custom-call | bytes 1048576 | tf_op jit(solution)/shard_map/pallas_call | solution.py:348
  60.4 4.8 %all-to-all-start.2 = ((bf16[64,32,128]{2,1,0:T(8,128)(2,1)}), bf16[64,32,128]{2,1,0:T(8,128)(2,1)S(1)}, u32[]{:S(2)}, u32[]{:S(2)}) async-start(bf16[64,32,128]{2,1,0:T(8,128)(2,1)} %shard_map.72), calls=%async_computation.2 | async-start | bytes 1048576 | tf_op jit(solution)/shard_map/all_to_all | solution.py:356
  65.2 1.9 %collective-permute-start.4 = (bf16[8,96,128]{2,1,0:T(8,128)(2,1)S(1)}, bf16[8,96,128]{2,1,0:T(8,128)(2,1)S(1)}, u32[]{:S(2)}, u32[]{:S(2)}) collective-permute-start(bf16[8,96,128]{2,1,0:T(8,128)(2,1)S(1)} %copy-done.6), channel_id=1, source_target_pairs={{0,1},{1,2},{2,3},{3,0},{4,5},{5,6},{6,7},{7,4},{8,9},{9,10},{10,1... | collective-permute-start | bytes 589832 | tf_op jit(solution)/shard_map/ppermute | solution.py:305
  67.1 4.1 %collective-permute-start.5 = (bf16[8,96,128]{2,1,0:T(8,128)(2,1)S(1)}, bf16[8,96,128]{2,1,0:T(8,128)(2,1)S(1)}, u32[]{:S(2)}, u32[]{:S(2)}) collective-permute-start(bf16[8,96,128]{2,1,0:T(8,128)(2,1)S(1)} %copy-done.4), channel_id=1, source_target_pairs={{0,2},{1,3},{2,0},{3,1},{4,6},{5,7},{6,4},{7,5},{8,10},{9,11},{10,... | collective-permute-start | bytes 589832 | tf_op jit(solution)/shard_map/ppermute | solution.py:305
  71.2 3.1 %collective-permute-start.6 = (bf16[8,96,128]{2,1,0:T(8,128)(2,1)S(1)}, bf16[8,96,128]{2,1,0:T(8,128)(2,1)S(1)}, u32[]{:S(2)}, u32[]{:S(2)}) collective-permute-start(bf16[8,96,128]{2,1,0:T(8,128)(2,1)S(1)} %get-tuple-element.43), channel_id=1, source_target_pairs={{0,3},{1,0},{2,1},{3,2},{4,7},{5,4},{6,5},{7,6},{8,11},{9,8},{10,9... | collective-permute-start | bytes 589832 | tf_op jit(solution)/shard_map/ppermute | solution.py:305
  74.3 3.6 %collective-permute-done.5.q2 = bf16[8,96,128]{2,1,0:T(8,128)(2,1)S(1)} collective-permute-done((bf16[8,96,128]{2,1,0:T(8,128)(2,1)S(1)}, bf16[8,96,128]{2,1,0:T(8,128)(2,1)S(1)}, u32[]{:S(2)}, u32[]{:S(2)}) %collective-permute-start.5) | collective-permute-done | bytes 196640 | tf_op jit(solution)/shard_map/ppermute | solution.py:305
  77.9 2.5 %collective-permute-done.6.q3 = bf16[8,96,128]{2,1,0:T(8,128)(2,1)S(1)} collective-permute-done((bf16[8,96,128]{2,1,0:T(8,128)(2,1)S(1)}, bf16[8,96,128]{2,1,0:T(8,128)(2,1)S(1)}, u32[]{:S(2)}, u32[]{:S(2)}) %collective-permute-start.6) | collective-permute-done | bytes 196640 | tf_op jit(solution)/shard_map/ppermute | solution.py:305
  80.4 2.3 %all-to-all-done.2.told_ref.own_ref = bf16[64,32,128]{2,1,0:T(8,128)(2,1)S(1)} async-done(((bf16[64,32,128]{2,1,0:T(8,128)(2,1)}), bf16[64,32,128]{2,1,0:T(8,128)(2,1)S(1)}, u32[]{:S(2)}, u32[]{:S(2)}) %all-to-all-start.2) | async-done | bytes 524320 | tf_op jit(solution)/shard_map/all_to_all | solution.py:356
  82.7 5.0 %collective-permute-start.8 = (bf16[64,32,128]{2,1,0:T(8,128)(2,1)S(1)}, bf16[64,32,128]{2,1,0:T(8,128)(2,1)S(1)}, u32[]{:S(2)}, u32[]{:S(2)}) collective-permute-start(bf16[64,32,128]{2,1,0:T(8,128)(2,1)S(1)} %all-to-all-done.2.told_ref.own_ref), channel_id=1, source_target_pairs={{0,4},{4,0},{1,5},{5,1},{2,6},{6,2},{3,7},{7,3},{8,12},{12,8},{9,1... | collective-permute-start | bytes 1572872 | tf_op jit(solution)/shard_map/ppermute | solution.py:359
  87.7 2.1 %shard_map.73 = (bf16[8,128,128]{2,1,0:T(8,128)(2,1)S(1)}, bf16[8,128,128]{2,1,0:T(8,128)(2,1)S(1)}) custom-call(bf16[64,32,128]{2,1,0:T(8,128)(2,1)S(1)} %all-to-all-done.2.told_ref.own_ref, bf16[8,128,128]{2,1,0:T(8,128)(2,1)S(1)} %get-tuple-element.45.own_ref, bf16[8,128,128]{2,1,0:T(8,128)(2,1)S(1)} %collective-permute-done.3.away_ref, ...), custom_call_target="tpu_custom_call" | custom-call | flops 805306368 | bytes 2097152 | tf_op jit(solution)/shard_map/pallas_call | solution.py:360
  89.8 1.9 %collective-permute-start.7 = (bf16[8,128,128]{2,1,0:T(8,128)(2,1)S(1)}, bf16[8,128,128]{2,1,0:T(8,128)(2,1)S(1)}, u32[]{:S(2)}, u32[]{:S(2)}) collective-permute-start(bf16[8,128,128]{2,1,0:T(8,128)(2,1)S(1)} %get-tuple-element.51), channel_id=1, source_target_pairs={{0,4},{4,0},{1,5},{5,1},{2,6},{6,2},{3,7},{7,3},{8,12},{12,8},{9,1... | collective-permute-start | bytes 786440 | tf_op jit(solution)/shard_map/ppermute | solution.py:363
  91.7 1.2 %shard_map.74 = bf16[96,4096]{1,0:T(8,128)(2,1)} custom-call(s32[1]{0:T(128)} %bitcast.3.core_ref.at_ref, bf16[64,32,128]{2,1,0:T(8,128)(2,1)S(1)} %all-to-all-done.2.told_ref.own_ref, bf16[64,32,128]{2,1,0:T(8,128)(2,1)S(1)} %collective-permute-done.8.other_ref), custom_call_target="tpu_custom_call" | custom-call | bytes 2097152 | tf_op jit(solution)/shard_map/pallas_call | solution.py:375
  (25 shorter events, 3.5 us)
Async XLA Ops:
  0.6 12.6 %copy-start.2 = (bf16[96,4096]{1,0:T(8,128)(2,1)S(1)}, bf16[96,4096]{1,0:T(8,128)(2,1)}, u32[]{:S(2)}) copy-start(bf16[96,4096]{1,0:T(8,128)(2,1)} %g_ref.3) | copy-start | bytes 2359300
  2.8 10.5 %copy-start.1 = (bf16[96,4096]{1,0:T(8,128)(2,1)S(1)}, bf16[96,4096]{1,0:T(8,128)(2,1)}, u32[]{:S(2)}) copy-start(bf16[96,4096]{1,0:T(8,128)(2,1)} %q_ref.3) | copy-start | bytes 2359300
  2.8 27.7 %all-to-all-start = ((bf16[16,128,128]{2,1,0:T(8,128)(2,1)}), bf16[16,128,128]{2,1,0:T(8,128)(2,1)S(1)}, u32[]{:S(2)}, u32[]{:S(2)}) async-start(bf16[16,128,128]{2,1,0:T(8,128)(2,1)} %shard_map.67.in_ref), calls=%async_computation | async-start | bytes 1048576 | tf_op jit(solution)/shard_map/all_to_all | solution.py:328
  13.9 9.0 %collective-permute-start = (bf16[96,128]{1,0:T(8,128)(2,1)S(1)}, bf16[96,128]{1,0:T(8,128)(2,1)S(1)}, u32[]{:S(2)}, u32[]{:S(2)}) collective-permute-start(bf16[96,128]{1,0:T(8,128)(2,1)S(1)} %get-tuple-element.31), channel_id=1, source_target_pairs={{0,1},{1,2},{2,3},{3,0},{4,5},{5,6},{6,7},{7,4},{8,9},{9,10},{10,1... | collective-permute-start | bytes 73736 | tf_op jit(solution)/shard_map/ppermute | solution.py:305
  15.9 7.1 %collective-permute-start.1 = (bf16[96,128]{1,0:T(8,128)(2,1)S(1)}, bf16[96,128]{1,0:T(8,128)(2,1)S(1)}, u32[]{:S(2)}, u32[]{:S(2)}) collective-permute-start(bf16[96,128]{1,0:T(8,128)(2,1)S(1)} %get-tuple-element.32), channel_id=1, source_target_pairs={{0,2},{1,3},{2,0},{3,1},{4,6},{5,7},{6,4},{7,5},{8,10},{9,11},{10,... | collective-permute-start | bytes 73736 | tf_op jit(solution)/shard_map/ppermute | solution.py:305
  19.8 4.9 %collective-permute-start.2 = (bf16[96,128]{1,0:T(8,128)(2,1)S(1)}, bf16[96,128]{1,0:T(8,128)(2,1)S(1)}, u32[]{:S(2)}, u32[]{:S(2)}) collective-permute-start(bf16[96,128]{1,0:T(8,128)(2,1)S(1)} %get-tuple-element.33), channel_id=1, source_target_pairs={{0,3},{1,0},{2,1},{3,2},{4,7},{5,4},{6,5},{7,6},{8,11},{9,8},{10,9... | collective-permute-start | bytes 73736 | tf_op jit(solution)/shard_map/ppermute | solution.py:305
  34.3 11.4 %copy-start = (bf16[16,128,128]{2,1,0:T(8,128)(2,1)S(1)}, bf16[16,128,128]{2,1,0:T(8,128)(2,1)}, u32[]{:S(2)}) copy-start(bf16[16,128,128]{2,1,0:T(8,128)(2,1)} %shard_map.67.in_ref) | copy-start | bytes 1572868
  34.3 24.1 %all-to-all-start.1 = ((f32[32,16,128]{2,1,0:T(8,128)}), f32[32,16,128]{2,1,0:T(8,128)S(1)}, u32[]{:S(2)}, u32[]{:S(2)}) async-start(f32[32,16,128]{2,1,0:T(8,128)} %shard_map.69), calls=%async_computation.1 | async-start | bytes 524288 | tf_op jit(solution)/shard_map/all_to_all | solution.py:345
  45.8 4.7 %collective-permute-start.3 = (bf16[8,128,128]{2,1,0:T(8,128)(2,1)S(1)}, bf16[8,128,128]{2,1,0:T(8,128)(2,1)S(1)}, u32[]{:S(2)}, u32[]{:S(2)}) collective-permute-start(bf16[8,128,128]{2,1,0:T(8,128)(2,1)S(1)} %get-tuple-element.34), channel_id=1, source_target_pairs={{0,4},{4,0},{1,5},{5,1},{2,6},{6,2},{3,7},{7,3},{8,12},{12,8},{9,1... | collective-permute-start | bytes 786440 | tf_op jit(solution)/shard_map/ppermute | solution.py:332
  49.0 0.7 copy-start.3
  49.7 0.7 copy-start.5
  60.4 4.8 %copy-start.6 = (bf16[8,96,128]{2,1,0:T(8,128)(2,1)S(1)}, bf16[8,96,128]{2,1,0:T(8,128)(2,1)}, u32[]{:S(2)}) copy-start(bf16[8,96,128]{2,1,0:T(8,128)(2,1)} %copy-done.5) | copy-start | bytes 589828
  60.4 6.7 %copy-start.4 = (bf16[8,96,128]{2,1,0:T(8,128)(2,1)S(1)}, bf16[8,96,128]{2,1,0:T(8,128)(2,1)}, u32[]{:S(2)}) copy-start(bf16[8,96,128]{2,1,0:T(8,128)(2,1)} %copy-done.3) | copy-start | bytes 589828
  60.4 22.3 %all-to-all-start.2 = ((bf16[64,32,128]{2,1,0:T(8,128)(2,1)}), bf16[64,32,128]{2,1,0:T(8,128)(2,1)S(1)}, u32[]{:S(2)}, u32[]{:S(2)}) async-start(bf16[64,32,128]{2,1,0:T(8,128)(2,1)} %shard_map.72), calls=%async_computation.2 | async-start | bytes 1048576 | tf_op jit(solution)/shard_map/all_to_all | solution.py:356
  65.2 9.2 %collective-permute-start.4 = (bf16[8,96,128]{2,1,0:T(8,128)(2,1)S(1)}, bf16[8,96,128]{2,1,0:T(8,128)(2,1)S(1)}, u32[]{:S(2)}, u32[]{:S(2)}) collective-permute-start(bf16[8,96,128]{2,1,0:T(8,128)(2,1)S(1)} %copy-done.6), channel_id=1, source_target_pairs={{0,1},{1,2},{2,3},{3,0},{4,5},{5,6},{6,7},{7,4},{8,9},{9,10},{10,1... | collective-permute-start | bytes 589832 | tf_op jit(solution)/shard_map/ppermute | solution.py:305
  67.1 10.8 %collective-permute-start.5 = (bf16[8,96,128]{2,1,0:T(8,128)(2,1)S(1)}, bf16[8,96,128]{2,1,0:T(8,128)(2,1)S(1)}, u32[]{:S(2)}, u32[]{:S(2)}) collective-permute-start(bf16[8,96,128]{2,1,0:T(8,128)(2,1)S(1)} %copy-done.4), channel_id=1, source_target_pairs={{0,2},{1,3},{2,0},{3,1},{4,6},{5,7},{6,4},{7,5},{8,10},{9,11},{10,... | collective-permute-start | bytes 589832 | tf_op jit(solution)/shard_map/ppermute | solution.py:305
  71.2 9.1 %collective-permute-start.6 = (bf16[8,96,128]{2,1,0:T(8,128)(2,1)S(1)}, bf16[8,96,128]{2,1,0:T(8,128)(2,1)S(1)}, u32[]{:S(2)}, u32[]{:S(2)}) collective-permute-start(bf16[8,96,128]{2,1,0:T(8,128)(2,1)S(1)} %get-tuple-element.43), channel_id=1, source_target_pairs={{0,3},{1,0},{2,1},{3,2},{4,7},{5,4},{6,5},{7,6},{8,11},{9,8},{10,9... | collective-permute-start | bytes 589832 | tf_op jit(solution)/shard_map/ppermute | solution.py:305
  82.7 9.0 %collective-permute-start.8 = (bf16[64,32,128]{2,1,0:T(8,128)(2,1)S(1)}, bf16[64,32,128]{2,1,0:T(8,128)(2,1)S(1)}, u32[]{:S(2)}, u32[]{:S(2)}) collective-permute-start(bf16[64,32,128]{2,1,0:T(8,128)(2,1)S(1)} %all-to-all-done.2.told_ref.own_ref), channel_id=1, source_target_pairs={{0,4},{4,0},{1,5},{5,1},{2,6},{6,2},{3,7},{7,3},{8,12},{12,8},{9,1... | collective-permute-start | bytes 1572872 | tf_op jit(solution)/shard_map/ppermute | solution.py:359
  89.8 3.4 %collective-permute-start.7 = (bf16[8,128,128]{2,1,0:T(8,128)(2,1)S(1)}, bf16[8,128,128]{2,1,0:T(8,128)(2,1)S(1)}, u32[]{:S(2)}, u32[]{:S(2)}) collective-permute-start(bf16[8,128,128]{2,1,0:T(8,128)(2,1)S(1)} %get-tuple-element.51), channel_id=1, source_target_pairs={{0,4},{4,0},{1,5},{5,1},{2,6},{6,2},{3,7},{7,3},{8,12},{12,8},{9,1... | collective-permute-start | bytes 786440 | tf_op jit(solution)/shard_map/ppermute | solution.py:363

commit v6 on v5

--- a/solution.py
+++ b/solution.py
@@ -148,9 +148,9 @@
             t = 128 * min(z, 2)
             a = MINE * r + 8 * z
             b = MINE * r + 64 + 4 * z
-            out_ref[z * NX + owner, 0:8, :] = both[a : a + 8, :]
+            out_ref[owner * NZ + z, 0:8, :] = both[a : a + 8, :]
             rows = [both[b : b + 4, :], lse[:, t : t + 128], mean[:, t : t + 128]] + own
-            out_ref[z * NX + owner, 8:16, :] = jnp.concatenate(rows, axis=0)
+            out_ref[owner * NZ + z, 8:16, :] = jnp.concatenate(rows, axis=0)
 
 
 def weights(logs, means):
@@ -175,8 +175,8 @@
     top = lax.broadcasted_iota(jnp.int32, (8, 128), 0) < 4
     full, half = [], []
     for u in range(NX):
-        logs = jnp.concatenate([in_ref[d * NX + u, 14:15, :] for d in range(NZ)], axis=0)
-        means = jnp.concatenate([in_ref[d * NX + u, 15:16, :] for d in range(NZ)], axis=0)
+        logs = jnp.concatenate([in_ref[u * NZ + d, 14:15, :] for d in range(NZ)], axis=0)
+        means = jnp.concatenate([in_ref[u * NZ + d, 15:16, :] for d in range(NZ)], axis=0)
         _, offset, w = weights(logs, means)
         shift = w * (means - offset)
         col_ref[u] = jnp.concatenate([w, shift, jnp.zeros((112, 128), F32)], axis=0).T
@@ -186,15 +186,15 @@
         a = jnp.zeros((8, 128), F32)
         b = jnp.zeros((8, 128), F32)
         for d in range(NZ):
-            tile = in_ref[d * NX + u]
+            tile = in_ref[u * NZ + d]
             a += tile[0:8] * jnp.where(low, cols[:, d : d + 1], cols[:, 8 + d : 9 + d])
             b += tile[8:16] * jnp.where(low, ends[:, d : d + 1], ends[:, 8 + d : 9 + d])
         full.append(a + pltpu.roll(a, 64, 1))
         half.append(b + pltpu.roll(b, 64, 1))
     f = [jnp.where(low, full[2 * p], full[2 * p + 1]) for p in range(2)]
     h = [jnp.where(low, half[2 * p], half[2 * p + 1]) for p in range(2)]
-    logs = jnp.concatenate([in_ref[d * NX + x, 12:13, :] for d in range(NZ)], axis=0)
-    means = jnp.concatenate([in_ref[d * NX + x, 13:14, :] for d in range(NZ)], axis=0)
+    logs = jnp.concatenate([in_ref[x * NZ + d, 12:13, :] for d in range(NZ)], axis=0)
+    means = jnp.concatenate([in_ref[x * NZ + d, 13:14, :] for d in range(NZ)], axis=0)
     lse, offset, _ = weights(logs, means)
     stats = three(lse) + three(offset) + [jnp.zeros((2, 128), F32)]
     piece = jnp.concatenate([f[0], f[1], jnp.where(top, h[0], pltpu.roll(h[1], 4, 0))] + stats, axis=0)
@@ -213,7 +213,7 @@
     def heads(f0, f1):
         return jnp.where(low, f0, pltpu.roll(f1, 64, 1)), jnp.where(low, pltpu.roll(f0, 64, 1), f1)
 
-    where = [(z4 + i) * NY + y for i in range(4)]
+    where = [y * NZ + z4 + i for i in range(4)]
     pairs = [by_core(at_ref, own_ref[w].astype(F32), other_ref[w].astype(F32)) for w in where]
     pieces = [[pairs[i][c] for i in range(4)] for c in range(NC)]
     for p in range(2):
@@ -281,7 +281,7 @@
 def head_grads(told_ref, y, kv, qs):
     logs, offsets = [], []
     for t in range(3):
-        piece = told_ref[t * NY + y].astype(F32)
+        piece = told_ref[y * NZ + t].astype(F32)
         logs.append(piece[24:25] + piece[25:26] + piece[26:27])
         offsets.append(piece[27:28] + piece[28:29] + piece[29:30])
     lse = jnp.concatenate(logs, axis=1)
@@ -342,7 +342,7 @@
         moved=mega,
         exps=MEMS * ROWS,
     )(at, memory, *mine)
-    part = lax.all_to_all(part, ("z", "row"), 0, 0, tiled=True)
+    part = lax.all_to_all(part, ("row", "z"), 0, 0, tiled=True)
     heads = call(pack_query, [shape((NY, MINE, 128), BF16)] * NX, 2, smem=1, moved=3 * mega)(at, query, out_grad)
     part, away, *heads = lax.optimization_barrier((part, away, *heads))
     piece = call(
@@ -353,7 +353,7 @@
         scratch=[pltpu.VMEM((NX, 128, 128), F32)],
         moved=mega,
     )(zx, part)
-    piece = lax.all_to_all(piece, ("z", "y"), 0, 0, tiled=True)
+    piece = lax.all_to_all(piece, ("y", "z"), 0, 0, tiled=True)
     heads = around(list(heads))
     piece, *heads = lax.optimization_barrier((piece, *heads))
     other = lax.ppermute(piece, "core", SWAP)

time: 94.8 us -> 93.5 us (0.986)
  waiting for transfers between devices: 24.3 us -> 20.4 us
  starting transfers between devices: 53.4 us -> 56.1 us
    all_to_all x2, waiting for transfers between devices: 10.3 us -> 6.68 us  [the longest x1 6.58 us: local(): part = lax.all_to_all(part, ('row', 'z'), 0, 0, tiled=True)]
    ppermute x1, starting transfers between devices: 4.98 us -> 6.84 us  [local(): other = lax.ppermute(piece, 'core', SWAP)]
where the time goes in v6:
time: 93.5 us; the launch traced here: 92.9 us
  starting transfers between devices  56.1 us (60%)
  waiting for transfers between devices  20.4 us (22%)
  Pallas kernels  14.1 us (15%)
  local copies, waits for them, and re-layouts  1.37 us (1%)
    ppermute x6, starting transfers between devices, around(): lax.ppermute(parts[k], 'row', [(i, (i + k) % NX) for i in range(NX)])  18.5 us
    all_to_all x1, starting transfers between devices, local(): part = lax.all_to_all(part, ('row', 'z'), 0, 0, tiled=True)  11.4 us
    all_to_all x1, starting transfers between devices, local(): lax.all_to_all(home, ('y', 'core'), 0, 0, tiled=True).reshape(MEMS, 128)  10.4 us
    ppermute x6, waiting for transfers between devices, around(): lax.ppermute(parts[k], 'row', [(i, (i + k) % NX) for i in range(NX)])  7.53 us
    ppermute x1, starting transfers between devices, local(): other = lax.ppermute(piece, 'core', SWAP)  6.84 us
    all_to_all x1, waiting for transfers between devices, local(): part = lax.all_to_all(part, ('row', 'z'), 0, 0, tiled=True)  6.58 us
    all_to_all x1, waiting for transfers between devices, local(): lax.all_to_all(home, ('y', 'core'), 0, 0, tiled=True).reshape(MEMS, 128)  5.82 us
    all_to_all x1, starting transfers between devices, local(): piece = lax.all_to_all(piece, ('y', 'z'), 0, 0, tiled=True)  5.08 us
  transfers between devices with their start and end apart: 12, of which 7 were waited for; matrix products, arithmetic and copies ran while one was open for 0% of the time, Pallas kernels for 6%

profile of v6, /device:TPU:1, one launch (start us, length us, event | category | flops | bytes accessed | tf_op | source)
XLA Modules:
  0.0 92.9 jit_solution(2864626170453762767)
XLA Ops:
  0.6 2.1 %shard_map.67.in_ref = bf16[16,128,128]{2,1,0:T(8,128)(2,1)} custom-call(bf16[128,1024]{1,0:T(8,128)(2,1)} %k_hbm.1, bf16[128,1024]{1,0:T(8,128)(2,1)} %v_hbm.1), custom_call_target="tpu_custom_call" | custom-call | bytes 1048576 | tf_op jit(solution)/shard_map/pallas_call | solution.py:319
  2.8 10.4 %all-to-all-start = ((bf16[16,128,128]{2,1,0:T(8,128)(2,1)}), bf16[16,128,128]{2,1,0:T(8,128)(2,1)S(1)}, u32[]{:S(2)}, u32[]{:S(2)}) async-start(bf16[16,128,128]{2,1,0:T(8,128)(2,1)} %shard_map.67.in_ref), calls=%async_computation | async-start | bytes 1048576 | tf_op jit(solution)/shard_map/all_to_all | solution.py:328
  13.9 1.9 %collective-permute-start = (bf16[96,128]{1,0:T(8,128)(2,1)S(1)}, bf16[96,128]{1,0:T(8,128)(2,1)S(1)}, u32[]{:S(2)}, u32[]{:S(2)}) collective-permute-start(bf16[96,128]{1,0:T(8,128)(2,1)S(1)} %get-tuple-element.31), channel_id=1, source_target_pairs={{0,1},{1,2},{2,3},{3,0},{4,5},{5,6},{6,7},{7,4},{8,9},{9,10},{10,1... | collective-permute-start | bytes 73736 | tf_op jit(solution)/shard_map/ppermute | solution.py:305
  15.9 4.0 %collective-permute-start.1 = (bf16[96,128]{1,0:T(8,128)(2,1)S(1)}, bf16[96,128]{1,0:T(8,128)(2,1)S(1)}, u32[]{:S(2)}, u32[]{:S(2)}) collective-permute-start(bf16[96,128]{1,0:T(8,128)(2,1)S(1)} %get-tuple-element.32), channel_id=1, source_target_pairs={{0,2},{1,3},{2,0},{3,1},{4,6},{5,7},{6,4},{7,5},{8,10},{9,11},{10,... | collective-permute-start | bytes 73736 | tf_op jit(solution)/shard_map/ppermute | solution.py:305
  19.8 3.1 %collective-permute-start.2 = (bf16[96,128]{1,0:T(8,128)(2,1)S(1)}, bf16[96,128]{1,0:T(8,128)(2,1)S(1)}, u32[]{:S(2)}, u32[]{:S(2)}) collective-permute-start(bf16[96,128]{1,0:T(8,128)(2,1)S(1)} %get-tuple-element.33), channel_id=1, source_target_pairs={{0,3},{1,0},{2,1},{3,2},{4,7},{5,4},{6,5},{7,6},{8,11},{9,8},{10,9... | collective-permute-start | bytes 73736 | tf_op jit(solution)/shard_map/ppermute | solution.py:305
  22.9 1.8 %collective-permute-done.2.q3 = bf16[96,128]{1,0:T(8,128)(2,1)S(1)} collective-permute-done((bf16[96,128]{1,0:T(8,128)(2,1)S(1)}, bf16[96,128]{1,0:T(8,128)(2,1)S(1)}, u32[]{:S(2)}, u32[]{:S(2)}) %collective-permute-start.2) | collective-permute-done | bytes 24608 | tf_op jit(solution)/shard_map/ppermute | solution.py:305
  24.7 5.8 %all-to-all-done = bf16[16,128,128]{2,1,0:T(8,128)(2,1)S(1)} async-done(((bf16[16,128,128]{2,1,0:T(8,128)(2,1)}), bf16[16,128,128]{2,1,0:T(8,128)(2,1)S(1)}, u32[]{:S(2)}, u32[]{:S(2)}) %all-to-all-start) | async-done | bytes 524320 | tf_op jit(solution)/shard_map/all_to_all | solution.py:328
  30.5 3.8 %shard_map.69 = f32[32,16,128]{2,1,0:T(8,128)} custom-call(s32[3]{0:T(128)S(1)} %pad_add_fusion.1.at_ref, bf16[2048,128]{1,0:T(8,128)(2,1)S(1)} %bitcast.5, bf16[96,128]{1,0:T(8,128)(2,1)S(1)} %get-tuple-element.30.q0, bf16[96,128]{1,0:T(8,128)(2,1)S(1)} %collective-permute-done.q1, bf16[96,128]{1,0:T(8,128)(2,1)S(1)} %collective-permute-done.1.q2, ...), custom_call_target="tpu_custom_call" | custom-call | flops 805306368 | bytes 1048576 | tf_op jit(solution)/shard_map/pallas_call | solution.py:335
  34.3 11.4 %all-to-all-start.1 = ((f32[32,16,128]{2,1,0:T(8,128)}), f32[32,16,128]{2,1,0:T(8,128)S(1)}, u32[]{:S(2)}, u32[]{:S(2)}) async-start(f32[32,16,128]{2,1,0:T(8,128)} %shard_map.69), calls=%async_computation.1 | async-start | bytes 524288 | tf_op jit(solution)/shard_map/all_to_all | solution.py:345
  45.8 1.9 %collective-permute-start.3 = (bf16[8,128,128]{2,1,0:T(8,128)(2,1)S(1)}, bf16[8,128,128]{2,1,0:T(8,128)(2,1)S(1)}, u32[]{:S(2)}, u32[]{:S(2)}) collective-permute-start(bf16[8,128,128]{2,1,0:T(8,128)(2,1)S(1)} %get-tuple-element.34), channel_id=1, source_target_pairs={{0,4},{4,0},{1,5},{5,1},{2,6},{6,2},{3,7},{7,3},{8,12},{12,8},{9,1... | collective-permute-start | bytes 786440 | tf_op jit(solution)/shard_map/ppermute | solution.py:332
  47.7 1.3 %shard_map.71 = (bf16[8,96,128]{2,1,0:T(8,128)(2,1)S(1)}, bf16[8,96,128]{2,1,0:T(8,128)(2,1)S(1)}, bf16[8,96,128]{2,1,0:T(8,128)(2,1)S(1)}, bf16[8,96,128]{2,1,0:T(8,128)(2,1)S(1)}) custom-call(s32[3]{0:T(128)S(1)} %pad_add_fusion.1.at_ref, bf16[96,4096]{1,0:T(8,128)(2,1)S(1)} %copy-done.1, bf16[96,4096]{1,0:T(8,128)(2,1)S(1)} %copy-done.2), custom_call_target="tpu_custom_call" | custom-call | bytes 3145728 | tf_op jit(solution)/shard_map/pallas_call | solution.py:346
  50.4 6.6 %all-to-all-done.1.in_ref = f32[32,16,128]{2,1,0:T(8,128)S(1)} async-done(((f32[32,16,128]{2,1,0:T(8,128)}), f32[32,16,128]{2,1,0:T(8,128)S(1)}, u32[]{:S(2)}, u32[]{:S(2)}) %all-to-all-start.1) | async-done | bytes 262176 | tf_op jit(solution)/shard_map/all_to_all | solution.py:345
  57.0 2.0 %shard_map.72 = bf16[64,32,128]{2,1,0:T(8,128)(2,1)} custom-call(s32[2]{0:T(128)S(1)} %pad_add_fusion.at_ref, f32[32,16,128]{2,1,0:T(8,128)S(1)} %all-to-all-done.1.in_ref), custom_call_target="tpu_custom_call" | custom-call | bytes 1048576 | tf_op jit(solution)/shard_map/pallas_call | solution.py:348
  59.0 5.1 %all-to-all-start.2 = ((bf16[64,32,128]{2,1,0:T(8,128)(2,1)}), bf16[64,32,128]{2,1,0:T(8,128)(2,1)S(1)}, u32[]{:S(2)}, u32[]{:S(2)}) async-start(bf16[64,32,128]{2,1,0:T(8,128)(2,1)} %shard_map.72), calls=%async_computation.2 | async-start | bytes 1048576 | tf_op jit(solution)/shard_map/all_to_all | solution.py:356
  64.1 2.2 %collective-permute-start.4 = (bf16[8,96,128]{2,1,0:T(8,128)(2,1)S(1)}, bf16[8,96,128]{2,1,0:T(8,128)(2,1)S(1)}, u32[]{:S(2)}, u32[]{:S(2)}) collective-permute-start(bf16[8,96,128]{2,1,0:T(8,128)(2,1)S(1)} %copy-done.6), channel_id=1, source_target_pairs={{0,1},{1,2},{2,3},{3,0},{4,5},{5,6},{6,7},{7,4},{8,9},{9,10},{10,1... | collective-permute-start | bytes 589832 | tf_op jit(solution)/shard_map/ppermute | solution.py:305
  66.3 4.3 %collective-permute-start.5 = (bf16[8,96,128]{2,1,0:T(8,128)(2,1)S(1)}, bf16[8,96,128]{2,1,0:T(8,128)(2,1)S(1)}, u32[]{:S(2)}, u32[]{:S(2)}) collective-permute-start(bf16[8,96,128]{2,1,0:T(8,128)(2,1)S(1)} %copy-done.4), channel_id=1, source_target_pairs={{0,2},{1,3},{2,0},{3,1},{4,6},{5,7},{6,4},{7,5},{8,10},{9,11},{10,... | collective-permute-start | bytes 589832 | tf_op jit(solution)/shard_map/ppermute | solution.py:305
  70.6 3.0 %collective-permute-start.6 = (bf16[8,96,128]{2,1,0:T(8,128)(2,1)S(1)}, bf16[8,96,128]{2,1,0:T(8,128)(2,1)S(1)}, u32[]{:S(2)}, u32[]{:S(2)}) collective-permute-start(bf16[8,96,128]{2,1,0:T(8,128)(2,1)S(1)} %get-tuple-element.43), channel_id=1, source_target_pairs={{0,3},{1,0},{2,1},{3,2},{4,7},{5,4},{6,5},{7,6},{8,11},{9,8},{10,9... | collective-permute-start | bytes 589832 | tf_op jit(solution)/shard_map/ppermute | solution.py:305
  73.7 2.9 %collective-permute-done.5.q2 = bf16[8,96,128]{2,1,0:T(8,128)(2,1)S(1)} collective-permute-done((bf16[8,96,128]{2,1,0:T(8,128)(2,1)S(1)}, bf16[8,96,128]{2,1,0:T(8,128)(2,1)S(1)}, u32[]{:S(2)}, u32[]{:S(2)}) %collective-permute-start.5) | collective-permute-done | bytes 196640 | tf_op jit(solution)/shard_map/ppermute | solution.py:305
  76.6 2.9 %collective-permute-done.6.q3 = bf16[8,96,128]{2,1,0:T(8,128)(2,1)S(1)} collective-permute-done((bf16[8,96,128]{2,1,0:T(8,128)(2,1)S(1)}, bf16[8,96,128]{2,1,0:T(8,128)(2,1)S(1)}, u32[]{:S(2)}, u32[]{:S(2)}) %collective-permute-start.6) | collective-permute-done | bytes 196640 | tf_op jit(solution)/shard_map/ppermute | solution.py:305
  79.6 6.8 %collective-permute-start.8 = (bf16[64,32,128]{2,1,0:T(8,128)(2,1)S(1)}, bf16[64,32,128]{2,1,0:T(8,128)(2,1)S(1)}, u32[]{:S(2)}, u32[]{:S(2)}) collective-permute-start(bf16[64,32,128]{2,1,0:T(8,128)(2,1)S(1)} %all-to-all-done.2.told_ref.own_ref), channel_id=1, source_target_pairs={{0,4},{4,0},{1,5},{5,1},{2,6},{6,2},{3,7},{7,3},{8,12},{12,8},{9,1... | collective-permute-start | bytes 1572872 | tf_op jit(solution)/shard_map/ppermute | solution.py:359
  86.4 2.1 %shard_map.73 = (bf16[8,128,128]{2,1,0:T(8,128)(2,1)S(1)}, bf16[8,128,128]{2,1,0:T(8,128)(2,1)S(1)}) custom-call(bf16[64,32,128]{2,1,0:T(8,128)(2,1)S(1)} %all-to-all-done.2.told_ref.own_ref, bf16[8,128,128]{2,1,0:T(8,128)(2,1)S(1)} %get-tuple-element.45.own_ref, bf16[8,128,128]{2,1,0:T(8,128)(2,1)S(1)} %collective-permute-done.3.away_ref, ...), custom_call_target="tpu_custom_call" | custom-call | flops 805306368 | bytes 2097152 | tf_op jit(solution)/shard_map/pallas_call | solution.py:360
  88.5 1.9 %collective-permute-start.7 = (bf16[8,128,128]{2,1,0:T(8,128)(2,1)S(1)}, bf16[8,128,128]{2,1,0:T(8,128)(2,1)S(1)}, u32[]{:S(2)}, u32[]{:S(2)}) collective-permute-start(bf16[8,128,128]{2,1,0:T(8,128)(2,1)S(1)} %get-tuple-element.51), channel_id=1, source_target_pairs={{0,4},{4,0},{1,5},{5,1},{2,6},{6,2},{3,7},{7,3},{8,12},{12,8},{9,1... | collective-permute-start | bytes 786440 | tf_op jit(solution)/shard_map/ppermute | solution.py:363
  90.4 1.2 %shard_map.74 = bf16[96,4096]{1,0:T(8,128)(2,1)} custom-call(s32[1]{0:T(128)} %bitcast.3.core_ref.at_ref, bf16[64,32,128]{2,1,0:T(8,128)(2,1)S(1)} %all-to-all-done.2.told_ref.own_ref, bf16[64,32,128]{2,1,0:T(8,128)(2,1)S(1)} %collective-permute-done.8.other_ref), custom_call_target="tpu_custom_call" | custom-call | bytes 2097152 | tf_op jit(solution)/shard_map/pallas_call | solution.py:375
  91.9 1.0 %shard_map.75 = (bf16[128,1024]{1,0:T(8,128)(2,1)}, bf16[128,1024]{1,0:T(8,128)(2,1)}) custom-call(s32[1]{0:T(128)} %bitcast.3.core_ref.at_ref, bf16[8,128,128]{2,1,0:T(8,128)(2,1)S(1)} %get-tuple-element.53.grads_ref, bf16[8,128,128]{2,1,0:T(8,128)(2,1)S(1)} %collective-permute-done.7.sent_ref), custom_call_target="tpu_custom_call" | custom-call | bytes 2097152 | tf_op jit(solution)/shard_map/pallas_call | solution.py:377
  (25 shorter events, 2.7 us)
Async XLA Ops:
  0.6 12.6 %copy-start.2 = (bf16[96,4096]{1,0:T(8,128)(2,1)S(1)}, bf16[96,4096]{1,0:T(8,128)(2,1)}, u32[]{:S(2)}) copy-start(bf16[96,4096]{1,0:T(8,128)(2,1)} %g_ref.3) | copy-start | bytes 2359300
  2.8 10.5 %copy-start.1 = (bf16[96,4096]{1,0:T(8,128)(2,1)S(1)}, bf16[96,4096]{1,0:T(8,128)(2,1)}, u32[]{:S(2)}) copy-start(bf16[96,4096]{1,0:T(8,128)(2,1)} %q_ref.3) | copy-start | bytes 2359300
  2.8 27.7 %all-to-all-start = ((bf16[16,128,128]{2,1,0:T(8,128)(2,1)}), bf16[16,128,128]{2,1,0:T(8,128)(2,1)S(1)}, u32[]{:S(2)}, u32[]{:S(2)}) async-start(bf16[16,128,128]{2,1,0:T(8,128)(2,1)} %shard_map.67.in_ref), calls=%async_computation | async-start | bytes 1048576 | tf_op jit(solution)/shard_map/all_to_all | solution.py:328
  13.9 9.0 %collective-permute-start = (bf16[96,128]{1,0:T(8,128)(2,1)S(1)}, bf16[96,128]{1,0:T(8,128)(2,1)S(1)}, u32[]{:S(2)}, u32[]{:S(2)}) collective-permute-start(bf16[96,128]{1,0:T(8,128)(2,1)S(1)} %get-tuple-element.31), channel_id=1, source_target_pairs={{0,1},{1,2},{2,3},{3,0},{4,5},{5,6},{6,7},{7,4},{8,9},{9,10},{10,1... | collective-permute-start | bytes 73736 | tf_op jit(solution)/shard_map/ppermute | solution.py:305
  15.9 7.1 %collective-permute-start.1 = (bf16[96,128]{1,0:T(8,128)(2,1)S(1)}, bf16[96,128]{1,0:T(8,128)(2,1)S(1)}, u32[]{:S(2)}, u32[]{:S(2)}) collective-permute-start(bf16[96,128]{1,0:T(8,128)(2,1)S(1)} %get-tuple-element.32), channel_id=1, source_target_pairs={{0,2},{1,3},{2,0},{3,1},{4,6},{5,7},{6,4},{7,5},{8,10},{9,11},{10,... | collective-permute-start | bytes 73736 | tf_op jit(solution)/shard_map/ppermute | solution.py:305
  19.8 4.9 %collective-permute-start.2 = (bf16[96,128]{1,0:T(8,128)(2,1)S(1)}, bf16[96,128]{1,0:T(8,128)(2,1)S(1)}, u32[]{:S(2)}, u32[]{:S(2)}) collective-permute-start(bf16[96,128]{1,0:T(8,128)(2,1)S(1)} %get-tuple-element.33), channel_id=1, source_target_pairs={{0,3},{1,0},{2,1},{3,2},{4,7},{5,4},{6,5},{7,6},{8,11},{9,8},{10,9... | collective-permute-start | bytes 73736 | tf_op jit(solution)/shard_map/ppermute | solution.py:305
  34.3 11.4 %copy-start = (bf16[16,128,128]{2,1,0:T(8,128)(2,1)S(1)}, bf16[16,128,128]{2,1,0:T(8,128)(2,1)}, u32[]{:S(2)}) copy-start(bf16[16,128,128]{2,1,0:T(8,128)(2,1)} %shard_map.67.in_ref) | copy-start | bytes 1572868
  34.3 22.7 %all-to-all-start.1 = ((f32[32,16,128]{2,1,0:T(8,128)}), f32[32,16,128]{2,1,0:T(8,128)S(1)}, u32[]{:S(2)}, u32[]{:S(2)}) async-start(f32[32,16,128]{2,1,0:T(8,128)} %shard_map.69), calls=%async_computation.1 | async-start | bytes 524288 | tf_op jit(solution)/shard_map/all_to_all | solution.py:345
  45.8 4.7 %collective-permute-start.3 = (bf16[8,128,128]{2,1,0:T(8,128)(2,1)S(1)}, bf16[8,128,128]{2,1,0:T(8,128)(2,1)S(1)}, u32[]{:S(2)}, u32[]{:S(2)}) collective-permute-start(bf16[8,128,128]{2,1,0:T(8,128)(2,1)S(1)} %get-tuple-element.34), channel_id=1, source_target_pairs={{0,4},{4,0},{1,5},{5,1},{2,6},{6,2},{3,7},{7,3},{8,12},{12,8},{9,1... | collective-permute-start | bytes 786440 | tf_op jit(solution)/shard_map/ppermute | solution.py:332
  49.0 0.7 copy-start.3
  49.7 0.7 copy-start.5
  59.0 5.1 %copy-start.6 = (bf16[8,96,128]{2,1,0:T(8,128)(2,1)S(1)}, bf16[8,96,128]{2,1,0:T(8,128)(2,1)}, u32[]{:S(2)}) copy-start(bf16[8,96,128]{2,1,0:T(8,128)(2,1)} %copy-done.5) | copy-start | bytes 589828
  59.0 7.3 %copy-start.4 = (bf16[8,96,128]{2,1,0:T(8,128)(2,1)S(1)}, bf16[8,96,128]{2,1,0:T(8,128)(2,1)}, u32[]{:S(2)}) copy-start(bf16[8,96,128]{2,1,0:T(8,128)(2,1)} %copy-done.3) | copy-start | bytes 589828
  59.0 20.6 %all-to-all-start.2 = ((bf16[64,32,128]{2,1,0:T(8,128)(2,1)}), bf16[64,32,128]{2,1,0:T(8,128)(2,1)S(1)}, u32[]{:S(2)}, u32[]{:S(2)}) async-start(bf16[64,32,128]{2,1,0:T(8,128)(2,1)} %shard_map.72), calls=%async_computation.2 | async-start | bytes 1048576 | tf_op jit(solution)/shard_map/all_to_all | solution.py:356
  64.1 9.6 %collective-permute-start.4 = (bf16[8,96,128]{2,1,0:T(8,128)(2,1)S(1)}, bf16[8,96,128]{2,1,0:T(8,128)(2,1)S(1)}, u32[]{:S(2)}, u32[]{:S(2)}) collective-permute-start(bf16[8,96,128]{2,1,0:T(8,128)(2,1)S(1)} %copy-done.6), channel_id=1, source_target_pairs={{0,1},{1,2},{2,3},{3,0},{4,5},{5,6},{6,7},{7,4},{8,9},{9,10},{10,1... | collective-permute-start | bytes 589832 | tf_op jit(solution)/shard_map/ppermute | solution.py:305
  66.3 10.3 %collective-permute-start.5 = (bf16[8,96,128]{2,1,0:T(8,128)(2,1)S(1)}, bf16[8,96,128]{2,1,0:T(8,128)(2,1)S(1)}, u32[]{:S(2)}, u32[]{:S(2)}) collective-permute-start(bf16[8,96,128]{2,1,0:T(8,128)(2,1)S(1)} %copy-done.4), channel_id=1, source_target_pairs={{0,2},{1,3},{2,0},{3,1},{4,6},{5,7},{6,4},{7,5},{8,10},{9,11},{10,... | collective-permute-start | bytes 589832 | tf_op jit(solution)/shard_map/ppermute | solution.py:305
  70.6 8.8 %collective-permute-start.6 = (bf16[8,96,128]{2,1,0:T(8,128)(2,1)S(1)}, bf16[8,96,128]{2,1,0:T(8,128)(2,1)S(1)}, u32[]{:S(2)}, u32[]{:S(2)}) collective-permute-start(bf16[8,96,128]{2,1,0:T(8,128)(2,1)S(1)} %get-tuple-element.43), channel_id=1, source_target_pairs={{0,3},{1,0},{2,1},{3,2},{4,7},{5,4},{6,5},{7,6},{8,11},{9,8},{10,9... | collective-permute-start | bytes 589832 | tf_op jit(solution)/shard_map/ppermute | solution.py:305
  79.6 10.9 %collective-permute-start.8 = (bf16[64,32,128]{2,1,0:T(8,128)(2,1)S(1)}, bf16[64,32,128]{2,1,0:T(8,128)(2,1)S(1)}, u32[]{:S(2)}, u32[]{:S(2)}) collective-permute-start(bf16[64,32,128]{2,1,0:T(8,128)(2,1)S(1)} %all-to-all-done.2.told_ref.own_ref), channel_id=1, source_target_pairs={{0,4},{4,0},{1,5},{5,1},{2,6},{6,2},{3,7},{7,3},{8,12},{12,8},{9,1... | collective-permute-start | bytes 1572872 | tf_op jit(solution)/shard_map/ppermute | solution.py:359
  88.5 3.4 %collective-permute-start.7 = (bf16[8,128,128]{2,1,0:T(8,128)(2,1)S(1)}, bf16[8,128,128]{2,1,0:T(8,128)(2,1)S(1)}, u32[]{:S(2)}, u32[]{:S(2)}) collective-permute-start(bf16[8,128,128]{2,1,0:T(8,128)(2,1)S(1)} %get-tuple-element.51), channel_id=1, source_target_pairs={{0,4},{4,0},{1,5},{5,1},{2,6},{6,2},{3,7},{7,3},{8,12},{12,8},{9,1... | collective-permute-start | bytes 786440 | tf_op jit(solution)/shard_map/ppermute | solution.py:363

commit v7 on v6

--- a/solution.py
+++ b/solution.py
@@ -59,15 +59,15 @@
             copies[t // 2 + 1].wait()
         k = k_ref[:, 128 * t : 128 * t + 128]
         v = v_ref[:, 128 * t : 128 * t + 128]
-        out_ref[2 * t] = jnp.concatenate([k[:, :64], v[:, :64]], axis=1)
-        out_ref[2 * t + 1] = jnp.concatenate([k[:, 64:], v[:, 64:]], axis=1)
+        out_ref[t] = jnp.concatenate([k[:, :64], v[:, :64]], axis=1)
+        out_ref[NY + t] = jnp.concatenate([k[:, 64:], v[:, 64:]], axis=1)
 
 
 def split_heads(core_ref, in_ref, own_ref, away_ref):
     c = core_ref[0]
     for t in range(HEADS // 2):
-        own_ref[t] = in_ref[2 * t + c]
-        away_ref[t] = in_ref[2 * t + 1 - c]
+        own_ref[t] = in_ref[NY * c + t]
+        away_ref[t] = in_ref[NY * (1 - c) + t]
 
 
 def pack_mine(at_ref, q_ref, g_ref, *outs):
@@ -325,7 +325,7 @@
         compiler_params=pltpu.CompilerParams(vmem_limit_bytes=60 * 2**20),
         cost_estimate=pl.CostEstimate(flops=0, bytes_accessed=mega, transcendentals=0),
     )(keys, values)
-    memory = lax.all_to_all(home, ("y", "core"), 0, 0, tiled=True).reshape(MEMS, 128)
+    memory = lax.all_to_all(home, ("core", "y"), 0, 0, tiled=True).reshape(MEMS, 128)
     mine = call(pack_mine, [shape((MINE, 128), BF16)] * NX, 2, smem=1, moved=mega)(at, query, out_grad)
     mine = around(list(mine))
     home_own, home_away = call(split_heads, [half, half], 1, smem=1, moved=mega)(corez, home)

time: 93.5 us -> 93.7 us (level)
  starting transfers between devices: 56.1 us -> 60.5 us
  waiting for transfers between devices: 20.4 us -> 16.1 us
    all_to_all x1, starting transfers between devices: 5.08 us -> 9.71 us  [local(): piece = lax.all_to_all(piece, ('y', 'z'), 0, 0, tiled=True)]
    all_to_all x1, waiting for transfers between devices: 6.58 us -> 3.69 us  [local(): part = lax.all_to_all(part, ('row', 'z'), 0, 0, tiled=True)]
    all_to_all x1, waiting for transfers between devices: 5.82 us -> 3.3 us  [local(): lax.all_to_all(home, ('core', 'y'), 0, 0, tiled=True).reshape(MEMS, 128)]
    ppermute x1, starting transfers between devices: 1.92 us -> 3.18 us  [local(): away = lax.ppermute(home_away, 'core', SWAP)]
    all_to_all x1, waiting for transfers between devices: 0.1 us -> 1.27 us  [local(): piece = lax.all_to_all(piece, ('y', 'z'), 0, 0, tiled=True)]
where the time goes in v7:
time: 93.7 us; the launch traced here: 93.1 us
  starting transfers between devices  60.5 us (65%)
  waiting for transfers between devices  16.1 us (17%)
  Pallas kernels  14.1 us (15%)
  local copies, waits for them, and re-layouts  1.37 us (1%)
    ppermute x6, starting transfers between devices, around(): lax.ppermute(parts[k], 'row', [(i, (i + k) % NX) for i in range(NX)])  17.8 us
    all_to_all x1, starting transfers between devices, local(): part = lax.all_to_all(part, ('row', 'z'), 0, 0, tiled=True)  11.3 us
    all_to_all x1, starting transfers between devices, local(): lax.all_to_all(home, ('core', 'y'), 0, 0, tiled=True).reshape(MEMS, 128)  10.4 us
    all_to_all x1, starting transfers between devices, local(): piece = lax.all_to_all(piece, ('y', 'z'), 0, 0, tiled=True)  9.71 us
    ppermute x6, waiting for transfers between devices, around(): lax.ppermute(parts[k], 'row', [(i, (i + k) % NX) for i in range(NX)])  7.48 us
    ppermute x1, starting transfers between devices, local(): other = lax.ppermute(piece, 'core', SWAP)  6.16 us
    pallas_call x1, Pallas kernels, local(): call(local_part, shape((NZ * NX, 16, 128), F32), 5, smem=1, scratch=[pltp...  3.8 us
    all_to_all x1, waiting for transfers between devices, local(): part = lax.all_to_all(part, ('row', 'z'), 0, 0, tiled=True)  3.69 us
  transfers between devices with their start and end apart: 12, of which 7 were waited for; matrix products, arithmetic and copies ran while one was open for 0% of the time, Pallas kernels for 6%

profile of v7, /device:TPU:1, one launch (start us, length us, event | category | flops | bytes accessed | tf_op | source)
XLA Modules:
  0.0 93.1 jit_solution(16675184256362532281)
XLA Ops:
  0.6 2.1 %shard_map.67.in_ref = bf16[16,128,128]{2,1,0:T(8,128)(2,1)} custom-call(bf16[128,1024]{1,0:T(8,128)(2,1)} %k_hbm.1, bf16[128,1024]{1,0:T(8,128)(2,1)} %v_hbm.1), custom_call_target="tpu_custom_call" | custom-call | bytes 1048576 | tf_op jit(solution)/shard_map/pallas_call | solution.py:319
  2.8 10.4 %all-to-all-start = ((bf16[16,128,128]{2,1,0:T(8,128)(2,1)}), bf16[16,128,128]{2,1,0:T(8,128)(2,1)S(1)}, u32[]{:S(2)}, u32[]{:S(2)}) async-start(bf16[16,128,128]{2,1,0:T(8,128)(2,1)} %shard_map.67.in_ref), calls=%async_computation | async-start | bytes 1048576 | tf_op jit(solution)/shard_map/all_to_all | solution.py:328
  14.0 1.9 %collective-permute-start = (bf16[96,128]{1,0:T(8,128)(2,1)S(1)}, bf16[96,128]{1,0:T(8,128)(2,1)S(1)}, u32[]{:S(2)}, u32[]{:S(2)}) collective-permute-start(bf16[96,128]{1,0:T(8,128)(2,1)S(1)} %get-tuple-element.31), channel_id=1, source_target_pairs={{0,1},{1,2},{2,3},{3,0},{4,5},{5,6},{6,7},{7,4},{8,9},{9,10},{10,1... | collective-permute-start | bytes 73736 | tf_op jit(solution)/shard_map/ppermute | solution.py:305
  15.9 3.9 %collective-permute-start.1 = (bf16[96,128]{1,0:T(8,128)(2,1)S(1)}, bf16[96,128]{1,0:T(8,128)(2,1)S(1)}, u32[]{:S(2)}, u32[]{:S(2)}) collective-permute-start(bf16[96,128]{1,0:T(8,128)(2,1)S(1)} %get-tuple-element.32), channel_id=1, source_target_pairs={{0,2},{1,3},{2,0},{3,1},{4,6},{5,7},{6,4},{7,5},{8,10},{9,11},{10,... | collective-permute-start | bytes 73736 | tf_op jit(solution)/shard_map/ppermute | solution.py:305
  19.8 3.1 %collective-permute-start.2 = (bf16[96,128]{1,0:T(8,128)(2,1)S(1)}, bf16[96,128]{1,0:T(8,128)(2,1)S(1)}, u32[]{:S(2)}, u32[]{:S(2)}) collective-permute-start(bf16[96,128]{1,0:T(8,128)(2,1)S(1)} %get-tuple-element.33), channel_id=1, source_target_pairs={{0,3},{1,0},{2,1},{3,2},{4,7},{5,4},{6,5},{7,6},{8,11},{9,8},{10,9... | collective-permute-start | bytes 73736 | tf_op jit(solution)/shard_map/ppermute | solution.py:305
  22.9 1.8 %collective-permute-done.2.q3 = bf16[96,128]{1,0:T(8,128)(2,1)S(1)} collective-permute-done((bf16[96,128]{1,0:T(8,128)(2,1)S(1)}, bf16[96,128]{1,0:T(8,128)(2,1)S(1)}, u32[]{:S(2)}, u32[]{:S(2)}) %collective-permute-start.2) | collective-permute-done | bytes 24608 | tf_op jit(solution)/shard_map/ppermute | solution.py:305
  24.7 3.3 %all-to-all-done = bf16[16,128,128]{2,1,0:T(8,128)(2,1)S(1)} async-done(((bf16[16,128,128]{2,1,0:T(8,128)(2,1)}), bf16[16,128,128]{2,1,0:T(8,128)(2,1)S(1)}, u32[]{:S(2)}, u32[]{:S(2)}) %all-to-all-start) | async-done | bytes 524320 | tf_op jit(solution)/shard_map/all_to_all | solution.py:328
  28.0 3.8 %shard_map.69 = f32[32,16,128]{2,1,0:T(8,128)} custom-call(s32[3]{0:T(128)S(1)} %pad_add_fusion.1.at_ref, bf16[2048,128]{1,0:T(8,128)(2,1)S(1)} %bitcast.5, bf16[96,128]{1,0:T(8,128)(2,1)S(1)} %get-tuple-element.30.q0, bf16[96,128]{1,0:T(8,128)(2,1)S(1)} %collective-permute-done.q1, bf16[96,128]{1,0:T(8,128)(2,1)S(1)} %collective-permute-done.1.q2, ...), custom_call_target="tpu_custom_call" | custom-call | flops 805306368 | bytes 1048576 | tf_op jit(solution)/shard_map/pallas_call | solution.py:335
  31.8 11.3 %all-to-all-start.1 = ((f32[32,16,128]{2,1,0:T(8,128)}), f32[32,16,128]{2,1,0:T(8,128)S(1)}, u32[]{:S(2)}, u32[]{:S(2)}) async-start(f32[32,16,128]{2,1,0:T(8,128)} %shard_map.69), calls=%async_computation.1 | async-start | bytes 524288 | tf_op jit(solution)/shard_map/all_to_all | solution.py:345
  43.2 3.2 %collective-permute-start.3 = (bf16[8,128,128]{2,1,0:T(8,128)(2,1)S(1)}, bf16[8,128,128]{2,1,0:T(8,128)(2,1)S(1)}, u32[]{:S(2)}, u32[]{:S(2)}) collective-permute-start(bf16[8,128,128]{2,1,0:T(8,128)(2,1)S(1)} %get-tuple-element.34), channel_id=1, source_target_pairs={{0,4},{4,0},{1,5},{5,1},{2,6},{6,2},{3,7},{7,3},{8,12},{12,8},{9,1... | collective-permute-start | bytes 786440 | tf_op jit(solution)/shard_map/ppermute | solution.py:332
  46.4 1.3 %shard_map.71 = (bf16[8,96,128]{2,1,0:T(8,128)(2,1)S(1)}, bf16[8,96,128]{2,1,0:T(8,128)(2,1)S(1)}, bf16[8,96,128]{2,1,0:T(8,128)(2,1)S(1)}, bf16[8,96,128]{2,1,0:T(8,128)(2,1)S(1)}) custom-call(s32[3]{0:T(128)S(1)} %pad_add_fusion.1.at_ref, bf16[96,4096]{1,0:T(8,128)(2,1)S(1)} %copy-done.1, bf16[96,4096]{1,0:T(8,128)(2,1)S(1)} %copy-done.2), custom_call_target="tpu_custom_call" | custom-call | bytes 3145728 | tf_op jit(solution)/shard_map/pallas_call | solution.py:346
  49.1 3.7 %all-to-all-done.1.in_ref = f32[32,16,128]{2,1,0:T(8,128)S(1)} async-done(((f32[32,16,128]{2,1,0:T(8,128)}), f32[32,16,128]{2,1,0:T(8,128)S(1)}, u32[]{:S(2)}, u32[]{:S(2)}) %all-to-all-start.1) | async-done | bytes 262176 | tf_op jit(solution)/shard_map/all_to_all | solution.py:345
  52.8 2.0 %shard_map.72 = bf16[64,32,128]{2,1,0:T(8,128)(2,1)} custom-call(s32[2]{0:T(128)S(1)} %pad_add_fusion.at_ref, f32[32,16,128]{2,1,0:T(8,128)S(1)} %all-to-all-done.1.in_ref), custom_call_target="tpu_custom_call" | custom-call | bytes 1048576 | tf_op jit(solution)/shard_map/pallas_call | solution.py:348
  54.8 9.7 %all-to-all-start.2 = ((bf16[64,32,128]{2,1,0:T(8,128)(2,1)}), bf16[64,32,128]{2,1,0:T(8,128)(2,1)S(1)}, u32[]{:S(2)}, u32[]{:S(2)}) async-start(bf16[64,32,128]{2,1,0:T(8,128)(2,1)} %shard_map.72), calls=%async_computation.2 | async-start | bytes 1048576 | tf_op jit(solution)/shard_map/all_to_all | solution.py:356
  64.5 2.2 %collective-permute-start.4 = (bf16[8,96,128]{2,1,0:T(8,128)(2,1)S(1)}, bf16[8,96,128]{2,1,0:T(8,128)(2,1)S(1)}, u32[]{:S(2)}, u32[]{:S(2)}) collective-permute-start(bf16[8,96,128]{2,1,0:T(8,128)(2,1)S(1)} %copy-done.6), channel_id=1, source_target_pairs={{0,1},{1,2},{2,3},{3,0},{4,5},{5,6},{6,7},{7,4},{8,9},{9,10},{10,1... | collective-permute-start | bytes 589832 | tf_op jit(solution)/shard_map/ppermute | solution.py:305
  66.8 3.7 %collective-permute-start.5 = (bf16[8,96,128]{2,1,0:T(8,128)(2,1)S(1)}, bf16[8,96,128]{2,1,0:T(8,128)(2,1)S(1)}, u32[]{:S(2)}, u32[]{:S(2)}) collective-permute-start(bf16[8,96,128]{2,1,0:T(8,128)(2,1)S(1)} %copy-done.4), channel_id=1, source_target_pairs={{0,2},{1,3},{2,0},{3,1},{4,6},{5,7},{6,4},{7,5},{8,10},{9,11},{10,... | collective-permute-start | bytes 589832 | tf_op jit(solution)/shard_map/ppermute | solution.py:305
  70.4 3.0 %collective-permute-start.6 = (bf16[8,96,128]{2,1,0:T(8,128)(2,1)S(1)}, bf16[8,96,128]{2,1,0:T(8,128)(2,1)S(1)}, u32[]{:S(2)}, u32[]{:S(2)}) collective-permute-start(bf16[8,96,128]{2,1,0:T(8,128)(2,1)S(1)} %get-tuple-element.43), channel_id=1, source_target_pairs={{0,3},{1,0},{2,1},{3,2},{4,7},{5,4},{6,5},{7,6},{8,11},{9,8},{10,9... | collective-permute-start | bytes 589832 | tf_op jit(solution)/shard_map/ppermute | solution.py:305
  73.5 3.4 %collective-permute-done.5.q2 = bf16[8,96,128]{2,1,0:T(8,128)(2,1)S(1)} collective-permute-done((bf16[8,96,128]{2,1,0:T(8,128)(2,1)S(1)}, bf16[8,96,128]{2,1,0:T(8,128)(2,1)S(1)}, u32[]{:S(2)}, u32[]{:S(2)}) %collective-permute-start.5) | collective-permute-done | bytes 196640 | tf_op jit(solution)/shard_map/ppermute | solution.py:305
  76.9 2.3 %collective-permute-done.6.q3 = bf16[8,96,128]{2,1,0:T(8,128)(2,1)S(1)} collective-permute-done((bf16[8,96,128]{2,1,0:T(8,128)(2,1)S(1)}, bf16[8,96,128]{2,1,0:T(8,128)(2,1)S(1)}, u32[]{:S(2)}, u32[]{:S(2)}) %collective-permute-start.6) | collective-permute-done | bytes 196640 | tf_op jit(solution)/shard_map/ppermute | solution.py:305
  79.2 1.3 %all-to-all-done.2.told_ref.own_ref = bf16[64,32,128]{2,1,0:T(8,128)(2,1)S(1)} async-done(((bf16[64,32,128]{2,1,0:T(8,128)(2,1)}), bf16[64,32,128]{2,1,0:T(8,128)(2,1)S(1)}, u32[]{:S(2)}, u32[]{:S(2)}) %all-to-all-start.2) | async-done | bytes 524320 | tf_op jit(solution)/shard_map/all_to_all | solution.py:356
  80.4 6.2 %collective-permute-start.8 = (bf16[64,32,128]{2,1,0:T(8,128)(2,1)S(1)}, bf16[64,32,128]{2,1,0:T(8,128)(2,1)S(1)}, u32[]{:S(2)}, u32[]{:S(2)}) collective-permute-start(bf16[64,32,128]{2,1,0:T(8,128)(2,1)S(1)} %all-to-all-done.2.told_ref.own_ref), channel_id=1, source_target_pairs={{0,4},{4,0},{1,5},{5,1},{2,6},{6,2},{3,7},{7,3},{8,12},{12,8},{9,1... | collective-permute-start | bytes 1572872 | tf_op jit(solution)/shard_map/ppermute | solution.py:359
  86.6 2.1 %shard_map.73 = (bf16[8,128,128]{2,1,0:T(8,128)(2,1)S(1)}, bf16[8,128,128]{2,1,0:T(8,128)(2,1)S(1)}) custom-call(bf16[64,32,128]{2,1,0:T(8,128)(2,1)S(1)} %all-to-all-done.2.told_ref.own_ref, bf16[8,128,128]{2,1,0:T(8,128)(2,1)S(1)} %get-tuple-element.45.own_ref, bf16[8,128,128]{2,1,0:T(8,128)(2,1)S(1)} %collective-permute-done.3.away_ref, ...), custom_call_target="tpu_custom_call" | custom-call | flops 805306368 | bytes 2097152 | tf_op jit(solution)/shard_map/pallas_call | solution.py:360
  88.7 1.9 %collective-permute-start.7 = (bf16[8,128,128]{2,1,0:T(8,128)(2,1)S(1)}, bf16[8,128,128]{2,1,0:T(8,128)(2,1)S(1)}, u32[]{:S(2)}, u32[]{:S(2)}) collective-permute-start(bf16[8,128,128]{2,1,0:T(8,128)(2,1)S(1)} %get-tuple-element.51), channel_id=1, source_target_pairs={{0,4},{4,0},{1,5},{5,1},{2,6},{6,2},{3,7},{7,3},{8,12},{12,8},{9,1... | collective-permute-start | bytes 786440 | tf_op jit(solution)/shard_map/ppermute | solution.py:363
  90.6 1.2 %shard_map.74 = bf16[96,4096]{1,0:T(8,128)(2,1)} custom-call(s32[1]{0:T(128)} %bitcast.3.core_ref.at_ref, bf16[64,32,128]{2,1,0:T(8,128)(2,1)S(1)} %all-to-all-done.2.told_ref.own_ref, bf16[64,32,128]{2,1,0:T(8,128)(2,1)S(1)} %collective-permute-done.8.other_ref), custom_call_target="tpu_custom_call" | custom-call | bytes 2097152 | tf_op jit(solution)/shard_map/pallas_call | solution.py:375
  (25 shorter events, 3.5 us)
Async XLA Ops:
  0.6 12.7 %copy-start.2 = (bf16[96,4096]{1,0:T(8,128)(2,1)S(1)}, bf16[96,4096]{1,0:T(8,128)(2,1)}, u32[]{:S(2)}) copy-start(bf16[96,4096]{1,0:T(8,128)(2,1)} %g_ref.3) | copy-start | bytes 2359300
  2.8 10.5 %copy-start.1 = (bf16[96,4096]{1,0:T(8,128)(2,1)S(1)}, bf16[96,4096]{1,0:T(8,128)(2,1)}, u32[]{:S(2)}) copy-start(bf16[96,4096]{1,0:T(8,128)(2,1)} %q_ref.3) | copy-start | bytes 2359300
  2.8 25.2 %all-to-all-start = ((bf16[16,128,128]{2,1,0:T(8,128)(2,1)}), bf16[16,128,128]{2,1,0:T(8,128)(2,1)S(1)}, u32[]{:S(2)}, u32[]{:S(2)}) async-start(bf16[16,128,128]{2,1,0:T(8,128)(2,1)} %shard_map.67.in_ref), calls=%async_computation | async-start | bytes 1048576 | tf_op jit(solution)/shard_map/all_to_all | solution.py:328
  14.0 8.9 %collective-permute-start = (bf16[96,128]{1,0:T(8,128)(2,1)S(1)}, bf16[96,128]{1,0:T(8,128)(2,1)S(1)}, u32[]{:S(2)}, u32[]{:S(2)}) collective-permute-start(bf16[96,128]{1,0:T(8,128)(2,1)S(1)} %get-tuple-element.31), channel_id=1, source_target_pairs={{0,1},{1,2},{2,3},{3,0},{4,5},{5,6},{6,7},{7,4},{8,9},{9,10},{10,1... | collective-permute-start | bytes 73736 | tf_op jit(solution)/shard_map/ppermute | solution.py:305
  15.9 7.0 %collective-permute-start.1 = (bf16[96,128]{1,0:T(8,128)(2,1)S(1)}, bf16[96,128]{1,0:T(8,128)(2,1)S(1)}, u32[]{:S(2)}, u32[]{:S(2)}) collective-permute-start(bf16[96,128]{1,0:T(8,128)(2,1)S(1)} %get-tuple-element.32), channel_id=1, source_target_pairs={{0,2},{1,3},{2,0},{3,1},{4,6},{5,7},{6,4},{7,5},{8,10},{9,11},{10,... | collective-permute-start | bytes 73736 | tf_op jit(solution)/shard_map/ppermute | solution.py:305
  19.8 4.9 %collective-permute-start.2 = (bf16[96,128]{1,0:T(8,128)(2,1)S(1)}, bf16[96,128]{1,0:T(8,128)(2,1)S(1)}, u32[]{:S(2)}, u32[]{:S(2)}) collective-permute-start(bf16[96,128]{1,0:T(8,128)(2,1)S(1)} %get-tuple-element.33), channel_id=1, source_target_pairs={{0,3},{1,0},{2,1},{3,2},{4,7},{5,4},{6,5},{7,6},{8,11},{9,8},{10,9... | collective-permute-start | bytes 73736 | tf_op jit(solution)/shard_map/ppermute | solution.py:305
  31.8 11.4 %copy-start = (bf16[16,128,128]{2,1,0:T(8,128)(2,1)S(1)}, bf16[16,128,128]{2,1,0:T(8,128)(2,1)}, u32[]{:S(2)}) copy-start(bf16[16,128,128]{2,1,0:T(8,128)(2,1)} %shard_map.67.in_ref) | copy-start | bytes 1572868
  31.8 21.0 %all-to-all-start.1 = ((f32[32,16,128]{2,1,0:T(8,128)}), f32[32,16,128]{2,1,0:T(8,128)S(1)}, u32[]{:S(2)}, u32[]{:S(2)}) async-start(f32[32,16,128]{2,1,0:T(8,128)} %shard_map.69), calls=%async_computation.1 | async-start | bytes 524288 | tf_op jit(solution)/shard_map/all_to_all | solution.py:345
  43.2 5.9 %collective-permute-start.3 = (bf16[8,128,128]{2,1,0:T(8,128)(2,1)S(1)}, bf16[8,128,128]{2,1,0:T(8,128)(2,1)S(1)}, u32[]{:S(2)}, u32[]{:S(2)}) collective-permute-start(bf16[8,128,128]{2,1,0:T(8,128)(2,1)S(1)} %get-tuple-element.34), channel_id=1, source_target_pairs={{0,4},{4,0},{1,5},{5,1},{2,6},{6,2},{3,7},{7,3},{8,12},{12,8},{9,1... | collective-permute-start | bytes 786440 | tf_op jit(solution)/shard_map/ppermute | solution.py:332
  47.7 0.7 copy-start.3
  48.4 0.7 copy-start.5
  54.8 9.7 %copy-start.6 = (bf16[8,96,128]{2,1,0:T(8,128)(2,1)S(1)}, bf16[8,96,128]{2,1,0:T(8,128)(2,1)}, u32[]{:S(2)}) copy-start(bf16[8,96,128]{2,1,0:T(8,128)(2,1)} %copy-done.5) | copy-start | bytes 589828
  54.8 12.0 %copy-start.4 = (bf16[8,96,128]{2,1,0:T(8,128)(2,1)S(1)}, bf16[8,96,128]{2,1,0:T(8,128)(2,1)}, u32[]{:S(2)}) copy-start(bf16[8,96,128]{2,1,0:T(8,128)(2,1)} %copy-done.3) | copy-start | bytes 589828
  54.8 25.6 %all-to-all-start.2 = ((bf16[64,32,128]{2,1,0:T(8,128)(2,1)}), bf16[64,32,128]{2,1,0:T(8,128)(2,1)S(1)}, u32[]{:S(2)}, u32[]{:S(2)}) async-start(bf16[64,32,128]{2,1,0:T(8,128)(2,1)} %shard_map.72), calls=%async_computation.2 | async-start | bytes 1048576 | tf_op jit(solution)/shard_map/all_to_all | solution.py:356
  64.5 8.9 %collective-permute-start.4 = (bf16[8,96,128]{2,1,0:T(8,128)(2,1)S(1)}, bf16[8,96,128]{2,1,0:T(8,128)(2,1)S(1)}, u32[]{:S(2)}, u32[]{:S(2)}) collective-permute-start(bf16[8,96,128]{2,1,0:T(8,128)(2,1)S(1)} %copy-done.6), channel_id=1, source_target_pairs={{0,1},{1,2},{2,3},{3,0},{4,5},{5,6},{6,7},{7,4},{8,9},{9,10},{10,1... | collective-permute-start | bytes 589832 | tf_op jit(solution)/shard_map/ppermute | solution.py:305
  66.8 10.1 %collective-permute-start.5 = (bf16[8,96,128]{2,1,0:T(8,128)(2,1)S(1)}, bf16[8,96,128]{2,1,0:T(8,128)(2,1)S(1)}, u32[]{:S(2)}, u32[]{:S(2)}) collective-permute-start(bf16[8,96,128]{2,1,0:T(8,128)(2,1)S(1)} %copy-done.4), channel_id=1, source_target_pairs={{0,2},{1,3},{2,0},{3,1},{4,6},{5,7},{6,4},{7,5},{8,10},{9,11},{10,... | collective-permute-start | bytes 589832 | tf_op jit(solution)/shard_map/ppermute | solution.py:305
  70.4 8.7 %collective-permute-start.6 = (bf16[8,96,128]{2,1,0:T(8,128)(2,1)S(1)}, bf16[8,96,128]{2,1,0:T(8,128)(2,1)S(1)}, u32[]{:S(2)}, u32[]{:S(2)}) collective-permute-start(bf16[8,96,128]{2,1,0:T(8,128)(2,1)S(1)} %get-tuple-element.43), channel_id=1, source_target_pairs={{0,3},{1,0},{2,1},{3,2},{4,7},{5,4},{6,5},{7,6},{8,11},{9,8},{10,9... | collective-permute-start | bytes 589832 | tf_op jit(solution)/shard_map/ppermute | solution.py:305
  80.4 10.2 %collective-permute-start.8 = (bf16[64,32,128]{2,1,0:T(8,128)(2,1)S(1)}, bf16[64,32,128]{2,1,0:T(8,128)(2,1)S(1)}, u32[]{:S(2)}, u32[]{:S(2)}) collective-permute-start(bf16[64,32,128]{2,1,0:T(8,128)(2,1)S(1)} %all-to-all-done.2.told_ref.own_ref), channel_id=1, source_target_pairs={{0,4},{4,0},{1,5},{5,1},{2,6},{6,2},{3,7},{7,3},{8,12},{12,8},{9,1... | collective-permute-start | bytes 1572872 | tf_op jit(solution)/shard_map/ppermute | solution.py:359
  88.7 3.4 %collective-permute-start.7 = (bf16[8,128,128]{2,1,0:T(8,128)(2,1)S(1)}, bf16[8,128,128]{2,1,0:T(8,128)(2,1)S(1)}, u32[]{:S(2)}, u32[]{:S(2)}) collective-permute-start(bf16[8,128,128]{2,1,0:T(8,128)(2,1)S(1)} %get-tuple-element.51), channel_id=1, source_target_pairs={{0,4},{4,0},{1,5},{5,1},{2,6},{6,2},{3,7},{7,3},{8,12},{12,8},{9,1... | collective-permute-start | bytes 786440 | tf_op jit(solution)/shard_map/ppermute | solution.py:363

commit v8 on v6

--- a/solution.py
+++ b/solution.py
@@ -264,12 +264,11 @@
 
 def join_memory(at_ref, grads_ref, sent_ref, k_hbm, v_hbm, k_ref, v_ref, sems):
     copies, send = sender(sems)
-    low = low_lanes((BLOCK, 128))
     for y in range(NY):
-        a, b = by_core(at_ref, grads_ref[y].astype(F32), sent_ref[y].astype(F32))
+        a, b = by_core(at_ref, grads_ref[y], sent_ref[y])
         lanes = slice(128 * y, 128 * y + 128)
-        k_ref[:, lanes] = jnp.where(low, a, pltpu.roll(b, 64, 1)).astype(BF16)
-        v_ref[:, lanes] = jnp.where(low, pltpu.roll(a, 64, 1), b).astype(BF16)
+        k_ref[:, lanes] = jnp.concatenate([a[:, :64], b[:, :64]], axis=1)
+        v_ref[:, lanes] = jnp.concatenate([a[:, 64:], b[:, 64:]], axis=1)
         if y % 2 == 1:
             part = pl.ds(128 * (y - 1), 256)
             send(k_ref.at[:, part], k_hbm.at[:, part])

time: 93.5 us -> 93.5 us (level)
  no operation moved by 1% of the time
where the time goes in v8:
time: 93.5 us; the launch traced here: 92.9 us
  starting transfers between devices  56.1 us (60%)
  waiting for transfers between devices  20.4 us (22%)
  Pallas kernels  14.1 us (15%)
  local copies, waits for them, and re-layouts  1.37 us (1%)
    ppermute x6, starting transfers between devices, around(): lax.ppermute(parts[k], 'row', [(i, (i + k) % NX) for i in range(NX)])  18.5 us
    all_to_all x1, starting transfers between devices, local(): part = lax.all_to_all(part, ('row', 'z'), 0, 0, tiled=True)  11.4 us
    all_to_all x1, starting transfers between devices, local(): lax.all_to_all(home, ('y', 'core'), 0, 0, tiled=True).reshape(MEMS, 128)  10.4 us
    ppermute x6, waiting for transfers between devices, around(): lax.ppermute(parts[k], 'row', [(i, (i + k) % NX) for i in range(NX)])  7.53 us
    ppermute x1, starting transfers between devices, local(): other = lax.ppermute(piece, 'core', SWAP)  6.84 us
    all_to_all x1, waiting for transfers between devices, local(): part = lax.all_to_all(part, ('row', 'z'), 0, 0, tiled=True)  6.58 us
    all_to_all x1, waiting for transfers between devices, local(): lax.all_to_all(home, ('y', 'core'), 0, 0, tiled=True).reshape(MEMS, 128)  5.82 us
    all_to_all x1, starting transfers between devices, local(): piece = lax.all_to_all(piece, ('y', 'z'), 0, 0, tiled=True)  5.08 us
  transfers between devices with their start and end apart: 12, of which 7 were waited for; matrix products, arithmetic and copies ran while one was open for 0% of the time, Pallas kernels for 6%

profile of v8, /device:TPU:1, one launch (start us, length us, event | category | flops | bytes accessed | tf_op | source)
XLA Modules:
  0.0 92.9 jit_solution(17206670799744004504)
XLA Ops:
  0.6 2.1 %shard_map.67.in_ref = bf16[16,128,128]{2,1,0:T(8,128)(2,1)} custom-call(bf16[128,1024]{1,0:T(8,128)(2,1)} %k_hbm.1, bf16[128,1024]{1,0:T(8,128)(2,1)} %v_hbm.1), custom_call_target="tpu_custom_call" | custom-call | bytes 1048576 | tf_op jit(solution)/shard_map/pallas_call | solution.py:318
  2.8 10.4 %all-to-all-start = ((bf16[16,128,128]{2,1,0:T(8,128)(2,1)}), bf16[16,128,128]{2,1,0:T(8,128)(2,1)S(1)}, u32[]{:S(2)}, u32[]{:S(2)}) async-start(bf16[16,128,128]{2,1,0:T(8,128)(2,1)} %shard_map.67.in_ref), calls=%async_computation | async-start | bytes 1048576 | tf_op jit(solution)/shard_map/all_to_all | solution.py:327
  13.9 1.9 %collective-permute-start = (bf16[96,128]{1,0:T(8,128)(2,1)S(1)}, bf16[96,128]{1,0:T(8,128)(2,1)S(1)}, u32[]{:S(2)}, u32[]{:S(2)}) collective-permute-start(bf16[96,128]{1,0:T(8,128)(2,1)S(1)} %get-tuple-element.31), channel_id=1, source_target_pairs={{0,1},{1,2},{2,3},{3,0},{4,5},{5,6},{6,7},{7,4},{8,9},{9,10},{10,1... | collective-permute-start | bytes 73736 | tf_op jit(solution)/shard_map/ppermute | solution.py:304
  15.9 4.0 %collective-permute-start.1 = (bf16[96,128]{1,0:T(8,128)(2,1)S(1)}, bf16[96,128]{1,0:T(8,128)(2,1)S(1)}, u32[]{:S(2)}, u32[]{:S(2)}) collective-permute-start(bf16[96,128]{1,0:T(8,128)(2,1)S(1)} %get-tuple-element.32), channel_id=1, source_target_pairs={{0,2},{1,3},{2,0},{3,1},{4,6},{5,7},{6,4},{7,5},{8,10},{9,11},{10,... | collective-permute-start | bytes 73736 | tf_op jit(solution)/shard_map/ppermute | solution.py:304
  19.8 3.1 %collective-permute-start.2 = (bf16[96,128]{1,0:T(8,128)(2,1)S(1)}, bf16[96,128]{1,0:T(8,128)(2,1)S(1)}, u32[]{:S(2)}, u32[]{:S(2)}) collective-permute-start(bf16[96,128]{1,0:T(8,128)(2,1)S(1)} %get-tuple-element.33), channel_id=1, source_target_pairs={{0,3},{1,0},{2,1},{3,2},{4,7},{5,4},{6,5},{7,6},{8,11},{9,8},{10,9... | collective-permute-start | bytes 73736 | tf_op jit(solution)/shard_map/ppermute | solution.py:304
  22.9 1.8 %collective-permute-done.2.q3 = bf16[96,128]{1,0:T(8,128)(2,1)S(1)} collective-permute-done((bf16[96,128]{1,0:T(8,128)(2,1)S(1)}, bf16[96,128]{1,0:T(8,128)(2,1)S(1)}, u32[]{:S(2)}, u32[]{:S(2)}) %collective-permute-start.2) | collective-permute-done | bytes 24608 | tf_op jit(solution)/shard_map/ppermute | solution.py:304
  24.7 5.8 %all-to-all-done = bf16[16,128,128]{2,1,0:T(8,128)(2,1)S(1)} async-done(((bf16[16,128,128]{2,1,0:T(8,128)(2,1)}), bf16[16,128,128]{2,1,0:T(8,128)(2,1)S(1)}, u32[]{:S(2)}, u32[]{:S(2)}) %all-to-all-start) | async-done | bytes 524320 | tf_op jit(solution)/shard_map/all_to_all | solution.py:327
  30.5 3.8 %shard_map.69 = f32[32,16,128]{2,1,0:T(8,128)} custom-call(s32[3]{0:T(128)S(1)} %pad_add_fusion.1.at_ref, bf16[2048,128]{1,0:T(8,128)(2,1)S(1)} %bitcast.5, bf16[96,128]{1,0:T(8,128)(2,1)S(1)} %get-tuple-element.30.q0, bf16[96,128]{1,0:T(8,128)(2,1)S(1)} %collective-permute-done.q1, bf16[96,128]{1,0:T(8,128)(2,1)S(1)} %collective-permute-done.1.q2, ...), custom_call_target="tpu_custom_call" | custom-call | flops 805306368 | bytes 1048576 | tf_op jit(solution)/shard_map/pallas_call | solution.py:334
  34.3 11.4 %all-to-all-start.1 = ((f32[32,16,128]{2,1,0:T(8,128)}), f32[32,16,128]{2,1,0:T(8,128)S(1)}, u32[]{:S(2)}, u32[]{:S(2)}) async-start(f32[32,16,128]{2,1,0:T(8,128)} %shard_map.69), calls=%async_computation.1 | async-start | bytes 524288 | tf_op jit(solution)/shard_map/all_to_all | solution.py:344
  45.8 1.9 %collective-permute-start.3 = (bf16[8,128,128]{2,1,0:T(8,128)(2,1)S(1)}, bf16[8,128,128]{2,1,0:T(8,128)(2,1)S(1)}, u32[]{:S(2)}, u32[]{:S(2)}) collective-permute-start(bf16[8,128,128]{2,1,0:T(8,128)(2,1)S(1)} %get-tuple-element.34), channel_id=1, source_target_pairs={{0,4},{4,0},{1,5},{5,1},{2,6},{6,2},{3,7},{7,3},{8,12},{12,8},{9,1... | collective-permute-start | bytes 786440 | tf_op jit(solution)/shard_map/ppermute | solution.py:331
  47.7 1.3 %shard_map.71 = (bf16[8,96,128]{2,1,0:T(8,128)(2,1)S(1)}, bf16[8,96,128]{2,1,0:T(8,128)(2,1)S(1)}, bf16[8,96,128]{2,1,0:T(8,128)(2,1)S(1)}, bf16[8,96,128]{2,1,0:T(8,128)(2,1)S(1)}) custom-call(s32[3]{0:T(128)S(1)} %pad_add_fusion.1.at_ref, bf16[96,4096]{1,0:T(8,128)(2,1)S(1)} %copy-done.1, bf16[96,4096]{1,0:T(8,128)(2,1)S(1)} %copy-done.2), custom_call_target="tpu_custom_call" | custom-call | bytes 3145728 | tf_op jit(solution)/shard_map/pallas_call | solution.py:345
  50.4 6.6 %all-to-all-done.1.in_ref = f32[32,16,128]{2,1,0:T(8,128)S(1)} async-done(((f32[32,16,128]{2,1,0:T(8,128)}), f32[32,16,128]{2,1,0:T(8,128)S(1)}, u32[]{:S(2)}, u32[]{:S(2)}) %all-to-all-start.1) | async-done | bytes 262176 | tf_op jit(solution)/shard_map/all_to_all | solution.py:344
  57.0 2.0 %shard_map.72 = bf16[64,32,128]{2,1,0:T(8,128)(2,1)} custom-call(s32[2]{0:T(128)S(1)} %pad_add_fusion.at_ref, f32[32,16,128]{2,1,0:T(8,128)S(1)} %all-to-all-done.1.in_ref), custom_call_target="tpu_custom_call" | custom-call | bytes 1048576 | tf_op jit(solution)/shard_map/pallas_call | solution.py:347
  59.0 5.1 %all-to-all-start.2 = ((bf16[64,32,128]{2,1,0:T(8,128)(2,1)}), bf16[64,32,128]{2,1,0:T(8,128)(2,1)S(1)}, u32[]{:S(2)}, u32[]{:S(2)}) async-start(bf16[64,32,128]{2,1,0:T(8,128)(2,1)} %shard_map.72), calls=%async_computation.2 | async-start | bytes 1048576 | tf_op jit(solution)/shard_map/all_to_all | solution.py:355
  64.1 2.2 %collective-permute-start.4 = (bf16[8,96,128]{2,1,0:T(8,128)(2,1)S(1)}, bf16[8,96,128]{2,1,0:T(8,128)(2,1)S(1)}, u32[]{:S(2)}, u32[]{:S(2)}) collective-permute-start(bf16[8,96,128]{2,1,0:T(8,128)(2,1)S(1)} %copy-done.6), channel_id=1, source_target_pairs={{0,1},{1,2},{2,3},{3,0},{4,5},{5,6},{6,7},{7,4},{8,9},{9,10},{10,1... | collective-permute-start | bytes 589832 | tf_op jit(solution)/shard_map/ppermute | solution.py:304
  66.3 4.3 %collective-permute-start.5 = (bf16[8,96,128]{2,1,0:T(8,128)(2,1)S(1)}, bf16[8,96,128]{2,1,0:T(8,128)(2,1)S(1)}, u32[]{:S(2)}, u32[]{:S(2)}) collective-permute-start(bf16[8,96,128]{2,1,0:T(8,128)(2,1)S(1)} %copy-done.4), channel_id=1, source_target_pairs={{0,2},{1,3},{2,0},{3,1},{4,6},{5,7},{6,4},{7,5},{8,10},{9,11},{10,... | collective-permute-start | bytes 589832 | tf_op jit(solution)/shard_map/ppermute | solution.py:304
  70.6 3.0 %collective-permute-start.6 = (bf16[8,96,128]{2,1,0:T(8,128)(2,1)S(1)}, bf16[8,96,128]{2,1,0:T(8,128)(2,1)S(1)}, u32[]{:S(2)}, u32[]{:S(2)}) collective-permute-start(bf16[8,96,128]{2,1,0:T(8,128)(2,1)S(1)} %get-tuple-element.43), channel_id=1, source_target_pairs={{0,3},{1,0},{2,1},{3,2},{4,7},{5,4},{6,5},{7,6},{8,11},{9,8},{10,9... | collective-permute-start | bytes 589832 | tf_op jit(solution)/shard_map/ppermute | solution.py:304
  73.7 2.9 %collective-permute-done.5.q2 = bf16[8,96,128]{2,1,0:T(8,128)(2,1)S(1)} collective-permute-done((bf16[8,96,128]{2,1,0:T(8,128)(2,1)S(1)}, bf16[8,96,128]{2,1,0:T(8,128)(2,1)S(1)}, u32[]{:S(2)}, u32[]{:S(2)}) %collective-permute-start.5) | collective-permute-done | bytes 196640 | tf_op jit(solution)/shard_map/ppermute | solution.py:304
  76.6 2.9 %collective-permute-done.6.q3 = bf16[8,96,128]{2,1,0:T(8,128)(2,1)S(1)} collective-permute-done((bf16[8,96,128]{2,1,0:T(8,128)(2,1)S(1)}, bf16[8,96,128]{2,1,0:T(8,128)(2,1)S(1)}, u32[]{:S(2)}, u32[]{:S(2)}) %collective-permute-start.6) | collective-permute-done | bytes 196640 | tf_op jit(solution)/shard_map/ppermute | solution.py:304
  79.6 6.8 %collective-permute-start.8 = (bf16[64,32,128]{2,1,0:T(8,128)(2,1)S(1)}, bf16[64,32,128]{2,1,0:T(8,128)(2,1)S(1)}, u32[]{:S(2)}, u32[]{:S(2)}) collective-permute-start(bf16[64,32,128]{2,1,0:T(8,128)(2,1)S(1)} %all-to-all-done.2.told_ref.own_ref), channel_id=1, source_target_pairs={{0,4},{4,0},{1,5},{5,1},{2,6},{6,2},{3,7},{7,3},{8,12},{12,8},{9,1... | collective-permute-start | bytes 1572872 | tf_op jit(solution)/shard_map/ppermute | solution.py:358
  86.4 2.1 %shard_map.73 = (bf16[8,128,128]{2,1,0:T(8,128)(2,1)S(1)}, bf16[8,128,128]{2,1,0:T(8,128)(2,1)S(1)}) custom-call(bf16[64,32,128]{2,1,0:T(8,128)(2,1)S(1)} %all-to-all-done.2.told_ref.own_ref, bf16[8,128,128]{2,1,0:T(8,128)(2,1)S(1)} %get-tuple-element.45.own_ref, bf16[8,128,128]{2,1,0:T(8,128)(2,1)S(1)} %collective-permute-done.3.away_ref, ...), custom_call_target="tpu_custom_call" | custom-call | flops 805306368 | bytes 2097152 | tf_op jit(solution)/shard_map/pallas_call | solution.py:359
  88.5 1.9 %collective-permute-start.7 = (bf16[8,128,128]{2,1,0:T(8,128)(2,1)S(1)}, bf16[8,128,128]{2,1,0:T(8,128)(2,1)S(1)}, u32[]{:S(2)}, u32[]{:S(2)}) collective-permute-start(bf16[8,128,128]{2,1,0:T(8,128)(2,1)S(1)} %get-tuple-element.51), channel_id=1, source_target_pairs={{0,4},{4,0},{1,5},{5,1},{2,6},{6,2},{3,7},{7,3},{8,12},{12,8},{9,1... | collective-permute-start | bytes 786440 | tf_op jit(solution)/shard_map/ppermute | solution.py:362
  90.4 1.2 %shard_map.74 = bf16[96,4096]{1,0:T(8,128)(2,1)} custom-call(s32[1]{0:T(128)} %bitcast.3.core_ref.at_ref, bf16[64,32,128]{2,1,0:T(8,128)(2,1)S(1)} %all-to-all-done.2.told_ref.own_ref, bf16[64,32,128]{2,1,0:T(8,128)(2,1)S(1)} %collective-permute-done.8.other_ref), custom_call_target="tpu_custom_call" | custom-call | bytes 2097152 | tf_op jit(solution)/shard_map/pallas_call | solution.py:374
  91.9 1.0 %shard_map.75 = (bf16[128,1024]{1,0:T(8,128)(2,1)}, bf16[128,1024]{1,0:T(8,128)(2,1)}) custom-call(s32[1]{0:T(128)} %bitcast.3.core_ref.at_ref, bf16[8,128,128]{2,1,0:T(8,128)(2,1)S(1)} %get-tuple-element.53.grads_ref, bf16[8,128,128]{2,1,0:T(8,128)(2,1)S(1)} %collective-permute-done.7.sent_ref), custom_call_target="tpu_custom_call" | custom-call | bytes 2097152 | tf_op jit(solution)/shard_map/pallas_call | solution.py:376
  (25 shorter events, 2.7 us)
Async XLA Ops:
  0.6 12.6 %copy-start.2 = (bf16[96,4096]{1,0:T(8,128)(2,1)S(1)}, bf16[96,4096]{1,0:T(8,128)(2,1)}, u32[]{:S(2)}) copy-start(bf16[96,4096]{1,0:T(8,128)(2,1)} %g_ref.3) | copy-start | bytes 2359300
  2.8 10.5 %copy-start.1 = (bf16[96,4096]{1,0:T(8,128)(2,1)S(1)}, bf16[96,4096]{1,0:T(8,128)(2,1)}, u32[]{:S(2)}) copy-start(bf16[96,4096]{1,0:T(8,128)(2,1)} %q_ref.3) | copy-start | bytes 2359300
  2.8 27.7 %all-to-all-start = ((bf16[16,128,128]{2,1,0:T(8,128)(2,1)}), bf16[16,128,128]{2,1,0:T(8,128)(2,1)S(1)}, u32[]{:S(2)}, u32[]{:S(2)}) async-start(bf16[16,128,128]{2,1,0:T(8,128)(2,1)} %shard_map.67.in_ref), calls=%async_computation | async-start | bytes 1048576 | tf_op jit(solution)/shard_map/all_to_all | solution.py:327
  13.9 9.0 %collective-permute-start = (bf16[96,128]{1,0:T(8,128)(2,1)S(1)}, bf16[96,128]{1,0:T(8,128)(2,1)S(1)}, u32[]{:S(2)}, u32[]{:S(2)}) collective-permute-start(bf16[96,128]{1,0:T(8,128)(2,1)S(1)} %get-tuple-element.31), channel_id=1, source_target_pairs={{0,1},{1,2},{2,3},{3,0},{4,5},{5,6},{6,7},{7,4},{8,9},{9,10},{10,1... | collective-permute-start | bytes 73736 | tf_op jit(solution)/shard_map/ppermute | solution.py:304
  15.9 7.1 %collective-permute-start.1 = (bf16[96,128]{1,0:T(8,128)(2,1)S(1)}, bf16[96,128]{1,0:T(8,128)(2,1)S(1)}, u32[]{:S(2)}, u32[]{:S(2)}) collective-permute-start(bf16[96,128]{1,0:T(8,128)(2,1)S(1)} %get-tuple-element.32), channel_id=1, source_target_pairs={{0,2},{1,3},{2,0},{3,1},{4,6},{5,7},{6,4},{7,5},{8,10},{9,11},{10,... | collective-permute-start | bytes 73736 | tf_op jit(solution)/shard_map/ppermute | solution.py:304
  19.8 4.9 %collective-permute-start.2 = (bf16[96,128]{1,0:T(8,128)(2,1)S(1)}, bf16[96,128]{1,0:T(8,128)(2,1)S(1)}, u32[]{:S(2)}, u32[]{:S(2)}) collective-permute-start(bf16[96,128]{1,0:T(8,128)(2,1)S(1)} %get-tuple-element.33), channel_id=1, source_target_pairs={{0,3},{1,0},{2,1},{3,2},{4,7},{5,4},{6,5},{7,6},{8,11},{9,8},{10,9... | collective-permute-start | bytes 73736 | tf_op jit(solution)/shard_map/ppermute | solution.py:304
  34.3 11.4 %copy-start = (bf16[16,128,128]{2,1,0:T(8,128)(2,1)S(1)}, bf16[16,128,128]{2,1,0:T(8,128)(2,1)}, u32[]{:S(2)}) copy-start(bf16[16,128,128]{2,1,0:T(8,128)(2,1)} %shard_map.67.in_ref) | copy-start | bytes 1572868
  34.3 22.7 %all-to-all-start.1 = ((f32[32,16,128]{2,1,0:T(8,128)}), f32[32,16,128]{2,1,0:T(8,128)S(1)}, u32[]{:S(2)}, u32[]{:S(2)}) async-start(f32[32,16,128]{2,1,0:T(8,128)} %shard_map.69), calls=%async_computation.1 | async-start | bytes 524288 | tf_op jit(solution)/shard_map/all_to_all | solution.py:344
  45.8 4.7 %collective-permute-start.3 = (bf16[8,128,128]{2,1,0:T(8,128)(2,1)S(1)}, bf16[8,128,128]{2,1,0:T(8,128)(2,1)S(1)}, u32[]{:S(2)}, u32[]{:S(2)}) collective-permute-start(bf16[8,128,128]{2,1,0:T(8,128)(2,1)S(1)} %get-tuple-element.34), channel_id=1, source_target_pairs={{0,4},{4,0},{1,5},{5,1},{2,6},{6,2},{3,7},{7,3},{8,12},{12,8},{9,1... | collective-permute-start | bytes 786440 | tf_op jit(solution)/shard_map/ppermute | solution.py:331
  49.0 0.7 copy-start.3
  49.7 0.7 copy-start.5
  59.0 5.1 %copy-start.6 = (bf16[8,96,128]{2,1,0:T(8,128)(2,1)S(1)}, bf16[8,96,128]{2,1,0:T(8,128)(2,1)}, u32[]{:S(2)}) copy-start(bf16[8,96,128]{2,1,0:T(8,128)(2,1)} %copy-done.5) | copy-start | bytes 589828
  59.0 7.3 %copy-start.4 = (bf16[8,96,128]{2,1,0:T(8,128)(2,1)S(1)}, bf16[8,96,128]{2,1,0:T(8,128)(2,1)}, u32[]{:S(2)}) copy-start(bf16[8,96,128]{2,1,0:T(8,128)(2,1)} %copy-done.3) | copy-start | bytes 589828
  59.0 20.6 %all-to-all-start.2 = ((bf16[64,32,128]{2,1,0:T(8,128)(2,1)}), bf16[64,32,128]{2,1,0:T(8,128)(2,1)S(1)}, u32[]{:S(2)}, u32[]{:S(2)}) async-start(bf16[64,32,128]{2,1,0:T(8,128)(2,1)} %shard_map.72), calls=%async_computation.2 | async-start | bytes 1048576 | tf_op jit(solution)/shard_map/all_to_all | solution.py:355
  64.1 9.6 %collective-permute-start.4 = (bf16[8,96,128]{2,1,0:T(8,128)(2,1)S(1)}, bf16[8,96,128]{2,1,0:T(8,128)(2,1)S(1)}, u32[]{:S(2)}, u32[]{:S(2)}) collective-permute-start(bf16[8,96,128]{2,1,0:T(8,128)(2,1)S(1)} %copy-done.6), channel_id=1, source_target_pairs={{0,1},{1,2},{2,3},{3,0},{4,5},{5,6},{6,7},{7,4},{8,9},{9,10},{10,1... | collective-permute-start | bytes 589832 | tf_op jit(solution)/shard_map/ppermute | solution.py:304
  66.3 10.3 %collective-permute-start.5 = (bf16[8,96,128]{2,1,0:T(8,128)(2,1)S(1)}, bf16[8,96,128]{2,1,0:T(8,128)(2,1)S(1)}, u32[]{:S(2)}, u32[]{:S(2)}) collective-permute-start(bf16[8,96,128]{2,1,0:T(8,128)(2,1)S(1)} %copy-done.4), channel_id=1, source_target_pairs={{0,2},{1,3},{2,0},{3,1},{4,6},{5,7},{6,4},{7,5},{8,10},{9,11},{10,... | collective-permute-start | bytes 589832 | tf_op jit(solution)/shard_map/ppermute | solution.py:304
  70.6 8.8 %collective-permute-start.6 = (bf16[8,96,128]{2,1,0:T(8,128)(2,1)S(1)}, bf16[8,96,128]{2,1,0:T(8,128)(2,1)S(1)}, u32[]{:S(2)}, u32[]{:S(2)}) collective-permute-start(bf16[8,96,128]{2,1,0:T(8,128)(2,1)S(1)} %get-tuple-element.43), channel_id=1, source_target_pairs={{0,3},{1,0},{2,1},{3,2},{4,7},{5,4},{6,5},{7,6},{8,11},{9,8},{10,9... | collective-permute-start | bytes 589832 | tf_op jit(solution)/shard_map/ppermute | solution.py:304
  79.6 10.9 %collective-permute-start.8 = (bf16[64,32,128]{2,1,0:T(8,128)(2,1)S(1)}, bf16[64,32,128]{2,1,0:T(8,128)(2,1)S(1)}, u32[]{:S(2)}, u32[]{:S(2)}) collective-permute-start(bf16[64,32,128]{2,1,0:T(8,128)(2,1)S(1)} %all-to-all-done.2.told_ref.own_ref), channel_id=1, source_target_pairs={{0,4},{4,0},{1,5},{5,1},{2,6},{6,2},{3,7},{7,3},{8,12},{12,8},{9,1... | collective-permute-start | bytes 1572872 | tf_op jit(solution)/shard_map/ppermute | solution.py:358
  88.5 3.4 %collective-permute-start.7 = (bf16[8,128,128]{2,1,0:T(8,128)(2,1)S(1)}, bf16[8,128,128]{2,1,0:T(8,128)(2,1)S(1)}, u32[]{:S(2)}, u32[]{:S(2)}) collective-permute-start(bf16[8,128,128]{2,1,0:T(8,128)(2,1)S(1)} %get-tuple-element.51), channel_id=1, source_target_pairs={{0,4},{4,0},{1,5},{5,1},{2,6},{6,2},{3,7},{7,3},{8,12},{12,8},{9,1... | collective-permute-start | bytes 786440 | tf_op jit(solution)/shard_map/ppermute | solution.py:362
